TPU v7x, 128 devices: a whole 4x4x4 slice. The times are simulated.
128 devices in a mesh: dp: 16 (over y, x_lo, core), fsdp: 8 (over z, x_hi).
Axes of the slice: x: 4 (x_hi: 2, x_lo: 2; x = x_hi * 2 + x_lo), y: 4, z: 4, core: 2. Of those that a mesh axis runs over, the one named last changes fastest.
Arguments:
- hidden: bfloat16 [1536, 28672], P('fsdp', 'dp'), may hold values from -6 to 6
- grad_out: bfloat16 [1536, 8192], P('fsdp', 'dp'), may hold values from -6 to 6
- weight: bfloat16 [28672, 8192], P('dp', 'fsdp'), may hold values from -0.0625 to 0.0625
- basis: bfloat16 [8192, 1024], P('fsdp'), may hold values from -0.1875 to 0.1875
- first_moment: float32 [1024, 28672], P('fsdp', 'dp'), may hold values from -60 to 60
- second_moment: float32 [1024, 28672], P('fsdp', 'dp'), may hold values from 1 to 100
Outputs:
- grad_hidden: bfloat16 [1536, 28672], P('fsdp', 'dp')
- update: bfloat16 [28672, 8192], P('dp', 'fsdp')
- new_first: float32 [1024, 28672], P('fsdp', 'dp')
- new_second: float32 [1024, 28672], P('fsdp', 'dp')
All inputs are finite; a program needn't handle non-finite values.
Results may differ from a plain program's by a relative error of at most 0.025.
Values may be sent and summed in bfloat16 or wider, within the bound.
No kernel may reach another device: no remote copies, remote signals or barrier semaphores. Data moves between devices by JAX's collectives and lax.ppermute only.
A program may use at most 128 MiB of HBM per device.

v0:
```python
import jax
import jax.numpy as jnp
from jax import lax
from jax.sharding import PartitionSpec as P

beta_one = 0.9
beta_two = 0.999
corr_one = 1.0 - 0.9**10
corr_two = 1.0 - 0.999**10
eps_adam = 1e-08
galore_scale = 0.25


def shards(hidden, grad_out, weight, basis, first_moment, second_moment):
    full_grad = lax.all_gather(grad_out, "dp", axis=1, tiled=True)
    col_grad = lax.all_to_all(full_grad, "fsdp", split_axis=1, concat_axis=0, tiled=True)
    low_sum = lax.psum_scatter(
        jnp.dot(col_grad, basis, preferred_element_type=jnp.float32).astype(jnp.bfloat16),
        "fsdp",
        scatter_dimension=0,
        tiled=True,
    )
    grad_hidden = lax.dot_general(
        full_grad,
        lax.all_gather(weight, "fsdp", axis=1, tiled=True),
        (((1,), (1,)), ((), ())),
        preferred_element_type=jnp.float32,
    ).astype(jnp.bfloat16)
    projected = lax.psum_scatter(
        lax.dot_general(
            low_sum, hidden, (((0,), (0,)), ((), ())), preferred_element_type=jnp.float32
        ).astype(jnp.bfloat16),
        "fsdp",
        scatter_dimension=0,
        tiled=True,
    ).astype(jnp.float32)
    new_first = beta_one * first_moment + (1.0 - beta_one) * projected
    new_second = beta_two * second_moment + (1.0 - beta_two) * projected * projected
    direction = (new_first / corr_one / (jnp.sqrt(new_second / corr_two) + eps_adam)).astype(
        jnp.bfloat16
    )
    expanded = lax.dot_general(
        lax.all_gather(direction, "fsdp", axis=0, tiled=True),
        basis,
        (((0,), (1,)), ((), ())),
        preferred_element_type=jnp.float32,
    )
    update = (galore_scale * expanded).astype(jnp.bfloat16)
    return (grad_hidden, update, new_first, new_second)


def solution(mesh):
    return jax.shard_map(
        shards,
        mesh=mesh,
        in_specs=(
            P("fsdp", "dp"),
            P("fsdp", "dp"),
            P("dp", "fsdp"),
            P("fsdp", None),
            P("fsdp", "dp"),
            P("fsdp", "dp"),
        ),
        out_specs=(P("fsdp", "dp"), P("dp", "fsdp"), P("fsdp", "dp"), P("fsdp", "dp")),
        check_vma=False,
    )
```

profile of v0, /device:TPU:0, one launch (start us, length us, event | category | flops | bytes accessed | tf_op | source)
XLA Modules:
  0.0 650.4 jit_solution(4097487019670606209)
XLA Ops:
  7.2 0.0 copy-start
  7.2 0.0 all-gather.4.cloned.1.call-start
  7.2 0.7 all-gather.4.cloned.1.call-update
  7.9 0.0 reduce-scatter.3.cloned.1.call-start
  8.0 40.1 %all-gather.4.cloned.1.call-done = bf16[192,8192]{1,0:T(8,128)(2,1)} async-done(((bf16[192,512]{1,0:T(8,128)(2,1)}), bf16[192,8192]{1,0:T(8,128)(2,1)}) %all-gather.4.cloned.1.call-update) | async-done | bytes 3145744 | tf_op jit(solution)/shard_map/all_gather | solution.py:15
  48.1 2.3 copy.14
  50.4 46.2 %all_to_all.19 = bf16[192,8,1024]{2,0,1:T(8,128)(2,1)S(1)} all-to-all(bf16[192,8,1024]{2,0,1:T(8,128)(2,1)S(1)} %bitcast.15), channel_id=1, replica_groups=mesh['dp'=16,'fsdp'=8] {'fsdp'}, dimensions={1} | all-to-all | bytes 6291456 | tf_op jit(solution)/shard_map/all_to_all | solution.py:16
  96.6 0.0 copy-done
  96.6 4.7 convolution_convert_fusion.1
  101.3 0.0 copy-start.2
  101.3 0.0 reduce-scatter.3.cloned.1.call-update
  101.4 0.0 reduce-scatter.5.cloned.1.call-start
  101.4 75.7 %reduce-scatter.3.cloned.1.call-done = bf16[192,1024]{1,0:T(8,128)(2,1)} async-done(((bf16[1536,1024]{1,0:T(8,128)(2,1)}), bf16[192,1024]{1,0:T(8,128)(2,1)}) %reduce-scatter.3.cloned.1.call-update) | async-done | bytes 393232 | tf_op jit(solution)/shard_map/reduce_scatter | solution.py:17
  177.1 0.0 copy-done.2
  177.2 4.0 convolution_convert_fusion
  181.2 0.0 copy-start.1
  181.2 0.0 reduce-scatter.5.cloned.1.call-update
  181.2 0.0 all-gather.8.cloned.1.call-start
  181.2 81.1 %reduce-scatter.5.cloned.1.call-done = bf16[128,1792]{1,0:T(8,128)(2,1)} async-done(((bf16[1024,1792]{1,0:T(8,128)(2,1)}), bf16[128,1792]{1,0:T(8,128)(2,1)}) %reduce-scatter.5.cloned.1.call-update) | async-done | bytes 458768 | tf_op jit(solution)/shard_map/reduce_scatter | solution.py:29
  262.3 0.0 copy-done.1
  262.3 3.0 divide_convert_fusion
  265.4 0.0 all-gather.8.cloned.1.call-update
  265.4 0.0 all-gather.6.cloned.1.call-start
  265.4 0.5 all-gather.6.cloned.1.call-update
  266.0 65.6 %all-gather.8.cloned.1.call-done = bf16[1024,1792]{1,0:T(8,128)(2,1)} async-done(((bf16[128,1792]{1,0:T(8,128)(2,1)}), bf16[1024,1792]{1,0:T(8,128)(2,1)}) %all-gather.8.cloned.1.call-update) | async-done | bytes 3670032 | tf_op jit(solution)/shard_map/all_gather | solution.py:43
  331.6 7.5 %multiply_convert_fusion = bf16[1792,1024]{1,0:T(8,128)(2,1)} fusion(bf16[1024,1792]{1,0:T(8,128)(2,1)} %all-gather.8.cloned.1.call-done, bf16[1024,1024]{1,0:T(8,128)(2,1)S(1)} %copy-done), kind=kOutput, calls=%fused_computation | convolution fusion | flops 3761766400 | bytes 9437184 | tf_op jit(solution)/shard_map/dot_general | solution.py:42
  339.1 288.9 %all-gather.6.cloned.1.call-done = bf16[1792,8192]{1,0:T(8,128)(2,1)} async-done(((bf16[1792,1024]{1,0:T(8,128)(2,1)}), bf16[1792,8192]{1,0:T(8,128)(2,1)}) %all-gather.6.cloned.1.call-update) | async-done | bytes 29360144 | tf_op jit(solution)/shard_map/all_gather | solution.py:25
  628.0 15.9 %convolution_convert_fusion.2 = bf16[192,1792]{1,0:T(8,128)(2,1)} fusion(bf16[192,8192]{1,0:T(8,128)(2,1)} %all-gather.4.cloned.1.call-done, bf16[1792,8192]{1,0:T(8,128)(2,1)} %all-gather.6.cloned.1.call-done), kind=kOutput, calls=%fused_computation.4 | convolution fusion | flops 5637488640 | bytes 33193984 | tf_op jit(solution)/shard_map/dot_general | solution.py:23
Async XLA Ops:
  7.2 89.4 %copy-start = (bf16[1024,1024]{1,0:T(8,128)(2,1)S(1)}, bf16[1024,1024]{1,0:T(8,128)(2,1)}, u32[]{:S(2)}) copy-start(bf16[1024,1024]{1,0:T(8,128)(2,1)} %param.9) | copy-start | bytes 6291460
  7.2 40.9 %all-gather.4.cloned.1.call-start = ((), (), s32[]{:S(2)}) async-start(), calls=%async_computation.3 | async-start | bytes 3342336 | tf_op jit(solution)/shard_map/all_gather | solution.py:15
  7.9 169.2 %reduce-scatter.3.cloned.1.call-start = ((), (), s32[]{:S(2)}) async-start(), calls=%async_computation.5 | async-start | bytes 3538944 | tf_op jit(solution)/shard_map/reduce_scatter | solution.py:17
  101.3 75.8 %copy-start.2 = (bf16[192,1792]{1,0:T(8,128)(2,1)S(1)}, bf16[192,1792]{1,0:T(8,128)(2,1)}, u32[]{:S(2)}) copy-start(bf16[192,1792]{1,0:T(8,128)(2,1)} %param.6) | copy-start | bytes 2064388
  101.4 160.9 %reduce-scatter.5.cloned.1.call-start = ((), (), s32[]{:S(2)}) async-start(), calls=%async_computation.6 | async-start | bytes 4128768 | tf_op jit(solution)/shard_map/reduce_scatter | solution.py:29
  181.2 81.2 %copy-start.1 = (f32[128,1792]{1,0:T(8,128)S(1)}, f32[128,1792]{1,0:T(8,128)}, u32[]{:S(2)}) copy-start(f32[128,1792]{1,0:T(8,128)} %param.10) | copy-start | bytes 2752516
  181.2 150.4 %all-gather.8.cloned.1.call-start = ((), (), s32[]{:S(2)}) async-start(), calls=%async_computation.7 | async-start | bytes 4128768 | tf_op jit(solution)/shard_map/all_gather | solution.py:43
  265.4 362.6 %all-gather.6.cloned.1.call-start = ((), (), s32[]{:S(2)}) async-start(), calls=%async_computation.4 | async-start | bytes 33030144 | tf_op jit(solution)/shard_map/all_gather | solution.py:25
Sparse Core Ops, SparseCore 0:
  9.7 38.3 all-gather.3
  101.5 75.6 reduce-scatter.2
  181.6 80.6 reduce-scatter.4
  265.5 66.0 all-gather.7
  333.8 294.2 all-gather.5
where the time goes:
time: 651 us; the launch traced here: 650 us
  waiting for transfers between devices  553 us (85%)
  blocking collectives  46.2 us (7%)
  matrix products  32.1 us (5%)
  between operations  13.8 us (2%)
    all_gather x1, waiting for transfers between devices, shards(): lax.all_gather(weight, 'fsdp', axis=1, tiled=True)  289 us
    reduce_scatter x1, waiting for transfers between devices, shards(): lax.psum_scatter(lax.dot_general(low_sum, hidden, (((0,), (0,)), ((), ())...  81.1 us
    reduce_scatter x1, waiting for transfers between devices, shards(): lax.psum_scatter(jnp.dot(col_grad, basis, preferred_element_type=jnp.floa...  75.7 us
    all_gather x1, waiting for transfers between devices, shards(): lax.all_gather(direction, 'fsdp', axis=0, tiled=True)  65.6 us
    all_to_all x1, blocking collectives, shards(): lax.all_to_all(full_grad, 'fsdp', split_axis=1, concat_axis=0, tiled=True)  46.2 us
    all_gather x1, waiting for transfers between devices, shards(): full_grad = lax.all_gather(grad_out, 'dp', axis=1, tiled=True)  40.1 us
    dot_general x1, matrix products, shards(): lax.dot_general(full_grad, lax.all_gather(weight, 'fsdp', axis=1, tiled=T...  15.9 us
  transfers between devices with their start and end apart: 5, of which 5 were waited for; matrix products, arithmetic and copies ran while one was open for 1% of the time, Pallas kernels for 0%

commit v1 on v0

v1 whole, which is shorter than its diff:
```python
import jax
import jax.numpy as jnp
from jax import lax
from jax.sharding import Mesh, PartitionSpec as P

beta_one = 0.9
beta_two = 0.999
corr_one = 1.0 - 0.9**10
corr_two = 1.0 - 0.999**10
eps_adam = 1e-08
galore_scale = 0.25

F32 = jnp.float32
BF16 = jnp.bfloat16


def ring(axis, step):
    pairs = [(i, (i + step) % 4) for i in range(4)]
    return lambda a: lax.ppermute(a, axis, pairs)


def swap(axis):
    return lambda a: lax.ppermute(a, axis, [(0, 1), (1, 0)])


z_up, z_down = ring("z", 1), ring("z", 3)
y_up, y_down, y_two = ring("y", 1), ring("y", 3), ring("y", 2)
x_far, x_near, core = swap("xh"), swap("xl"), swap("c")


def transpose_blocks(a):
    pairs = []
    for y in range(4):
        for xl in range(2):
            for z in range(4):
                for xh in range(2):
                    pairs.append((((y * 2 + xl) * 4 + z) * 2 + xh, ((z * 2 + xh) * 4 + y) * 2 + xl))
    return lax.ppermute(a, ("y", "xl", "z", "xh"), pairs)


def gather_tokens(a):
    other = x_near(a)
    same = lax.axis_index("xl") == lax.axis_index("xh")
    pair = jnp.concatenate([jnp.where(same, a, other), jnp.where(same, other, a)], axis=0)
    up, down, two = y_down(pair), y_up(pair), y_two(pair)
    return jnp.concatenate([pair, up, two, down], axis=0)


def token_block(a, i):
    y, z = lax.axis_index("y"), lax.axis_index("z")
    return lax.dynamic_slice_in_dim(a, ((z - y + i // 2) % 4 * 2 + i % 2) * 192, 192, axis=0)


def gather_start(a):
    return [a, x_far(a), z_up(a), z_down(a)]


def gather_end(a, x, below, above):
    half = a.shape[0] // 2
    first, second = z_up(below[:half]), z_down(above[half:])
    xbelow, xabove = z_up(x), z_down(x)
    two = jnp.concatenate([first, second], axis=0)
    xtwo = x_far(two)
    return [a, x, above, xabove, two, xtwo, below, xbelow]


def after(index, arrays):
    total = sum(a[0, 0].astype(F32) for a in arrays)
    return index + (total != total).astype(jnp.int32)


def dot(a, b, ca, cb):
    return lax.dot_general(a, b, (((ca,), (cb,)), ((), ())), preferred_element_type=F32)


def shards(hidden, grad_out, weight, basis, first_moment, second_moment):
    c, z, xh = (lax.axis_index(n) for n in ("c", "z", "xh"))
    t = transpose_blocks(grad_out)
    begun = gather_start(hidden)

    row = after(c, begun[1:]) * 512
    part = dot(t, lax.dynamic_slice_in_dim(basis, row, 512, axis=0), 1, 0).astype(BF16)
    part = part.reshape(192, 8, 128).transpose(1, 0, 2)
    part = lax.all_to_all(part, ("z", "xh"), 0, 0, tiled=True)
    mine = jnp.sum(part.astype(F32), axis=0).astype(BF16)
    mine = (mine.astype(F32) + core(mine).astype(F32)).astype(BF16)
    low = gather_tokens(mine)
    hidden_blocks = gather_end(*begun)

    half = gather_tokens(t)
    other = core(half)
    col = jnp.concatenate([jnp.where(c == 0, half, other), jnp.where(c == 0, other, half)], axis=1)

    def partial(i):
        return dot(token_block(col, i), weight, 1, 1)

    far = x_far(partial(5).astype(BF16))
    xsum_up, xsum_down = z_up(partial(3).astype(BF16)), z_down(partial(7).astype(BF16))
    two = (partial(4) + far.astype(F32)).astype(BF16)
    first, second = z_up(two[:96]), z_down(two[96:])
    up, down = partial(2), partial(6)
    up = jnp.concatenate([up[:96] + first.astype(F32), up[96:]], axis=0).astype(BF16)
    down = jnp.concatenate([down[:96], down[96:] + second.astype(F32)], axis=0).astype(BF16)
    up, down = z_up(up), z_down(down)
    xsum = (partial(1) + xsum_up.astype(F32) + xsum_down.astype(F32)).astype(BF16)
    xsum = x_far(xsum)
    grad_hidden = (partial(0) + up.astype(F32) + down.astype(F32) + xsum.astype(F32)).astype(BF16)

    projected = jnp.zeros((128, 1792), F32)
    for i, block in enumerate(hidden_blocks):
        projected = projected + dot(token_block(low, i), block, 0, 0).astype(BF16).astype(F32)

    new_first = beta_one * first_moment + (1.0 - beta_one) * projected
    new_second = beta_two * second_moment + (1.0 - beta_two) * projected * projected
    direction = (new_first / corr_one / (jnp.sqrt(new_second / corr_two) + eps_adam)).astype(BF16)

    ranks = jnp.zeros((1024, 1792), BF16)
    for i, block in enumerate(gather_end(*gather_start(direction))):
        place = (z + i // 2) % 4 * 2 + (xh + i % 2) % 2
        ranks = lax.dynamic_update_slice_in_dim(ranks, block, place * 128, axis=0)
    update = (galore_scale * dot(ranks, basis, 0, 1)).astype(BF16)
    return (grad_hidden, update, new_first, new_second)


def solution(mesh):
    fine = Mesh(mesh.devices.reshape(4, 2, 2, 4, 2), ("y", "xl", "c", "z", "xh"))
    fsdp, dp = ("z", "xh"), ("y", "xl", "c")
    return jax.shard_map(
        shards,
        mesh=fine,
        in_specs=(
            P(fsdp, dp),
            P(fsdp, dp),
            P(dp, fsdp),
            P(fsdp, None),
            P(fsdp, dp),
            P(fsdp, dp),
        ),
        out_specs=(P(fsdp, dp), P(dp, fsdp), P(fsdp, dp), P(fsdp, dp)),
        check_vma=False,
    )
```

time: 651 us -> 189 us (0.29)
  waiting for transfers between devices: 553 us -> 50.2 us
  starting transfers between devices: 0.2 us -> 78.1 us
  blocking collectives: 46.2 us -> 0 us
  local copies, waits for them, and re-layouts: 2.33 us -> 21.2 us
  between operations: 13.8 us -> 2.93 us
    all_gather x3 -> x0, waiting for transfers between devices: 395 us -> none  [the longest x1 289 us: shards(): lax.all_gather(weight, 'fsdp', axis=1, tiled=True)]
    reduce_scatter x2 -> x0, waiting for transfers between devices: 157 us -> none  [the longest x1 81.1 us: shards(): lax.psum_scatter(lax.dot_general(low_sum, hidden, (((0,), (0,)), ((), ())...]
    ppermute x0 -> x35, starting transfers between devices: none -> 69.7 us  [the longest x24 42.2 us: ring(): return lambda a: lax.ppermute(a, axis, pairs)]
    ppermute x0 -> x35, waiting for transfers between devices: none -> 50.2 us  [the longest x24 30.8 us: ring(): return lambda a: lax.ppermute(a, axis, pairs)]
    all_to_all x1 -> x0, blocking collectives: 46.2 us -> none  [shards(): lax.all_to_all(full_grad, 'fsdp', split_axis=1, concat_axis=0, tiled=True)]
    all_to_all x0 -> x1, starting transfers between devices: none -> 8.43 us  [shards(): part = lax.all_to_all(part, ('z', 'xh'), 0, 0, tiled=True)]
    dot_general x4 -> x18, matrix products: 32.1 us -> 28.8 us  [dot(): lax.dot_general(a, b, (((ca,), (cb,)), ((), ())), preferred_element_type=...]
  transfers between devices with their start and end apart: 5 -> 36, of which waited for: 5 -> 10; matrix products, arithmetic and copies ran while one was open for 1% -> 28% of each run, Pallas kernels for 0% -> 0%
where the time goes in v1:
time: 189 us; the launch traced here: 188 us
  starting transfers between devices  78.1 us (41%)
  waiting for transfers between devices  50.2 us (27%)
  matrix products  28.8 us (15%)
  local copies, waits for them, and re-layouts  21.2 us (11%)
  other arithmetic  6.22 us (3%)
  between operations  2.93 us (2%)
    ppermute x24, starting transfers between devices, ring(): return lambda a: lax.ppermute(a, axis, pairs)  42.2 us
    ppermute x24, waiting for transfers between devices, ring(): return lambda a: lax.ppermute(a, axis, pairs)  30.8 us
    dot_general x18, matrix products, dot(): lax.dot_general(a, b, (((ca,), (cb,)), ((), ())), preferred_element_type=...  28.8 us
    ppermute x10, starting transfers between devices, swap(): return lambda a: lax.ppermute(a, axis, [(0, 1), (1, 0)])  25.8 us
    ppermute x10, waiting for transfers between devices, swap(): return lambda a: lax.ppermute(a, axis, [(0, 1), (1, 0)])  19.5 us
    all_to_all x1, starting transfers between devices, shards(): part = lax.all_to_all(part, ('z', 'xh'), 0, 0, tiled=True)  8.43 us
    dynamic_update_slice x7, local copies, waits for them, and re-layouts, shards(): ranks = lax.dynamic_update_slice_in_dim(ranks, block, place * 128, axis=0)  5.6 us
    unnamed x16, local copies, waits for them, and re-layouts  5.4 us
  transfers between devices with their start and end apart: 36, of which 10 were waited for; matrix products, arithmetic and copies ran while one was open for 28% of the time, Pallas kernels for 0%

profile of v1, /device:TPU:0, one launch (start us, length us, event | category | flops | bytes accessed | tf_op | source)
XLA Modules:
  0.0 187.5 jit_solution(3522639440837079367)
XLA Ops:
  0.6 1.7 collective-permute-start
  2.4 8.7 %collective-permute-start.1 = (bf16[192,512]{1,0:T(8,128)(2,1)S(1)}, bf16[192,512]{1,0:T(8,128)(2,1)S(1)}, u32[]{:S(2)}, u32[]{:S(2)}) collective-permute-start(bf16[192,512]{1,0:T(8,128)(2,1)S(1)} %collective-permute-done), channel_id=1, source_target_pairs={{0,16},{16,0},{1,17},{17,1},{2,18},{18,2},{3,19},{19,3},{4,20},{20... | collective-permute-start | bytes 589832 | tf_op jit(solution)/shard_map/ppermute | solution.py:23
  11.1 4.2 %collective-permute-start.15 = (bf16[192,1792]{1,0:T(8,128)(2,1)}, bf16[192,1792]{1,0:T(8,128)(2,1)S(1)}, u32[]{:S(2)}, u32[]{:S(2)}) collective-permute-start(bf16[192,1792]{1,0:T(8,128)(2,1)} %param.6), channel_id=1, source_target_pairs={{0,2},{2,4},{4,6},{6,0},{1,3},{3,5},{5,7},{7,1},{8,10},{10,12},{12... | collective-permute-start | bytes 2064392 | tf_op jit(solution)/shard_map/ppermute | solution.py:19
  15.3 2.0 %collective-permute-start.14 = (bf16[192,1792]{1,0:T(8,128)(2,1)}, bf16[192,1792]{1,0:T(8,128)(2,1)}, u32[]{:S(2)}, u32[]{:S(2)}) collective-permute-start(bf16[192,1792]{1,0:T(8,128)(2,1)} %param.6), channel_id=1, source_target_pairs={{0,1},{1,0},{2,3},{3,2},{4,5},{5,4},{6,7},{7,6},{8,9},{9,8},{10,11... | collective-permute-start | bytes 2064392 | tf_op jit(solution)/shard_map/ppermute | solution.py:23
  17.3 8.1 %collective-permute-start.16 = (bf16[192,1792]{1,0:T(8,128)(2,1)}, bf16[192,1792]{1,0:T(8,128)(2,1)}, u32[]{:S(2)}, u32[]{:S(2)}) collective-permute-start(bf16[192,1792]{1,0:T(8,128)(2,1)} %param.6), channel_id=1, source_target_pairs={{0,6},{2,0},{4,2},{6,4},{1,7},{3,1},{5,3},{7,5},{8,14},{10,8},{12,... | collective-permute-start | bytes 2064392 | tf_op jit(solution)/shard_map/ppermute | solution.py:19
  27.6 2.2 %collective-permute-start.2 = (bf16[384,512]{1,0:T(8,128)(2,1)}, bf16[384,512]{1,0:T(8,128)(2,1)}, u32[]{:S(2)}, u32[]{:S(2)}) collective-permute-start(bf16[384,512]{1,0:T(8,128)(2,1)} %pad_maximum_fusion.2), channel_id=1, source_target_pairs={{0,96},{32,0},{64,32},{96,64},{1,97},{33,1},{65,33},{97,65},{2,98}... | collective-permute-start | bytes 1179656 | tf_op jit(solution)/shard_map/ppermute | solution.py:19
  29.8 1.5 collective-permute-start.3
  31.3 5.7 %collective-permute-done.15 = bf16[192,1792]{1,0:T(8,128)(2,1)S(1)} collective-permute-done((bf16[192,1792]{1,0:T(8,128)(2,1)}, bf16[192,1792]{1,0:T(8,128)(2,1)S(1)}, u32[]{:S(2)}, u32[]{:S(2)}) %collective-permute-start.15) | collective-permute-done | bytes 688160 | tf_op jit(solution)/shard_map/ppermute | solution.py:19
  37.9 1.2 slice.60
  40.4 1.2 slice.62
  43.4 8.4 %all-to-all-start = ((bf16[8,192,128]{2,1,0:T(8,128)(2,1)}), bf16[8,192,128]{2,1,0:T(8,128)(2,1)S(1)}, u32[]{:S(2)}, u32[]{:S(2)}) async-start(bf16[8,192,128]{2,1,0:T(8,128)(2,1)} %bitcast.28), calls=%async_computation | async-start | bytes 786432 | tf_op jit(solution)/shard_map/all_to_all | solution.py:84
  52.6 2.0 %collective-permute-start.23 = (bf16[96,1792]{1,0:T(8,128)(2,1)}, bf16[96,1792]{1,0:T(8,128)(2,1)}, u32[]{:S(2)}, u32[]{:S(2)}) collective-permute-start(bf16[96,1792]{1,0:T(8,128)(2,1)} %slice.63), channel_id=1, source_target_pairs={{0,2},{2,4},{4,6},{6,0},{1,3},{3,5},{5,7},{7,1},{8,10},{10,12},{12... | collective-permute-start | bytes 1032200 | tf_op jit(solution)/shard_map/ppermute | solution.py:19
  54.6 1.7 slice.64
  56.4 1.2 collective-permute-start.24
  58.4 1.8 constant_dynamic-update-slice_fusion.2
  60.2 2.4 %collective-permute-start.22 = (bf16[192,1792]{1,0:T(8,128)(2,1)}, bf16[192,1792]{1,0:T(8,128)(2,1)}, u32[]{:S(2)}, u32[]{:S(2)}) collective-permute-start(bf16[192,1792]{1,0:T(8,128)(2,1)} %collective-permute-done.14), channel_id=1, source_target_pairs={{0,6},{2,0},{4,2},{6,4},{1,7},{3,1},{5,3},{7,5},{8,14},{10,8},{12,... | collective-permute-start | bytes 2064392 | tf_op jit(solution)/shard_map/ppermute | solution.py:19
  62.6 1.8 constant_dynamic-update-slice_fusion.1
  65.1 1.8 constant_dynamic-update-slice_fusion
  69.9 2.4 %collective-permute-done.18 = bf16[192,128]{1,0:T(8,128)(2,1)S(1)} collective-permute-done((bf16[192,128]{1,0:T(8,128)(2,1)S(1)}, bf16[192,128]{1,0:T(8,128)(2,1)S(1)}, u32[]{:S(2)}, u32[]{:S(2)}) %collective-permute-start.18) | collective-permute-done | bytes 49184 | tf_op jit(solution)/shard_map/ppermute | solution.py:23
  73.2 3.6 %collective-permute-start.25 = (bf16[192,1792]{1,0:T(8,128)(2,1)S(1)}, bf16[192,1792]{1,0:T(8,128)(2,1)S(1)}, u32[]{:S(2)}, u32[]{:S(2)}) collective-permute-start(bf16[192,1792]{1,0:T(8,128)(2,1)S(1)} %constant_dynamic-update-slice_fusion.10), channel_id=1, source_target_pairs={{0,1},{1,0},{2,3},{3,2},{4,5},{5,4},{6,7},{7,6},{8,9},{9,8},{10,11... | collective-permute-start | bytes 2064392 | tf_op jit(solution)/shard_map/ppermute | solution.py:23
  77.7 5.6 %collective-permute-done.20 = bf16[384,128]{1,0:T(8,128)(2,1)S(1)} collective-permute-done((bf16[384,128]{1,0:T(8,128)(2,1)S(1)}, bf16[384,128]{1,0:T(8,128)(2,1)S(1)}, u32[]{:S(2)}, u32[]{:S(2)}) %collective-permute-start.20) | collective-permute-done | bytes 98336 | tf_op jit(solution)/shard_map/ppermute | solution.py:19
  84.3 4.8 %collective-permute-done.21 = bf16[384,128]{1,0:T(8,128)(2,1)S(1)} collective-permute-done((bf16[384,128]{1,0:T(8,128)(2,1)S(1)}, bf16[384,128]{1,0:T(8,128)(2,1)S(1)}, u32[]{:S(2)}, u32[]{:S(2)}) %collective-permute-start.21) | collective-permute-done | bytes 98336 | tf_op jit(solution)/shard_map/ppermute | solution.py:19
  89.1 1.4 fusion.18
  90.8 1.4 fusion.17
  93.2 1.4 fusion.15
  94.7 2.0 %broadcast_in_dim.3 = bf16[1024,1792]{1,0:T(8,128)(2,1)} broadcast(bf16[]{:T(256)} %constant.146.clone.1), dimensions={} | broadcast | bytes 3670018 | tf_op jit(solution)/shard_map/broadcast_in_dim | solution.py:117
  96.8 3.4 %constant_dynamic-update-slice_fusion.21 = (bf16[1024,1792]{1,0:T(8,128)(2,1)}, bf16[128,1792]{1,0:T(8,128)(2,1)}, f32[128,1792]{1,0:T(8,128)}, f32[128,1792]{1,0:T(8,128)}) fusion(bf16[1024,1792]{1,0:T(8,128)(2,1)} %broadcast_in_dim.3, s32[]{:T(128)S(6)} %select_n.206, f32[128,1792]{1,0:T(8,128)S(1)} %copy-done.3, f32[128,1792]{1,0:T(8,128)S(1)} %copy-done.4, ...), kind=kOutput, calls=%fused_computation.116 | convolution fusion | flops 91521024 | bytes 6242312 | tf_op jit(solution)/shard_map/dot_general | solution.py:73
  102.3 3.5 %collective-permute-start.27 = (bf16[128,1792]{1,0:T(8,128)(2,1)}, bf16[128,1792]{1,0:T(8,128)(2,1)S(1)}, u32[]{:S(2)}, u32[]{:S(2)}) collective-permute-start(bf16[128,1792]{1,0:T(8,128)(2,1)} %get-tuple-element.5), channel_id=1, source_target_pairs={{0,1},{1,0},{2,3},{3,2},{4,5},{5,4},{6,7},{7,6},{8,9},{9,8},{10,11... | collective-permute-start | bytes 1376264 | tf_op jit(solution)/shard_map/ppermute | solution.py:23
  105.8 5.2 %collective-permute-done.28 = bf16[128,1792]{1,0:T(8,128)(2,1)S(1)} collective-permute-done((bf16[128,1792]{1,0:T(8,128)(2,1)}, bf16[128,1792]{1,0:T(8,128)(2,1)S(1)}, u32[]{:S(2)}, u32[]{:S(2)}) %collective-permute-start.28) | collective-permute-done | bytes 458784 | tf_op jit(solution)/shard_map/ppermute | solution.py:19
  111.1 1.2 collective-permute-start.32
  113.5 3.0 %collective-permute-start.29 = (bf16[128,1792]{1,0:T(8,128)(2,1)S(1)}, bf16[128,1792]{1,0:T(8,128)(2,1)S(1)}, u32[]{:S(2)}, u32[]{:S(2)}) collective-permute-start(bf16[128,1792]{1,0:T(8,128)(2,1)S(1)} %collective-permute-done.27), channel_id=1, source_target_pairs={{0,6},{2,0},{4,2},{6,4},{1,7},{3,1},{5,3},{7,5},{8,14},{10,8},{12,... | collective-permute-start | bytes 1376264 | tf_op jit(solution)/shard_map/ppermute | solution.py:19
  118.1 2.2 %broadcast_select_fusion = (bf16[1536,512]{1,0:T(8,128)(2,1)S(1)}, bf16[1536,512]{1,0:T(8,128)(2,1)S(1)}) fusion(bf16[1536,512]{1,0:T(8,128)(2,1)} %collective-permute-done.5, bf16[1536,512]{1,0:T(8,128)(2,1)} %constant_dynamic-update-slice_fusion, pred[]{:T(512)S(6)} %eq.41), kind=kLoop, calls=%fused_computation.52 | loop fusion | flops 1572864 | bytes 6291457 | tf_op jit(solution)/shard_map/jit(_where)/select_n | solution.py:92
  121.1 1.4 convolution_convert_fusion.2
  122.5 1.4 convolution_convert_fusion
  123.8 1.3 fusion.36
  125.2 1.4 fusion.40
  127.7 1.4 convolution_convert_fusion.1
  130.2 3.6 %collective-permute-start.6 = (bf16[192,1792]{1,0:T(8,128)(2,1)S(1)}, bf16[192,1792]{1,0:T(8,128)(2,1)S(1)}, u32[]{:S(2)}, u32[]{:S(2)}) collective-permute-start(bf16[192,1792]{1,0:T(8,128)(2,1)S(1)} %convolution_convert_fusion.2), channel_id=1, source_target_pairs={{0,1},{1,0},{2,3},{3,2},{4,5},{5,4},{6,7},{7,6},{8,9},{9,8},{10,11... | collective-permute-start | bytes 2064392 | tf_op jit(solution)/shard_map/ppermute | solution.py:23
  135.5 17.0 %collective-permute-done.33 = bf16[128,1792]{1,0:T(8,128)(2,1)S(1)} collective-permute-done((bf16[128,1792]{1,0:T(8,128)(2,1)S(1)}, bf16[128,1792]{1,0:T(8,128)(2,1)S(1)}, u32[]{:S(2)}, u32[]{:S(2)}) %collective-permute-start.33) | collective-permute-done | bytes 458784 | tf_op jit(solution)/shard_map/ppermute | solution.py:23
  154.9 1.4 fusion.5
  156.7 1.4 fusion.4
  158.1 3.0 %collective-permute-start.13 = (bf16[192,1792]{1,0:T(8,128)(2,1)S(1)}, bf16[192,1792]{1,0:T(8,128)(2,1)S(1)}, u32[]{:S(2)}, u32[]{:S(2)}) collective-permute-start(bf16[192,1792]{1,0:T(8,128)(2,1)S(1)} %fusion.4), channel_id=1, source_target_pairs={{0,1},{1,0},{2,3},{3,2},{4,5},{5,4},{6,7},{7,6},{8,9},{9,8},{10,11... | collective-permute-start | bytes 2064392 | tf_op jit(solution)/shard_map/ppermute | solution.py:23
  161.1 3.0 %collective-permute-start.9 = (bf16[96,1792]{1,0:T(8,128)(2,1)S(1)}, bf16[96,1792]{1,0:T(8,128)(2,1)S(1)}, u32[]{:S(2)}, u32[]{:S(2)}) collective-permute-start(bf16[96,1792]{1,0:T(8,128)(2,1)S(1)} %get-tuple-element.19), channel_id=1, source_target_pairs={{0,6},{2,0},{4,2},{6,4},{1,7},{3,1},{5,3},{7,5},{8,14},{10,8},{12,... | collective-permute-start | bytes 1032200 | tf_op jit(solution)/shard_map/ppermute | solution.py:19
  164.1 4.4 %collective-permute-done.7 = bf16[96,1792]{1,0:T(8,128)(2,1)S(1)} collective-permute-done((bf16[96,1792]{1,0:T(8,128)(2,1)S(1)}, bf16[96,1792]{1,0:T(8,128)(2,1)S(1)}, u32[]{:S(2)}, u32[]{:S(2)}) %collective-permute-start.7) | collective-permute-done | bytes 344096 | tf_op jit(solution)/shard_map/ppermute | solution.py:19
  168.7 3.9 %collective-permute-done.9 = bf16[96,1792]{1,0:T(8,128)(2,1)S(1)} collective-permute-done((bf16[96,1792]{1,0:T(8,128)(2,1)S(1)}, bf16[96,1792]{1,0:T(8,128)(2,1)S(1)}, u32[]{:S(2)}, u32[]{:S(2)}) %collective-permute-start.9) | collective-permute-done | bytes 344096 | tf_op jit(solution)/shard_map/ppermute | solution.py:19
  172.7 4.0 %collective-permute-start.10 = (bf16[192,1792]{1,0:T(8,128)(2,1)S(1)}, bf16[192,1792]{1,0:T(8,128)(2,1)S(1)}, u32[]{:S(2)}, u32[]{:S(2)}) collective-permute-start(bf16[192,1792]{1,0:T(8,128)(2,1)S(1)} %pad_maximum_fusion.1), channel_id=1, source_target_pairs={{0,6},{2,0},{4,2},{6,4},{1,7},{3,1},{5,3},{7,5},{8,14},{10,8},{12,... | collective-permute-start | bytes 2064392 | tf_op jit(solution)/shard_map/ppermute | solution.py:19
  176.7 7.5 %multiply_convert_fusion = bf16[1792,1024]{1,0:T(8,128)(2,1)} fusion(bf16[1024,1792]{1,0:T(8,128)(2,1)} %constant_dynamic-update-slice_fusion.14, bf16[1024,1024]{1,0:T(8,128)(2,1)S(1)} %copy-done), kind=kOutput, calls=%fused_computation | convolution fusion | flops 3761766400 | bytes 9437184 | tf_op jit(solution)/shard_map/dot_general | solution.py:73
  185.2 2.4 %fusion.3 = bf16[192,1792]{1,0:T(8,128)(2,1)} fusion(bf16[1792,1024]{1,0:T(8,128)(2,1)S(1)} %copy-done.1, bf16[192,1792]{1,0:T(8,128)(2,1)S(1)} %collective-permute-done.13, bf16[192,1792]{1,0:T(8,128)(2,1)S(1)} %collective-permute-done.10, bf16[192,1792]{1,0:T(8,128)(2,1)S(1)} %collective-permute-done.8, s32[]{:T(128)S(6)} %select_n.189, ...), kind=kOutput, calls=%fused_computation.23 | convolution fusion | flops 707837952 | bytes 9568260 | tf_op jit(solution)/shard_map/dot_general | solution.py:73
  (94 shorter events, 27.5 us)
Async XLA Ops:
  0.6 41.6 %copy-start = (bf16[1024,1024]{1,0:T(8,128)(2,1)S(1)}, bf16[1024,1024]{1,0:T(8,128)(2,1)}, u32[]{:S(2)}) copy-start(bf16[1024,1024]{1,0:T(8,128)(2,1)} %param.9) | copy-start | bytes 6291460
  0.6 1.7 collective-permute-start
  2.4 23.0 %collective-permute-start.1 = (bf16[192,512]{1,0:T(8,128)(2,1)S(1)}, bf16[192,512]{1,0:T(8,128)(2,1)S(1)}, u32[]{:S(2)}, u32[]{:S(2)}) collective-permute-start(bf16[192,512]{1,0:T(8,128)(2,1)S(1)} %collective-permute-done), channel_id=1, source_target_pairs={{0,16},{16,0},{1,17},{17,1},{2,18},{18,2},{3,19},{19,3},{4,20},{20... | collective-permute-start | bytes 589832 | tf_op jit(solution)/shard_map/ppermute | solution.py:23
  11.1 25.9 %collective-permute-start.15 = (bf16[192,1792]{1,0:T(8,128)(2,1)}, bf16[192,1792]{1,0:T(8,128)(2,1)S(1)}, u32[]{:S(2)}, u32[]{:S(2)}) collective-permute-start(bf16[192,1792]{1,0:T(8,128)(2,1)} %param.6), channel_id=1, source_target_pairs={{0,2},{2,4},{4,6},{6,0},{1,3},{3,5},{5,7},{7,1},{8,10},{10,12},{12... | collective-permute-start | bytes 2064392 | tf_op jit(solution)/shard_map/ppermute | solution.py:19
  15.3 22.6 %collective-permute-start.14 = (bf16[192,1792]{1,0:T(8,128)(2,1)}, bf16[192,1792]{1,0:T(8,128)(2,1)}, u32[]{:S(2)}, u32[]{:S(2)}) collective-permute-start(bf16[192,1792]{1,0:T(8,128)(2,1)} %param.6), channel_id=1, source_target_pairs={{0,1},{1,0},{2,3},{3,2},{4,5},{5,4},{6,7},{7,6},{8,9},{9,8},{10,11... | collective-permute-start | bytes 2064392 | tf_op jit(solution)/shard_map/ppermute | solution.py:23
  17.3 23.0 %collective-permute-start.16 = (bf16[192,1792]{1,0:T(8,128)(2,1)}, bf16[192,1792]{1,0:T(8,128)(2,1)}, u32[]{:S(2)}, u32[]{:S(2)}) collective-permute-start(bf16[192,1792]{1,0:T(8,128)(2,1)} %param.6), channel_id=1, source_target_pairs={{0,6},{2,0},{4,2},{6,4},{1,7},{3,1},{5,3},{7,5},{8,14},{10,8},{12,... | collective-permute-start | bytes 2064392 | tf_op jit(solution)/shard_map/ppermute | solution.py:19
  27.6 30.0 %collective-permute-start.2 = (bf16[384,512]{1,0:T(8,128)(2,1)}, bf16[384,512]{1,0:T(8,128)(2,1)}, u32[]{:S(2)}, u32[]{:S(2)}) collective-permute-start(bf16[384,512]{1,0:T(8,128)(2,1)} %pad_maximum_fusion.2), channel_id=1, source_target_pairs={{0,96},{32,0},{64,32},{96,64},{1,97},{33,1},{65,33},{97,65},{2,98}... | collective-permute-start | bytes 1179656 | tf_op jit(solution)/shard_map/ppermute | solution.py:19
  29.8 30.3 %collective-permute-start.3 = (bf16[384,512]{1,0:T(8,128)(2,1)}, bf16[384,512]{1,0:T(8,128)(2,1)}, u32[]{:S(2)}, u32[]{:S(2)}) collective-permute-start(bf16[384,512]{1,0:T(8,128)(2,1)} %pad_maximum_fusion.2), channel_id=1, source_target_pairs={{0,64},{32,96},{64,0},{96,32},{1,65},{33,97},{65,1},{97,33},{2,66}... | collective-permute-start | bytes 1179656 | tf_op jit(solution)/shard_map/ppermute | solution.py:19
  37.0 28.1 %collective-permute-start.4 = (bf16[384,512]{1,0:T(8,128)(2,1)}, bf16[384,512]{1,0:T(8,128)(2,1)}, u32[]{:S(2)}, u32[]{:S(2)}) collective-permute-start(bf16[384,512]{1,0:T(8,128)(2,1)} %pad_maximum_fusion.2), channel_id=1, source_target_pairs={{0,32},{32,64},{64,96},{96,0},{1,33},{33,65},{65,97},{97,1},{2,34}... | collective-permute-start | bytes 1179656 | tf_op jit(solution)/shard_map/ppermute | solution.py:19
  43.4 20.9 %all-to-all-start = ((bf16[8,192,128]{2,1,0:T(8,128)(2,1)}), bf16[8,192,128]{2,1,0:T(8,128)(2,1)S(1)}, u32[]{:S(2)}, u32[]{:S(2)}) async-start(bf16[8,192,128]{2,1,0:T(8,128)(2,1)} %bitcast.28), calls=%async_computation | async-start | bytes 786432 | tf_op jit(solution)/shard_map/all_to_all | solution.py:84
  52.6 15.5 %collective-permute-start.23 = (bf16[96,1792]{1,0:T(8,128)(2,1)}, bf16[96,1792]{1,0:T(8,128)(2,1)}, u32[]{:S(2)}, u32[]{:S(2)}) collective-permute-start(bf16[96,1792]{1,0:T(8,128)(2,1)} %slice.63), channel_id=1, source_target_pairs={{0,2},{2,4},{4,6},{6,0},{1,3},{3,5},{5,7},{7,1},{8,10},{10,12},{12... | collective-permute-start | bytes 1032200 | tf_op jit(solution)/shard_map/ppermute | solution.py:19
  56.4 16.8 %collective-permute-start.24 = (bf16[96,1792]{1,0:T(8,128)(2,1)}, bf16[96,1792]{1,0:T(8,128)(2,1)S(1)}, u32[]{:S(2)}, u32[]{:S(2)}) collective-permute-start(bf16[96,1792]{1,0:T(8,128)(2,1)} %slice.64), channel_id=1, source_target_pairs={{0,6},{2,0},{4,2},{6,4},{1,7},{3,1},{5,3},{7,5},{8,14},{10,8},{12,... | collective-permute-start | bytes 1032200 | tf_op jit(solution)/shard_map/ppermute | solution.py:19
  57.6 37.1 %collective-permute-start.26 = (bf16[192,1792]{1,0:T(8,128)(2,1)}, bf16[192,1792]{1,0:T(8,128)(2,1)}, u32[]{:S(2)}, u32[]{:S(2)}) collective-permute-start(bf16[192,1792]{1,0:T(8,128)(2,1)} %collective-permute-done.14), channel_id=1, source_target_pairs={{0,2},{2,4},{4,6},{6,0},{1,3},{3,5},{5,7},{7,1},{8,10},{10,12},{12... | collective-permute-start | bytes 2064392 | tf_op jit(solution)/shard_map/ppermute | solution.py:19
  60.2 33.1 %collective-permute-start.22 = (bf16[192,1792]{1,0:T(8,128)(2,1)}, bf16[192,1792]{1,0:T(8,128)(2,1)}, u32[]{:S(2)}, u32[]{:S(2)}) collective-permute-start(bf16[192,1792]{1,0:T(8,128)(2,1)} %collective-permute-done.14), channel_id=1, source_target_pairs={{0,6},{2,0},{4,2},{6,4},{1,7},{3,1},{5,3},{7,5},{8,14},{10,8},{12,... | collective-permute-start | bytes 2064392 | tf_op jit(solution)/shard_map/ppermute | solution.py:19
  65.1 1.8 collective-permute-start.17
  66.8 51.3 %collective-permute-start.5 = (bf16[1536,512]{1,0:T(8,128)(2,1)}, bf16[1536,512]{1,0:T(8,128)(2,1)}, u32[]{:S(2)}, u32[]{:S(2)}) collective-permute-start(bf16[1536,512]{1,0:T(8,128)(2,1)} %constant_dynamic-update-slice_fusion), channel_id=1, source_target_pairs={{0,8},{8,0},{1,9},{9,1},{2,10},{10,2},{3,11},{11,3},{4,12},{12,4},... | collective-permute-start | bytes 4718600 | tf_op jit(solution)/shard_map/ppermute | solution.py:23
  68.2 4.2 %collective-permute-start.18 = (bf16[192,128]{1,0:T(8,128)(2,1)S(1)}, bf16[192,128]{1,0:T(8,128)(2,1)S(1)}, u32[]{:S(2)}, u32[]{:S(2)}) collective-permute-start(bf16[192,128]{1,0:T(8,128)(2,1)S(1)} %add_convert_fusion), channel_id=1, source_target_pairs={{0,16},{16,0},{1,17},{17,1},{2,18},{18,2},{3,19},{19,3},{4,20},{20... | collective-permute-start | bytes 147464 | tf_op jit(solution)/shard_map/ppermute | solution.py:23
  72.4 18.1 %copy-start.2 = (bf16[192,1792]{1,0:T(8,128)(2,1)S(1)}, bf16[192,1792]{1,0:T(8,128)(2,1)}, u32[]{:S(2)}) copy-start(bf16[192,1792]{1,0:T(8,128)(2,1)} %param.6) | copy-start | bytes 2064388
  72.4 4.7 %collective-permute-start.19 = (bf16[384,128]{1,0:T(8,128)(2,1)S(1)}, bf16[384,128]{1,0:T(8,128)(2,1)S(1)}, u32[]{:S(2)}, u32[]{:S(2)}) collective-permute-start(bf16[384,128]{1,0:T(8,128)(2,1)S(1)} %pad_maximum_fusion.3), channel_id=1, source_target_pairs={{0,96},{32,0},{64,32},{96,64},{1,97},{33,1},{65,33},{97,65},{2,98}... | collective-permute-start | bytes 294920 | tf_op jit(solution)/shard_map/ppermute | solution.py:19
  73.2 19.7 %collective-permute-start.25 = (bf16[192,1792]{1,0:T(8,128)(2,1)S(1)}, bf16[192,1792]{1,0:T(8,128)(2,1)S(1)}, u32[]{:S(2)}, u32[]{:S(2)}) collective-permute-start(bf16[192,1792]{1,0:T(8,128)(2,1)S(1)} %constant_dynamic-update-slice_fusion.10), channel_id=1, source_target_pairs={{0,1},{1,0},{2,3},{3,2},{4,5},{5,4},{6,7},{7,6},{8,9},{9,8},{10,11... | collective-permute-start | bytes 2064392 | tf_op jit(solution)/shard_map/ppermute | solution.py:23
  77.1 6.1 %collective-permute-start.20 = (bf16[384,128]{1,0:T(8,128)(2,1)S(1)}, bf16[384,128]{1,0:T(8,128)(2,1)S(1)}, u32[]{:S(2)}, u32[]{:S(2)}) collective-permute-start(bf16[384,128]{1,0:T(8,128)(2,1)S(1)} %pad_maximum_fusion.3), channel_id=1, source_target_pairs={{0,64},{32,96},{64,0},{96,32},{1,65},{33,97},{65,1},{97,33},{2,66}... | collective-permute-start | bytes 294920 | tf_op jit(solution)/shard_map/ppermute | solution.py:19
  83.2 5.8 %collective-permute-start.21 = (bf16[384,128]{1,0:T(8,128)(2,1)S(1)}, bf16[384,128]{1,0:T(8,128)(2,1)S(1)}, u32[]{:S(2)}, u32[]{:S(2)}) collective-permute-start(bf16[384,128]{1,0:T(8,128)(2,1)S(1)} %pad_maximum_fusion.3), channel_id=1, source_target_pairs={{0,32},{32,64},{64,96},{96,0},{1,33},{33,65},{65,97},{97,1},{2,34}... | collective-permute-start | bytes 294920 | tf_op jit(solution)/shard_map/ppermute | solution.py:19
  94.7 2.1 %copy-start.3 = (f32[128,1792]{1,0:T(8,128)S(1)}, f32[128,1792]{1,0:T(8,128)}, u32[]{:S(2)}) copy-start(f32[128,1792]{1,0:T(8,128)} %param.10) | copy-start | bytes 2752516
  94.7 2.1 %copy-start.4 = (f32[128,1792]{1,0:T(8,128)S(1)}, f32[128,1792]{1,0:T(8,128)}, u32[]{:S(2)}) copy-start(f32[128,1792]{1,0:T(8,128)} %param.11) | copy-start | bytes 2752516
  100.2 10.8 %collective-permute-start.28 = (bf16[128,1792]{1,0:T(8,128)(2,1)}, bf16[128,1792]{1,0:T(8,128)(2,1)S(1)}, u32[]{:S(2)}, u32[]{:S(2)}) collective-permute-start(bf16[128,1792]{1,0:T(8,128)(2,1)} %get-tuple-element.5), channel_id=1, source_target_pairs={{0,6},{2,0},{4,2},{6,4},{1,7},{3,1},{5,3},{7,5},{8,14},{10,8},{12,... | collective-permute-start | bytes 1376264 | tf_op jit(solution)/shard_map/ppermute | solution.py:19
  101.3 10.9 %collective-permute-start.30 = (bf16[128,1792]{1,0:T(8,128)(2,1)}, bf16[128,1792]{1,0:T(8,128)(2,1)S(1)}, u32[]{:S(2)}, u32[]{:S(2)}) collective-permute-start(bf16[128,1792]{1,0:T(8,128)(2,1)} %get-tuple-element.5), channel_id=1, source_target_pairs={{0,2},{2,4},{4,6},{6,0},{1,3},{3,5},{5,7},{7,1},{8,10},{10,12},{12... | collective-permute-start | bytes 1376264 | tf_op jit(solution)/shard_map/ppermute | solution.py:19
  102.3 11.0 %collective-permute-start.27 = (bf16[128,1792]{1,0:T(8,128)(2,1)}, bf16[128,1792]{1,0:T(8,128)(2,1)S(1)}, u32[]{:S(2)}, u32[]{:S(2)}) collective-permute-start(bf16[128,1792]{1,0:T(8,128)(2,1)} %get-tuple-element.5), channel_id=1, source_target_pairs={{0,1},{1,0},{2,3},{3,2},{4,5},{5,4},{6,7},{7,6},{8,9},{9,8},{10,11... | collective-permute-start | bytes 1376264 | tf_op jit(solution)/shard_map/ppermute | solution.py:23
  111.1 19.1 %collective-permute-start.32 = (bf16[64,1792]{1,0:T(8,128)(2,1)S(1)}, bf16[64,1792]{1,0:T(8,128)(2,1)S(1)}, u32[]{:S(2)}, u32[]{:S(2)}) collective-permute-start(bf16[64,1792]{1,0:T(8,128)(2,1)S(1)} %slice.66), channel_id=1, source_target_pairs={{0,6},{2,0},{4,2},{6,4},{1,7},{3,1},{5,3},{7,5},{8,14},{10,8},{12,... | collective-permute-start | bytes 688136 | tf_op jit(solution)/shard_map/ppermute | solution.py:19
  112.3 16.8 %collective-permute-start.31 = (bf16[64,1792]{1,0:T(8,128)(2,1)S(1)}, bf16[64,1792]{1,0:T(8,128)(2,1)S(1)}, u32[]{:S(2)}, u32[]{:S(2)}) collective-permute-start(bf16[64,1792]{1,0:T(8,128)(2,1)S(1)} %slice.65), channel_id=1, source_target_pairs={{0,2},{2,4},{4,6},{6,0},{1,3},{3,5},{5,7},{7,1},{8,10},{10,12},{12... | collective-permute-start | bytes 688136 | tf_op jit(solution)/shard_map/ppermute | solution.py:19
  113.3 40.8 %collective-permute-start.34 = (bf16[128,1792]{1,0:T(8,128)(2,1)S(1)}, bf16[128,1792]{1,0:T(8,128)(2,1)S(1)}, u32[]{:S(2)}, u32[]{:S(2)}) collective-permute-start(bf16[128,1792]{1,0:T(8,128)(2,1)S(1)} %collective-permute-done.27), channel_id=1, source_target_pairs={{0,2},{2,4},{4,6},{6,0},{1,3},{3,5},{5,7},{7,1},{8,10},{10,12},{12... | collective-permute-start | bytes 1376264 | tf_op jit(solution)/shard_map/ppermute | solution.py:19
  113.5 20.3 %collective-permute-start.29 = (bf16[128,1792]{1,0:T(8,128)(2,1)S(1)}, bf16[128,1792]{1,0:T(8,128)(2,1)S(1)}, u32[]{:S(2)}, u32[]{:S(2)}) collective-permute-start(bf16[128,1792]{1,0:T(8,128)(2,1)S(1)} %collective-permute-done.27), channel_id=1, source_target_pairs={{0,6},{2,0},{4,2},{6,4},{1,7},{3,1},{5,3},{7,5},{8,14},{10,8},{12,... | collective-permute-start | bytes 1376264 | tf_op jit(solution)/shard_map/ppermute | solution.py:19
  118.1 3.0 %copy-start.1 = (bf16[1792,1024]{1,0:T(8,128)(2,1)S(1)}, bf16[1792,1024]{1,0:T(8,128)(2,1)}, u32[]{:S(2)}) copy-start(bf16[1792,1024]{1,0:T(8,128)(2,1)} %param.8) | copy-start | bytes 11010052
  126.5 30.2 %collective-permute-start.12 = (bf16[192,1792]{1,0:T(8,128)(2,1)S(1)}, bf16[192,1792]{1,0:T(8,128)(2,1)S(1)}, u32[]{:S(2)}, u32[]{:S(2)}) collective-permute-start(bf16[192,1792]{1,0:T(8,128)(2,1)S(1)} %convolution_convert_fusion), channel_id=1, source_target_pairs={{0,6},{2,0},{4,2},{6,4},{1,7},{3,1},{5,3},{7,5},{8,14},{10,8},{12,... | collective-permute-start | bytes 2064392 | tf_op jit(solution)/shard_map/ppermute | solution.py:19
  129.1 27.6 %collective-permute-start.11 = (bf16[192,1792]{1,0:T(8,128)(2,1)S(1)}, bf16[192,1792]{1,0:T(8,128)(2,1)S(1)}, u32[]{:S(2)}, u32[]{:S(2)}) collective-permute-start(bf16[192,1792]{1,0:T(8,128)(2,1)S(1)} %convolution_convert_fusion.1), channel_id=1, source_target_pairs={{0,2},{2,4},{4,6},{6,0},{1,3},{3,5},{5,7},{7,1},{8,10},{10,12},{12... | collective-permute-start | bytes 2064392 | tf_op jit(solution)/shard_map/ppermute | solution.py:19
  130.2 24.7 %collective-permute-start.6 = (bf16[192,1792]{1,0:T(8,128)(2,1)S(1)}, bf16[192,1792]{1,0:T(8,128)(2,1)S(1)}, u32[]{:S(2)}, u32[]{:S(2)}) collective-permute-start(bf16[192,1792]{1,0:T(8,128)(2,1)S(1)} %convolution_convert_fusion.2), channel_id=1, source_target_pairs={{0,1},{1,0},{2,3},{3,2},{4,5},{5,4},{6,7},{7,6},{8,9},{9,8},{10,11... | collective-permute-start | bytes 2064392 | tf_op jit(solution)/shard_map/ppermute | solution.py:23
  133.8 18.7 %collective-permute-start.33 = (bf16[128,1792]{1,0:T(8,128)(2,1)S(1)}, bf16[128,1792]{1,0:T(8,128)(2,1)S(1)}, u32[]{:S(2)}, u32[]{:S(2)}) collective-permute-start(bf16[128,1792]{1,0:T(8,128)(2,1)S(1)} %constant_dynamic-update-slice_fusion.12), channel_id=1, source_target_pairs={{0,1},{1,0},{2,3},{3,2},{4,5},{5,4},{6,7},{7,6},{8,9},{9,8},{10,11... | collective-permute-start | bytes 1376264 | tf_op jit(solution)/shard_map/ppermute | solution.py:23
  156.3 12.2 %collective-permute-start.7 = (bf16[96,1792]{1,0:T(8,128)(2,1)S(1)}, bf16[96,1792]{1,0:T(8,128)(2,1)S(1)}, u32[]{:S(2)}, u32[]{:S(2)}) collective-permute-start(bf16[96,1792]{1,0:T(8,128)(2,1)S(1)} %get-tuple-element.18), channel_id=1, source_target_pairs={{0,2},{2,4},{4,6},{6,0},{1,3},{3,5},{5,7},{7,1},{8,10},{10,12},{12... | collective-permute-start | bytes 1032200 | tf_op jit(solution)/shard_map/ppermute | solution.py:19
  158.1 26.1 %collective-permute-start.13 = (bf16[192,1792]{1,0:T(8,128)(2,1)S(1)}, bf16[192,1792]{1,0:T(8,128)(2,1)S(1)}, u32[]{:S(2)}, u32[]{:S(2)}) collective-permute-start(bf16[192,1792]{1,0:T(8,128)(2,1)S(1)} %fusion.4), channel_id=1, source_target_pairs={{0,1},{1,0},{2,3},{3,2},{4,5},{5,4},{6,7},{7,6},{8,9},{9,8},{10,11... | collective-permute-start | bytes 2064392 | tf_op jit(solution)/shard_map/ppermute | solution.py:23
  161.1 11.5 %collective-permute-start.9 = (bf16[96,1792]{1,0:T(8,128)(2,1)S(1)}, bf16[96,1792]{1,0:T(8,128)(2,1)S(1)}, u32[]{:S(2)}, u32[]{:S(2)}) collective-permute-start(bf16[96,1792]{1,0:T(8,128)(2,1)S(1)} %get-tuple-element.19), channel_id=1, source_target_pairs={{0,6},{2,0},{4,2},{6,4},{1,7},{3,1},{5,3},{7,5},{8,14},{10,8},{12,... | collective-permute-start | bytes 1032200 | tf_op jit(solution)/shard_map/ppermute | solution.py:19
  168.6 15.6 %collective-permute-start.8 = (bf16[192,1792]{1,0:T(8,128)(2,1)S(1)}, bf16[192,1792]{1,0:T(8,128)(2,1)S(1)}, u32[]{:S(2)}, u32[]{:S(2)}) collective-permute-start(bf16[192,1792]{1,0:T(8,128)(2,1)S(1)} %pad_maximum_fusion), channel_id=1, source_target_pairs={{0,2},{2,4},{4,6},{6,0},{1,3},{3,5},{5,7},{7,1},{8,10},{10,12},{12... | collective-permute-start | bytes 2064392 | tf_op jit(solution)/shard_map/ppermute | solution.py:19
  172.7 12.4 %collective-permute-start.10 = (bf16[192,1792]{1,0:T(8,128)(2,1)S(1)}, bf16[192,1792]{1,0:T(8,128)(2,1)S(1)}, u32[]{:S(2)}, u32[]{:S(2)}) collective-permute-start(bf16[192,1792]{1,0:T(8,128)(2,1)S(1)} %pad_maximum_fusion.1), channel_id=1, source_target_pairs={{0,6},{2,0},{4,2},{6,4},{1,7},{3,1},{5,3},{7,5},{8,14},{10,8},{12,... | collective-permute-start | bytes 2064392 | tf_op jit(solution)/shard_map/ppermute | solution.py:19

commit v2 on v1

v2 whole, which is shorter than its diff:
```python
import jax
import jax.numpy as jnp
from jax import lax
from jax.sharding import Mesh, PartitionSpec as P

beta_one = 0.9
beta_two = 0.999
corr_one = 1.0 - 0.9**10
corr_two = 1.0 - 0.999**10
eps_adam = 1e-08
galore_scale = 0.25

F32 = jnp.float32
BF16 = jnp.bfloat16


def ring(axis, step):
    pairs = [(i, (i + step) % 4) for i in range(4)]
    return lambda a: lax.ppermute(a, axis, pairs)


def swap(axis):
    return lambda a: lax.ppermute(a, axis, [(0, 1), (1, 0)])


z_up, z_down = ring("z", 1), ring("z", 3)
z_two = ring("z", 2)
y_up, y_down, y_two = ring("y", 1), ring("y", 3), ring("y", 2)
x_far, x_near, core = swap("xh"), swap("xl"), swap("c")


def transpose_blocks(a):
    pairs = []
    for y in range(4):
        for xl in range(2):
            for z in range(4):
                for xh in range(2):
                    pairs.append((((y * 2 + xl) * 4 + z) * 2 + xh, ((z * 2 + xh) * 4 + y) * 2 + xl))
    return lax.ppermute(a, ("y", "xl", "z", "xh"), pairs)


def pair_tokens(a):
    other = x_near(a)
    same = lax.axis_index("xl") == lax.axis_index("xh")
    return jnp.concatenate([jnp.where(same, a, other), jnp.where(same, other, a)], axis=0)


def ring_tokens(pair):
    up, down, two = y_down(pair), y_up(pair), y_two(pair)
    return jnp.concatenate([pair, up, two, down], axis=0)


def token_block(a, i):
    y, z = lax.axis_index("y"), lax.axis_index("z")
    return lax.dynamic_slice_in_dim(a, ((z - y + i // 2) % 4 * 2 + i % 2) * 192, 192, axis=0)


def dot(a, b, ca, cb):
    return lax.dot_general(a, b, (((ca,), (cb,)), ((), ())), preferred_element_type=F32)


def shards(hidden, grad_out, weight, basis, first_moment, second_moment):
    c, z, xh = (lax.axis_index(n) for n in ("c", "z", "xh"))
    w_mine = lax.dynamic_slice_in_dim(weight, c * 512, 512, axis=1)
    w_other = lax.dynamic_slice_in_dim(weight, (1 - c) * 512, 512, axis=1)

    t = transpose_blocks(grad_out)
    hx, hbelow, habove = x_far(hidden), z_up(hidden), z_down(hidden)
    pair = pair_tokens(t)
    part = dot(t, lax.dynamic_slice_in_dim(basis, c * 512, 512, axis=0), 1, 0).astype(BF16)
    part = part.reshape(192, 8, 128).transpose(1, 0, 2)
    part, pair, hx, hbelow, habove = lax.optimization_barrier((part, pair, hx, hbelow, habove))

    hxbelow, hxabove = z_up(hx), z_down(hx)
    part = lax.all_to_all(part, ("z", "xh"), 0, 0, tiled=True)
    half = ring_tokens(pair)
    mine = jnp.sum(part.astype(F32), axis=0).astype(BF16)
    mine, half, hxbelow, hxabove = lax.optimization_barrier((mine, half, hxbelow, hxabove))
    hfirst, hsecond = z_up(hbelow[:96]), z_down(habove[96:])
    other = core(half)
    mine = (mine.astype(F32) + core(mine).astype(F32)).astype(BF16)
    mine = pair_tokens(mine)

    def partial(i):
        return dot(token_block(half, i), w_mine, 1, 1) + dot(token_block(other, i), w_other, 1, 1)

    xup, xdown = partial(3).astype(BF16), partial(7).astype(BF16)
    mine, xup, xdown, hfirst, hsecond = lax.optimization_barrier((mine, xup, xdown, hfirst, hsecond))
    xup, xdown = z_up(xup), z_down(xdown)
    far = x_far(partial(5).astype(BF16))
    htwo = jnp.concatenate([hfirst, hsecond], axis=0)
    hxtwo = x_far(htwo)
    low = ring_tokens(mine)
    low, far, xup, xdown = lax.optimization_barrier((low, far, xup, xdown))
    two = (partial(4) + far.astype(F32)).astype(BF16)
    first, second = z_up(two[:96]), z_down(two[96:])

    projected = jnp.zeros((128, 1792), F32)
    for i, block in enumerate([hidden, hx, habove, hxabove, htwo, hxtwo, hbelow, hxbelow]):
        projected = projected + dot(token_block(low, i), block, 0, 0).astype(BF16).astype(F32)
    new_first = beta_one * first_moment + (1.0 - beta_one) * projected
    new_second = beta_two * second_moment + (1.0 - beta_two) * projected * projected
    direction = (new_first / corr_one / (jnp.sqrt(new_second / corr_two) + eps_adam)).astype(BF16)

    direction, first, second = lax.optimization_barrier((direction, first, second))

    dx, dbelow, dabove, dtwo = x_far(direction), z_up(direction), z_down(direction), z_two(direction)
    dxbelow, dxabove, dxtwo = z_up(dx), z_down(dx), x_far(dtwo)

    def columns(side):
        starts = [(((z + r) % 4) * 2 + side) * 128 for r in range(4)]
        return jnp.concatenate([lax.dynamic_slice_in_dim(basis, s, 128, axis=1) for s in starts], axis=1)

    expanded = dot(jnp.concatenate([direction, dabove, dtwo, dbelow], axis=0), columns(xh), 0, 1)
    expanded += dot(jnp.concatenate([dx, dxabove, dxtwo, dxbelow], axis=0), columns(1 - xh), 0, 1)
    update = (galore_scale * expanded).astype(BF16)

    up, down = partial(2), partial(6)
    up = jnp.concatenate([up[:96] + first.astype(F32), up[96:]], axis=0).astype(BF16)
    down = jnp.concatenate([down[:96], down[96:] + second.astype(F32)], axis=0).astype(BF16)
    up, down = z_up(up), z_down(down)
    xsum = x_far((partial(1) + xup.astype(F32) + xdown.astype(F32)).astype(BF16))
    grad_hidden = (partial(0) + up.astype(F32) + down.astype(F32) + xsum.astype(F32)).astype(BF16)
    return (grad_hidden, update, new_first, new_second)


def solution(mesh):
    fine = Mesh(mesh.devices.reshape(4, 2, 2, 4, 2), ("y", "xl", "c", "z", "xh"))
    fsdp, dp = ("z", "xh"), ("y", "xl", "c")
    return jax.shard_map(
        shards,
        mesh=fine,
        in_specs=(
            P(fsdp, dp),
            P(fsdp, dp),
            P(dp, fsdp),
            P(fsdp, None),
            P(fsdp, dp),
            P(fsdp, dp),
        ),
        out_specs=(P(fsdp, dp), P(dp, fsdp), P(fsdp, dp), P(fsdp, dp)),
        check_vma=False,
    )
```

time: 189 us -> 176 us (0.931)
  starting transfers between devices: 78.1 us -> 55.8 us
  local copies, waits for them, and re-layouts: 21.2 us -> 4 us
  blocking collectives: 0 us -> 16.2 us
  waiting for transfers between devices: 50.2 us -> 66 us
  other arithmetic: 6.22 us -> 2.12 us
    ppermute x10, waiting for transfers between devices: 19.5 us -> 41.3 us  [swap(): return lambda a: lax.ppermute(a, axis, [(0, 1), (1, 0)])]
    all_to_all x0 -> x1, blocking collectives: none -> 16.2 us  [shards(): part = lax.all_to_all(part, ('z', 'xh'), 0, 0, tiled=True)]
    ppermute x10, starting transfers between devices: 25.8 us -> 15 us  [swap(): return lambda a: lax.ppermute(a, axis, [(0, 1), (1, 0)])]
    all_to_all x1 -> x0, starting transfers between devices: 8.43 us -> none  [shards(): part = lax.all_to_all(part, ('z', 'xh'), 0, 0, tiled=True)]
    ppermute x24 -> x23, waiting for transfers between devices: 30.8 us -> 24.7 us  [ring(): return lambda a: lax.ppermute(a, axis, pairs)]
    dynamic_update_slice x7 -> x0, local copies, waits for them, and re-layouts: 5.6 us -> none  [shards(): ranks = lax.dynamic_update_slice_in_dim(ranks, block, place * 128, axis=0)]
    unnamed x16 -> x21, local copies, waits for them, and re-layouts: 5.4 us -> 1.24 us
    slice x7 -> x2, local copies, waits for them, and re-layouts: 5.39 us -> 2.01 us  [shards(): hfirst, hsecond = (z_up(hbelow[:96]), z_down(habove[96:]))]
  transfers between devices with their start and end apart: 36 -> 34, of which waited for: 10 -> 16; matrix products, arithmetic and copies ran while one was open for 28% -> 18% of each run, Pallas kernels for 0% -> 0%
where the time goes in v2:
time: 176 us; the launch traced here: 175 us
  waiting for transfers between devices  66 us (38%)
  starting transfers between devices  55.8 us (32%)
  matrix products  30 us (17%)
  blocking collectives  16.2 us (9%)
  local copies, waits for them, and re-layouts  4 us (2%)
  other arithmetic  2.12 us (1%)
    ppermute x10, waiting for transfers between devices, swap(): return lambda a: lax.ppermute(a, axis, [(0, 1), (1, 0)])  41.3 us
    ppermute x23, starting transfers between devices, ring(): return lambda a: lax.ppermute(a, axis, pairs)  39.2 us
    dot_general x27, matrix products, dot(): lax.dot_general(a, b, (((ca,), (cb,)), ((), ())), preferred_element_type=...  30 us
    ppermute x23, waiting for transfers between devices, ring(): return lambda a: lax.ppermute(a, axis, pairs)  24.7 us
    all_to_all x1, blocking collectives, shards(): part = lax.all_to_all(part, ('z', 'xh'), 0, 0, tiled=True)  16.2 us
    ppermute x10, starting transfers between devices, swap(): return lambda a: lax.ppermute(a, axis, [(0, 1), (1, 0)])  15 us
  transfers between devices with their start and end apart: 34, of which 16 were waited for; matrix products, arithmetic and copies ran while one was open for 18% of the time, Pallas kernels for 0%

profile of v2, /device:TPU:0, one launch (start us, length us, event | category | flops | bytes accessed | tf_op | source)
XLA Modules:
  0.0 175.2 jit_solution(12371634196424458679)
XLA Ops:
  0.6 1.6 collective-permute-start
  2.2 3.5 %collective-permute-start.3 = (bf16[192,1792]{1,0:T(8,128)(2,1)}, bf16[192,1792]{1,0:T(8,128)(2,1)S(1)}, u32[]{:S(2)}, u32[]{:S(2)}) collective-permute-start(bf16[192,1792]{1,0:T(8,128)(2,1)} %param.6), channel_id=1, source_target_pairs={{0,2},{2,4},{4,6},{6,0},{1,3},{3,5},{5,7},{7,1},{8,10},{10,12},{12... | collective-permute-start | bytes 2064392 | tf_op jit(solution)/shard_map/ppermute | solution.py:19
  5.7 3.0 %collective-permute-start.2 = (bf16[192,1792]{1,0:T(8,128)(2,1)}, bf16[192,1792]{1,0:T(8,128)(2,1)}, u32[]{:S(2)}, u32[]{:S(2)}) collective-permute-start(bf16[192,1792]{1,0:T(8,128)(2,1)} %param.6), channel_id=1, source_target_pairs={{0,1},{1,0},{2,3},{3,2},{4,5},{5,4},{6,7},{7,6},{8,9},{9,8},{10,11... | collective-permute-start | bytes 2064392 | tf_op jit(solution)/shard_map/ppermute | solution.py:23
  8.7 2.7 %collective-permute-start.4 = (bf16[192,1792]{1,0:T(8,128)(2,1)}, bf16[192,1792]{1,0:T(8,128)(2,1)S(1)}, u32[]{:S(2)}, u32[]{:S(2)}) collective-permute-start(bf16[192,1792]{1,0:T(8,128)(2,1)} %param.6), channel_id=1, source_target_pairs={{0,6},{2,0},{4,2},{6,4},{1,7},{3,1},{5,3},{7,5},{8,14},{10,8},{12,... | collective-permute-start | bytes 2064392 | tf_op jit(solution)/shard_map/ppermute | solution.py:19
  12.1 1.6 fusion.42
  13.8 14.6 %collective-permute-done.1 = bf16[192,512]{1,0:T(8,128)(2,1)S(1)} collective-permute-done((bf16[192,512]{1,0:T(8,128)(2,1)S(1)}, bf16[192,512]{1,0:T(8,128)(2,1)S(1)}, u32[]{:S(2)}, u32[]{:S(2)}) %collective-permute-start.1) | collective-permute-done | bytes 196640 | tf_op jit(solution)/shard_map/ppermute | solution.py:23
  28.9 1.0 collective-permute-done.4
  29.9 10.0 %collective-permute-start.9 = (bf16[192,1792]{1,0:T(8,128)(2,1)}, bf16[192,1792]{1,0:T(8,128)(2,1)}, u32[]{:S(2)}, u32[]{:S(2)}) collective-permute-start(bf16[192,1792]{1,0:T(8,128)(2,1)} %collective-permute-done.2), channel_id=1, source_target_pairs={{0,6},{2,0},{4,2},{6,4},{1,7},{3,1},{5,3},{7,5},{8,14},{10,8},{12,... | collective-permute-start | bytes 2064392 | tf_op jit(solution)/shard_map/ppermute | solution.py:19
  39.9 0.9 collective-permute-start.7
  40.8 1.0 collective-permute-start.6
  41.8 2.6 %collective-permute-start.5 = (bf16[384,512]{1,0:T(8,128)(2,1)S(1)}, bf16[384,512]{1,0:T(8,128)(2,1)}, u32[]{:S(2)}, u32[]{:S(2)}) collective-permute-start(bf16[384,512]{1,0:T(8,128)(2,1)S(1)} %pad_maximum_fusion.3), channel_id=1, source_target_pairs={{0,96},{32,0},{64,32},{96,64},{1,97},{33,1},{65,33},{97,65},{2,98}... | collective-permute-start | bytes 1179656 | tf_op jit(solution)/shard_map/ppermute | solution.py:19
  44.4 16.2 %all_to_all.5 = bf16[8,192,128]{2,1,0:T(8,128)(2,1)S(1)} all-to-all(bf16[8,192,128]{2,1,0:T(8,128)(2,1)S(1)} %bitcast.18), channel_id=1, replica_groups=mesh['y'=4,'xl'=2,'c'=2,'z'=4,'xh'=2] {'z','xh'}, dimensions={0} | all-to-all | bytes 786432 | tf_op jit(solution)/shard_map/all_to_all | solution.py:75
  61.3 1.1 pad_maximum_fusion
  63.0 3.0 %collective-permute-done.11 = bf16[192,128]{1,0:T(8,128)(2,1)S(1)} collective-permute-done((bf16[192,128]{1,0:T(8,128)(2,1)S(1)}, bf16[192,128]{1,0:T(8,128)(2,1)S(1)}, u32[]{:S(2)}, u32[]{:S(2)}) %collective-permute-start.11) | collective-permute-done | bytes 49184 | tf_op jit(solution)/shard_map/ppermute | solution.py:23
  66.0 1.5 collective-permute-start.12
  67.5 1.0 slice.27
  68.5 1.0 slice.28
  70.3 1.4 collective-permute-start.13
  71.7 2.4 %fusion.69 = f32[192,1792]{1,0:T(8,128)S(1)} fusion(bf16[1792,1024]{1,0:T(8,128)(2,1)} %param.8, s32[]{:T(128)S(6)} %select_n.184, bf16[1536,512]{1,0:T(8,128)(2,1)S(1)} %collective-permute-done.10, s32[]{:T(128)S(6)} %select_n.192), kind=kOutput, calls=%fused_computation.100 | convolution fusion | flops 352321536 | bytes 3407880 | tf_op jit(solution)/shard_map/dot_general | solution.py:59
  76.6 2.8 %collective-permute-done.14 = bf16[96,1792]{1,0:T(8,128)(2,1)S(1)} collective-permute-done((bf16[96,1792]{1,0:T(8,128)(2,1)S(1)}, bf16[96,1792]{1,0:T(8,128)(2,1)S(1)}, u32[]{:S(2)}, u32[]{:S(2)}) %collective-permute-start.14) | collective-permute-done | bytes 344096 | tf_op jit(solution)/shard_map/ppermute | solution.py:19
  79.4 1.6 collective-permute-done.13
  81.0 0.9 collective-permute-start.17
  82.0 3.2 %collective-permute-start.16 = (bf16[384,128]{1,0:T(8,128)(2,1)S(1)}, bf16[384,128]{1,0:T(8,128)(2,1)S(1)}, u32[]{:S(2)}, u32[]{:S(2)}) collective-permute-start(bf16[384,128]{1,0:T(8,128)(2,1)S(1)} %pad_maximum_fusion.5), channel_id=1, source_target_pairs={{0,64},{32,96},{64,0},{96,32},{1,65},{33,97},{65,1},{97,33},{2,66}... | collective-permute-start | bytes 294920 | tf_op jit(solution)/shard_map/ppermute | solution.py:19
  88.3 2.0 %collective-permute-start.18 = (bf16[192,1792]{1,0:T(8,128)(2,1)S(1)}, bf16[192,1792]{1,0:T(8,128)(2,1)S(1)}, u32[]{:S(2)}, u32[]{:S(2)}) collective-permute-start(bf16[192,1792]{1,0:T(8,128)(2,1)S(1)} %fusion.9), channel_id=1, source_target_pairs={{0,1},{1,0},{2,3},{3,2},{4,5},{5,4},{6,7},{7,6},{8,9},{9,8},{10,11... | collective-permute-start | bytes 2064392 | tf_op jit(solution)/shard_map/ppermute | solution.py:23
  90.4 3.2 %collective-permute-start.20 = (bf16[192,1792]{1,0:T(8,128)(2,1)S(1)}, bf16[192,1792]{1,0:T(8,128)(2,1)S(1)}, u32[]{:S(2)}, u32[]{:S(2)}) collective-permute-start(bf16[192,1792]{1,0:T(8,128)(2,1)S(1)} %fusion.8), channel_id=1, source_target_pairs={{0,6},{2,0},{4,2},{6,4},{1,7},{3,1},{5,3},{7,5},{8,14},{10,8},{12,... | collective-permute-start | bytes 2064392 | tf_op jit(solution)/shard_map/ppermute | solution.py:19
  96.9 1.8 %collective-permute-start.21 = (bf16[192,1792]{1,0:T(8,128)(2,1)S(1)}, bf16[192,1792]{1,0:T(8,128)(2,1)S(1)}, u32[]{:S(2)}, u32[]{:S(2)}) collective-permute-start(bf16[192,1792]{1,0:T(8,128)(2,1)S(1)} %constant_dynamic-update-slice_fusion), channel_id=1, source_target_pairs={{0,1},{1,0},{2,3},{3,2},{4,5},{5,4},{6,7},{7,6},{8,9},{9,8},{10,11... | collective-permute-start | bytes 2064392 | tf_op jit(solution)/shard_map/ppermute | solution.py:23
  98.7 2.0 %collective-permute-done.15 = bf16[384,128]{1,0:T(8,128)(2,1)S(1)} collective-permute-done((bf16[384,128]{1,0:T(8,128)(2,1)S(1)}, bf16[384,128]{1,0:T(8,128)(2,1)S(1)}, u32[]{:S(2)}, u32[]{:S(2)}) %collective-permute-start.15) | collective-permute-done | bytes 98336 | tf_op jit(solution)/shard_map/ppermute | solution.py:19
  100.7 7.5 %collective-permute-done.18 = bf16[192,1792]{1,0:T(8,128)(2,1)S(1)} collective-permute-done((bf16[192,1792]{1,0:T(8,128)(2,1)S(1)}, bf16[192,1792]{1,0:T(8,128)(2,1)S(1)}, u32[]{:S(2)}, u32[]{:S(2)}) %collective-permute-start.18) | collective-permute-done | bytes 688160 | tf_op jit(solution)/shard_map/ppermute | solution.py:23
  109.1 1.0 copy-done.5
  110.5 1.8 %collective-permute-start.23 = (bf16[96,1792]{1,0:T(8,128)(2,1)S(1)}, bf16[96,1792]{1,0:T(8,128)(2,1)S(1)}, u32[]{:S(2)}, u32[]{:S(2)}) collective-permute-start(bf16[96,1792]{1,0:T(8,128)(2,1)S(1)} %get-tuple-element.57), channel_id=1, source_target_pairs={{0,6},{2,0},{4,2},{6,4},{1,7},{3,1},{5,3},{7,5},{8,14},{10,8},{12,... | collective-permute-start | bytes 1032200 | tf_op jit(solution)/shard_map/ppermute | solution.py:19
  113.4 2.0 %collective-permute-start.26 = (bf16[192,1792]{1,0:T(8,128)(2,1)S(1)}, bf16[192,1792]{1,0:T(8,128)(2,1)S(1)}, u32[]{:S(2)}, u32[]{:S(2)}) collective-permute-start(bf16[192,1792]{1,0:T(8,128)(2,1)S(1)} %fusion.11), channel_id=1, source_target_pairs={{0,1},{1,0},{2,3},{3,2},{4,5},{5,4},{6,7},{7,6},{8,9},{9,8},{10,11... | collective-permute-start | bytes 2064392 | tf_op jit(solution)/shard_map/ppermute | solution.py:23
  115.7 1.4 fusion.25
  117.5 1.4 fusion.21
  119.2 3.8 %collective-permute-done.21 = bf16[192,1792]{1,0:T(8,128)(2,1)S(1)} collective-permute-done((bf16[192,1792]{1,0:T(8,128)(2,1)S(1)}, bf16[192,1792]{1,0:T(8,128)(2,1)S(1)}, u32[]{:S(2)}, u32[]{:S(2)}) %collective-permute-start.21) | collective-permute-done | bytes 688160 | tf_op jit(solution)/shard_map/ppermute | solution.py:23
  123.4 3.2 %divide_convert_fusion = (bf16[128,1792]{1,0:T(8,128)(2,1)S(1)}, f32[128,1792]{1,0:T(8,128)}, f32[128,1792]{1,0:T(8,128)}) fusion(f32[128,1792]{1,0:T(8,128)S(1)} %copy-done.8, f32[128,1792]{1,0:T(8,128)S(1)} %copy-done.9, f32[128,1792]{1,0:T(8,128)S(1)} %fusion.17, bf16[192,1792]{1,0:T(8,128)(2,1)} %collective-permute-done.8, ...), kind=kOutput, calls=%fused_computation.79 | convolution fusion | flops 91521024 | bytes 5783556 | tf_op jit(solution)/shard_map/dot_general | solution.py:59
  126.5 1.9 %collective-permute-start.30 = (bf16[128,1792]{1,0:T(8,128)(2,1)S(1)}, bf16[128,1792]{1,0:T(8,128)(2,1)S(1)}, u32[]{:S(2)}, u32[]{:S(2)}) collective-permute-start(bf16[128,1792]{1,0:T(8,128)(2,1)S(1)} %get-tuple-element.45), channel_id=1, source_target_pairs={{0,1},{1,0},{2,3},{3,2},{4,5},{5,4},{6,7},{7,6},{8,9},{9,8},{10,11... | collective-permute-start | bytes 1376264 | tf_op jit(solution)/shard_map/ppermute | solution.py:23
  128.4 1.7 collective-permute-start.28
  130.1 1.5 collective-permute-start.27
  131.9 5.9 %collective-permute-done.26 = bf16[192,1792]{1,0:T(8,128)(2,1)S(1)} collective-permute-done((bf16[192,1792]{1,0:T(8,128)(2,1)S(1)}, bf16[192,1792]{1,0:T(8,128)(2,1)S(1)}, u32[]{:S(2)}, u32[]{:S(2)}) %collective-permute-start.26) | collective-permute-done | bytes 688160 | tf_op jit(solution)/shard_map/ppermute | solution.py:23
  138.0 6.6 %collective-permute-done.30 = bf16[128,1792]{1,0:T(8,128)(2,1)S(1)} collective-permute-done((bf16[128,1792]{1,0:T(8,128)(2,1)S(1)}, bf16[128,1792]{1,0:T(8,128)(2,1)S(1)}, u32[]{:S(2)}, u32[]{:S(2)}) %collective-permute-start.30) | collective-permute-done | bytes 458784 | tf_op jit(solution)/shard_map/ppermute | solution.py:23
  146.8 3.2 %collective-permute-start.31 = (bf16[128,1792]{1,0:T(8,128)(2,1)S(1)}, bf16[128,1792]{1,0:T(8,128)(2,1)S(1)}, u32[]{:S(2)}, u32[]{:S(2)}) collective-permute-start(bf16[128,1792]{1,0:T(8,128)(2,1)S(1)} %collective-permute-done.30), channel_id=1, source_target_pairs={{0,6},{2,0},{4,2},{6,4},{1,7},{3,1},{5,3},{7,5},{8,14},{10,8},{12,... | collective-permute-start | bytes 1376264 | tf_op jit(solution)/shard_map/ppermute | solution.py:19
  150.0 3.7 %collective-permute-done.27 = bf16[128,1792]{1,0:T(8,128)(2,1)S(1)} collective-permute-done((bf16[128,1792]{1,0:T(8,128)(2,1)S(1)}, bf16[128,1792]{1,0:T(8,128)(2,1)S(1)}, u32[]{:S(2)}, u32[]{:S(2)}) %collective-permute-start.27) | collective-permute-done | bytes 458784 | tf_op jit(solution)/shard_map/ppermute | solution.py:19
  153.8 1.7 collective-permute-start.32
  155.4 2.1 %fusion.27 = f32[1792,1024]{1,0:T(8,128)S(1)} fusion(bf16[128,1792]{1,0:T(8,128)(2,1)S(1)} %collective-permute-done.29, bf16[128,1792]{1,0:T(8,128)(2,1)S(1)} %collective-permute-done.28, bf16[128,1792]{1,0:T(8,128)(2,1)S(1)} %collective-permute-done.27, bf16[128,1792]{1,0:T(8,128)(2,1)S(1)} %get-tuple-element.45, ...), kind=kOutput, calls=%fused_computation.44 | convolution fusion | flops 1890582528 | bytes 10223616 | tf_op jit(solution)/shard_map/dot_general | solution.py:59
  157.6 9.1 %collective-permute-done.25 = bf16[192,1792]{1,0:T(8,128)(2,1)S(1)} collective-permute-done((bf16[192,1792]{1,0:T(8,128)(2,1)S(1)}, bf16[192,1792]{1,0:T(8,128)(2,1)S(1)}, u32[]{:S(2)}, u32[]{:S(2)}) %collective-permute-start.25) | collective-permute-done | bytes 688160 | tf_op jit(solution)/shard_map/ppermute | solution.py:19
  166.6 1.8 %fusion.6 = bf16[192,1792]{1,0:T(8,128)(2,1)} fusion(f32[192,1792]{1,0:T(8,128)S(1)} %fusion.75, bf16[192,1792]{1,0:T(8,128)(2,1)S(1)} %collective-permute-done.26, bf16[192,1792]{1,0:T(8,128)(2,1)S(1)} %collective-permute-done.25, bf16[192,1792]{1,0:T(8,128)(2,1)S(1)} %collective-permute-done.24, bf16[1792,1024]{1,0:T(8,128)(2,1)S(1)} %copy-done, ...), kind=kOutput, calls=%fused_computation.15 | convolution fusion | flops 355074048 | bytes 6160392 | tf_op jit(solution)/shard_map/dot_general | solution.py:59
  168.4 2.7 %collective-permute-done.33 = bf16[128,1792]{1,0:T(8,128)(2,1)S(1)} collective-permute-done((bf16[128,1792]{1,0:T(8,128)(2,1)S(1)}, bf16[128,1792]{1,0:T(8,128)(2,1)S(1)}, u32[]{:S(2)}, u32[]{:S(2)}) %collective-permute-start.33) | collective-permute-done | bytes 458784 | tf_op jit(solution)/shard_map/ppermute | solution.py:19
  171.6 3.6 %multiply_convert_fusion = bf16[1792,1024]{1,0:T(8,128)(2,1)} fusion(f32[1792,1024]{1,0:T(8,128)S(1)} %fusion.27, bf16[128,1792]{1,0:T(8,128)(2,1)S(1)} %collective-permute-done.33, bf16[128,1792]{1,0:T(8,128)(2,1)S(1)} %collective-permute-done.32, bf16[128,1792]{1,0:T(8,128)(2,1)S(1)} %collective-permute-done.31, ...), kind=kOutput, calls=%fused_computation | convolution fusion | flops 1896087552 | bytes 13893632 | tf_op jit(solution)/shard_map/dot_general | solution.py:59
  (89 shorter events, 18.9 us)
Async XLA Ops:
  0.6 10.8 %collective-permute-start = (bf16[192,512]{1,0:T(8,128)(2,1)}, bf16[192,512]{1,0:T(8,128)(2,1)S(1)}, u32[]{:S(2)}, u32[]{:S(2)}) collective-permute-start(bf16[192,512]{1,0:T(8,128)(2,1)} %param.7), channel_id=1, source_target_pairs={{0,0},{1,16},{2,32},{3,48},{4,64},{5,80},{6,96},{7,112},{16,1},{17... | collective-permute-start | bytes 589832 | tf_op jit(solution)/shard_map/ppermute | solution.py:39
  2.2 26.6 %collective-permute-start.3 = (bf16[192,1792]{1,0:T(8,128)(2,1)}, bf16[192,1792]{1,0:T(8,128)(2,1)S(1)}, u32[]{:S(2)}, u32[]{:S(2)}) collective-permute-start(bf16[192,1792]{1,0:T(8,128)(2,1)} %param.6), channel_id=1, source_target_pairs={{0,2},{2,4},{4,6},{6,0},{1,3},{3,5},{5,7},{7,1},{8,10},{10,12},{12... | collective-permute-start | bytes 2064392 | tf_op jit(solution)/shard_map/ppermute | solution.py:19
  5.7 23.1 %collective-permute-start.2 = (bf16[192,1792]{1,0:T(8,128)(2,1)}, bf16[192,1792]{1,0:T(8,128)(2,1)}, u32[]{:S(2)}, u32[]{:S(2)}) collective-permute-start(bf16[192,1792]{1,0:T(8,128)(2,1)} %param.6), channel_id=1, source_target_pairs={{0,1},{1,0},{2,3},{3,2},{4,5},{5,4},{6,7},{7,6},{8,9},{9,8},{10,11... | collective-permute-start | bytes 2064392 | tf_op jit(solution)/shard_map/ppermute | solution.py:23
  8.7 21.2 %collective-permute-start.4 = (bf16[192,1792]{1,0:T(8,128)(2,1)}, bf16[192,1792]{1,0:T(8,128)(2,1)S(1)}, u32[]{:S(2)}, u32[]{:S(2)}) collective-permute-start(bf16[192,1792]{1,0:T(8,128)(2,1)} %param.6), channel_id=1, source_target_pairs={{0,6},{2,0},{4,2},{6,4},{1,7},{3,1},{5,3},{7,5},{8,14},{10,8},{12,... | collective-permute-start | bytes 2064392 | tf_op jit(solution)/shard_map/ppermute | solution.py:19
  11.5 16.9 %collective-permute-start.1 = (bf16[192,512]{1,0:T(8,128)(2,1)S(1)}, bf16[192,512]{1,0:T(8,128)(2,1)S(1)}, u32[]{:S(2)}, u32[]{:S(2)}) collective-permute-start(bf16[192,512]{1,0:T(8,128)(2,1)S(1)} %collective-permute-done), channel_id=1, source_target_pairs={{0,16},{16,0},{1,17},{17,1},{2,18},{18,2},{3,19},{19,3},{4,20},{20... | collective-permute-start | bytes 589832 | tf_op jit(solution)/shard_map/ppermute | solution.py:23
  28.9 33.6 %copy-start.4 = (bf16[192,1792]{1,0:T(8,128)(2,1)}, bf16[192,1792]{1,0:T(8,128)(2,1)S(1)}, u32[]{:S(2)}) copy-start(bf16[192,1792]{1,0:T(8,128)(2,1)S(1)} %collective-permute-done.3) | copy-start | bytes 2064388
  29.9 31.4 %copy-start.2 = (bf16[192,1792]{1,0:T(8,128)(2,1)}, bf16[192,1792]{1,0:T(8,128)(2,1)S(1)}, u32[]{:S(2)}) copy-start(bf16[192,1792]{1,0:T(8,128)(2,1)S(1)} %collective-permute-done.4) | copy-start | bytes 2064388
  29.9 32.5 %collective-permute-start.9 = (bf16[192,1792]{1,0:T(8,128)(2,1)}, bf16[192,1792]{1,0:T(8,128)(2,1)}, u32[]{:S(2)}, u32[]{:S(2)}) collective-permute-start(bf16[192,1792]{1,0:T(8,128)(2,1)} %collective-permute-done.2), channel_id=1, source_target_pairs={{0,6},{2,0},{4,2},{6,4},{1,7},{3,1},{5,3},{7,5},{8,14},{10,8},{12,... | collective-permute-start | bytes 2064392 | tf_op jit(solution)/shard_map/ppermute | solution.py:19
  39.9 22.6 %collective-permute-start.8 = (bf16[192,1792]{1,0:T(8,128)(2,1)}, bf16[192,1792]{1,0:T(8,128)(2,1)}, u32[]{:S(2)}, u32[]{:S(2)}) collective-permute-start(bf16[192,1792]{1,0:T(8,128)(2,1)} %collective-permute-done.2), channel_id=1, source_target_pairs={{0,2},{2,4},{4,6},{6,0},{1,3},{3,5},{5,7},{7,1},{8,10},{10,12},{12... | collective-permute-start | bytes 2064392 | tf_op jit(solution)/shard_map/ppermute | solution.py:19
  39.9 21.4 %collective-permute-start.7 = (bf16[384,512]{1,0:T(8,128)(2,1)S(1)}, bf16[384,512]{1,0:T(8,128)(2,1)S(1)}, u32[]{:S(2)}, u32[]{:S(2)}) collective-permute-start(bf16[384,512]{1,0:T(8,128)(2,1)S(1)} %pad_maximum_fusion.3), channel_id=1, source_target_pairs={{0,32},{32,64},{64,96},{96,0},{1,33},{33,65},{65,97},{97,1},{2,34}... | collective-permute-start | bytes 1179656 | tf_op jit(solution)/shard_map/ppermute | solution.py:19
  40.8 20.5 %collective-permute-start.6 = (bf16[384,512]{1,0:T(8,128)(2,1)S(1)}, bf16[384,512]{1,0:T(8,128)(2,1)S(1)}, u32[]{:S(2)}, u32[]{:S(2)}) collective-permute-start(bf16[384,512]{1,0:T(8,128)(2,1)S(1)} %pad_maximum_fusion.3), channel_id=1, source_target_pairs={{0,64},{32,96},{64,0},{96,32},{1,65},{33,97},{65,1},{97,33},{2,66}... | collective-permute-start | bytes 1179656 | tf_op jit(solution)/shard_map/ppermute | solution.py:19
  41.8 19.5 %collective-permute-start.5 = (bf16[384,512]{1,0:T(8,128)(2,1)S(1)}, bf16[384,512]{1,0:T(8,128)(2,1)}, u32[]{:S(2)}, u32[]{:S(2)}) collective-permute-start(bf16[384,512]{1,0:T(8,128)(2,1)S(1)} %pad_maximum_fusion.3), channel_id=1, source_target_pairs={{0,96},{32,0},{64,32},{96,64},{1,97},{33,1},{65,33},{97,65},{2,98}... | collective-permute-start | bytes 1179656 | tf_op jit(solution)/shard_map/ppermute | solution.py:19
  61.3 1.3 copy-start.7
  62.5 9.2 %collective-permute-start.10 = (bf16[1536,512]{1,0:T(8,128)(2,1)S(1)}, bf16[1536,512]{1,0:T(8,128)(2,1)S(1)}, u32[]{:S(2)}, u32[]{:S(2)}) collective-permute-start(bf16[1536,512]{1,0:T(8,128)(2,1)S(1)} %pad_maximum_fusion), channel_id=1, source_target_pairs={{0,8},{8,0},{1,9},{9,1},{2,10},{10,2},{3,11},{11,3},{4,12},{12,4},... | collective-permute-start | bytes 4718600 | tf_op jit(solution)/shard_map/ppermute | solution.py:23
  62.6 3.5 %collective-permute-start.11 = (bf16[192,128]{1,0:T(8,128)(2,1)S(1)}, bf16[192,128]{1,0:T(8,128)(2,1)S(1)}, u32[]{:S(2)}, u32[]{:S(2)}) collective-permute-start(bf16[192,128]{1,0:T(8,128)(2,1)S(1)} %copy-done.7), channel_id=1, source_target_pairs={{0,8},{8,0},{1,9},{9,1},{2,10},{10,2},{3,11},{11,3},{4,12},{12,4},... | collective-permute-start | bytes 147464 | tf_op jit(solution)/shard_map/ppermute | solution.py:23
  66.0 5.6 %collective-permute-start.12 = (bf16[192,128]{1,0:T(8,128)(2,1)S(1)}, bf16[192,128]{1,0:T(8,128)(2,1)S(1)}, u32[]{:S(2)}, u32[]{:S(2)}) collective-permute-start(bf16[192,128]{1,0:T(8,128)(2,1)S(1)} %add_convert_fusion), channel_id=1, source_target_pairs={{0,16},{16,0},{1,17},{17,1},{2,18},{18,2},{3,19},{19,3},{4,20},{20... | collective-permute-start | bytes 147464 | tf_op jit(solution)/shard_map/ppermute | solution.py:23
  69.6 9.9 %collective-permute-start.14 = (bf16[96,1792]{1,0:T(8,128)(2,1)S(1)}, bf16[96,1792]{1,0:T(8,128)(2,1)S(1)}, u32[]{:S(2)}, u32[]{:S(2)}) collective-permute-start(bf16[96,1792]{1,0:T(8,128)(2,1)S(1)} %slice.28), channel_id=1, source_target_pairs={{0,6},{2,0},{4,2},{6,4},{1,7},{3,1},{5,3},{7,5},{8,14},{10,8},{12,... | collective-permute-start | bytes 1032200 | tf_op jit(solution)/shard_map/ppermute | solution.py:19
  70.3 10.8 %collective-permute-start.13 = (bf16[96,1792]{1,0:T(8,128)(2,1)S(1)}, bf16[96,1792]{1,0:T(8,128)(2,1)S(1)}, u32[]{:S(2)}, u32[]{:S(2)}) collective-permute-start(bf16[96,1792]{1,0:T(8,128)(2,1)S(1)} %slice.27), channel_id=1, source_target_pairs={{0,2},{2,4},{4,6},{6,0},{1,3},{3,5},{5,7},{7,1},{8,10},{10,12},{12... | collective-permute-start | bytes 1032200 | tf_op jit(solution)/shard_map/ppermute | solution.py:19
  71.7 2.6 %copy-start = (bf16[1792,1024]{1,0:T(8,128)(2,1)S(1)}, bf16[1792,1024]{1,0:T(8,128)(2,1)}, u32[]{:S(2)}) copy-start(bf16[1792,1024]{1,0:T(8,128)(2,1)} %param.8) | copy-start | bytes 11010052
  81.0 15.0 %collective-permute-start.17 = (bf16[384,128]{1,0:T(8,128)(2,1)S(1)}, bf16[384,128]{1,0:T(8,128)(2,1)S(1)}, u32[]{:S(2)}, u32[]{:S(2)}) collective-permute-start(bf16[384,128]{1,0:T(8,128)(2,1)S(1)} %pad_maximum_fusion.5), channel_id=1, source_target_pairs={{0,32},{32,64},{64,96},{96,0},{1,33},{33,65},{65,97},{97,1},{2,34}... | collective-permute-start | bytes 294920 | tf_op jit(solution)/shard_map/ppermute | solution.py:19
  82.0 14.9 %collective-permute-start.16 = (bf16[384,128]{1,0:T(8,128)(2,1)S(1)}, bf16[384,128]{1,0:T(8,128)(2,1)S(1)}, u32[]{:S(2)}, u32[]{:S(2)}) collective-permute-start(bf16[384,128]{1,0:T(8,128)(2,1)S(1)} %pad_maximum_fusion.5), channel_id=1, source_target_pairs={{0,64},{32,96},{64,0},{96,32},{1,65},{33,97},{65,1},{97,33},{2,66}... | collective-permute-start | bytes 294920 | tf_op jit(solution)/shard_map/ppermute | solution.py:19
  88.3 20.0 %collective-permute-start.18 = (bf16[192,1792]{1,0:T(8,128)(2,1)S(1)}, bf16[192,1792]{1,0:T(8,128)(2,1)S(1)}, u32[]{:S(2)}, u32[]{:S(2)}) collective-permute-start(bf16[192,1792]{1,0:T(8,128)(2,1)S(1)} %fusion.9), channel_id=1, source_target_pairs={{0,1},{1,0},{2,3},{3,2},{4,5},{5,4},{6,7},{7,6},{8,9},{9,8},{10,11... | collective-permute-start | bytes 2064392 | tf_op jit(solution)/shard_map/ppermute | solution.py:23
  90.3 18.0 %collective-permute-start.19 = (bf16[192,1792]{1,0:T(8,128)(2,1)S(1)}, bf16[192,1792]{1,0:T(8,128)(2,1)S(1)}, u32[]{:S(2)}, u32[]{:S(2)}) collective-permute-start(bf16[192,1792]{1,0:T(8,128)(2,1)S(1)} %fusion.7), channel_id=1, source_target_pairs={{0,2},{2,4},{4,6},{6,0},{1,3},{3,5},{5,7},{7,1},{8,10},{10,12},{12... | collective-permute-start | bytes 2064392 | tf_op jit(solution)/shard_map/ppermute | solution.py:19
  90.4 17.9 %collective-permute-start.20 = (bf16[192,1792]{1,0:T(8,128)(2,1)S(1)}, bf16[192,1792]{1,0:T(8,128)(2,1)S(1)}, u32[]{:S(2)}, u32[]{:S(2)}) collective-permute-start(bf16[192,1792]{1,0:T(8,128)(2,1)S(1)} %fusion.8), channel_id=1, source_target_pairs={{0,6},{2,0},{4,2},{6,4},{1,7},{3,1},{5,3},{7,5},{8,14},{10,8},{12,... | collective-permute-start | bytes 2064392 | tf_op jit(solution)/shard_map/ppermute | solution.py:19
  96.0 4.7 %collective-permute-start.15 = (bf16[384,128]{1,0:T(8,128)(2,1)S(1)}, bf16[384,128]{1,0:T(8,128)(2,1)S(1)}, u32[]{:S(2)}, u32[]{:S(2)}) collective-permute-start(bf16[384,128]{1,0:T(8,128)(2,1)S(1)} %pad_maximum_fusion.5), channel_id=1, source_target_pairs={{0,96},{32,0},{64,32},{96,64},{1,97},{33,1},{65,33},{97,65},{2,98}... | collective-permute-start | bytes 294920 | tf_op jit(solution)/shard_map/ppermute | solution.py:19
  96.9 26.1 %collective-permute-start.21 = (bf16[192,1792]{1,0:T(8,128)(2,1)S(1)}, bf16[192,1792]{1,0:T(8,128)(2,1)S(1)}, u32[]{:S(2)}, u32[]{:S(2)}) collective-permute-start(bf16[192,1792]{1,0:T(8,128)(2,1)S(1)} %constant_dynamic-update-slice_fusion), channel_id=1, source_target_pairs={{0,1},{1,0},{2,3},{3,2},{4,5},{5,4},{6,7},{7,6},{8,9},{9,8},{10,11... | collective-permute-start | bytes 2064392 | tf_op jit(solution)/shard_map/ppermute | solution.py:23
  109.0 1.1 copy-start.5
  110.5 16.1 %collective-permute-start.23 = (bf16[96,1792]{1,0:T(8,128)(2,1)S(1)}, bf16[96,1792]{1,0:T(8,128)(2,1)S(1)}, u32[]{:S(2)}, u32[]{:S(2)}) collective-permute-start(bf16[96,1792]{1,0:T(8,128)(2,1)S(1)} %get-tuple-element.57), channel_id=1, source_target_pairs={{0,6},{2,0},{4,2},{6,4},{1,7},{3,1},{5,3},{7,5},{8,14},{10,8},{12,... | collective-permute-start | bytes 1032200 | tf_op jit(solution)/shard_map/ppermute | solution.py:19
  112.2 3.2 %copy-start.6 = (bf16[192,1792]{1,0:T(8,128)(2,1)S(1)}, bf16[192,1792]{1,0:T(8,128)(2,1)}, u32[]{:S(2)}) copy-start(bf16[192,1792]{1,0:T(8,128)(2,1)} %param.6) | copy-start | bytes 2064388
  112.2 14.3 %collective-permute-start.22 = (bf16[96,1792]{1,0:T(8,128)(2,1)S(1)}, bf16[96,1792]{1,0:T(8,128)(2,1)S(1)}, u32[]{:S(2)}, u32[]{:S(2)}) collective-permute-start(bf16[96,1792]{1,0:T(8,128)(2,1)S(1)} %get-tuple-element.58), channel_id=1, source_target_pairs={{0,2},{2,4},{4,6},{6,0},{1,3},{3,5},{5,7},{7,1},{8,10},{10,12},{12... | collective-permute-start | bytes 1032200 | tf_op jit(solution)/shard_map/ppermute | solution.py:19
  113.4 3.7 %copy-start.3 = (bf16[192,1792]{1,0:T(8,128)(2,1)S(1)}, bf16[192,1792]{1,0:T(8,128)(2,1)}, u32[]{:S(2)}) copy-start(bf16[192,1792]{1,0:T(8,128)(2,1)} %copy-done.2) | copy-start | bytes 2064388
  113.4 24.3 %collective-permute-start.26 = (bf16[192,1792]{1,0:T(8,128)(2,1)S(1)}, bf16[192,1792]{1,0:T(8,128)(2,1)S(1)}, u32[]{:S(2)}, u32[]{:S(2)}) collective-permute-start(bf16[192,1792]{1,0:T(8,128)(2,1)S(1)} %fusion.11), channel_id=1, source_target_pairs={{0,1},{1,0},{2,3},{3,2},{4,5},{5,4},{6,7},{7,6},{8,9},{9,8},{10,11... | collective-permute-start | bytes 2064392 | tf_op jit(solution)/shard_map/ppermute | solution.py:23
  119.2 4.1 %copy-start.8 = (f32[128,1792]{1,0:T(8,128)S(1)}, f32[128,1792]{1,0:T(8,128)}, u32[]{:S(2)}) copy-start(f32[128,1792]{1,0:T(8,128)} %param.10) | copy-start | bytes 2752516
  119.2 4.1 %copy-start.9 = (f32[128,1792]{1,0:T(8,128)S(1)}, f32[128,1792]{1,0:T(8,128)}, u32[]{:S(2)}) copy-start(f32[128,1792]{1,0:T(8,128)} %param.11) | copy-start | bytes 2752516
  126.5 18.1 %collective-permute-start.30 = (bf16[128,1792]{1,0:T(8,128)(2,1)S(1)}, bf16[128,1792]{1,0:T(8,128)(2,1)S(1)}, u32[]{:S(2)}, u32[]{:S(2)}) collective-permute-start(bf16[128,1792]{1,0:T(8,128)(2,1)S(1)} %get-tuple-element.45), channel_id=1, source_target_pairs={{0,1},{1,0},{2,3},{3,2},{4,5},{5,4},{6,7},{7,6},{8,9},{9,8},{10,11... | collective-permute-start | bytes 1376264 | tf_op jit(solution)/shard_map/ppermute | solution.py:23
  128.4 18.4 %collective-permute-start.29 = (bf16[128,1792]{1,0:T(8,128)(2,1)S(1)}, bf16[128,1792]{1,0:T(8,128)(2,1)S(1)}, u32[]{:S(2)}, u32[]{:S(2)}) collective-permute-start(bf16[128,1792]{1,0:T(8,128)(2,1)S(1)} %get-tuple-element.45), channel_id=1, source_target_pairs={{0,2},{2,4},{4,6},{6,0},{1,3},{3,5},{5,7},{7,1},{8,10},{10,12},{12... | collective-permute-start | bytes 1376264 | tf_op jit(solution)/shard_map/ppermute | solution.py:19
  128.4 18.4 %collective-permute-start.28 = (bf16[128,1792]{1,0:T(8,128)(2,1)S(1)}, bf16[128,1792]{1,0:T(8,128)(2,1)S(1)}, u32[]{:S(2)}, u32[]{:S(2)}) collective-permute-start(bf16[128,1792]{1,0:T(8,128)(2,1)S(1)} %get-tuple-element.45), channel_id=1, source_target_pairs={{0,4},{2,6},{4,0},{6,2},{1,5},{3,7},{5,1},{7,3},{8,12},{10,14},{12... | collective-permute-start | bytes 1376264 | tf_op jit(solution)/shard_map/ppermute | solution.py:19
  130.1 23.6 %collective-permute-start.27 = (bf16[128,1792]{1,0:T(8,128)(2,1)S(1)}, bf16[128,1792]{1,0:T(8,128)(2,1)S(1)}, u32[]{:S(2)}, u32[]{:S(2)}) collective-permute-start(bf16[128,1792]{1,0:T(8,128)(2,1)S(1)} %get-tuple-element.45), channel_id=1, source_target_pairs={{0,6},{2,0},{4,2},{6,4},{1,7},{3,1},{5,3},{7,5},{8,14},{10,8},{12,... | collective-permute-start | bytes 1376264 | tf_op jit(solution)/shard_map/ppermute | solution.py:19
  131.7 12.9 %copy-start.1 = (bf16[1024,1024]{1,0:T(8,128)(2,1)S(1)}, bf16[1024,1024]{1,0:T(8,128)(2,1)}, u32[]{:S(2)}) copy-start(bf16[1024,1024]{1,0:T(8,128)(2,1)} %param.9) | copy-start | bytes 6291460
  137.7 28.9 %collective-permute-start.25 = (bf16[192,1792]{1,0:T(8,128)(2,1)S(1)}, bf16[192,1792]{1,0:T(8,128)(2,1)S(1)}, u32[]{:S(2)}, u32[]{:S(2)}) collective-permute-start(bf16[192,1792]{1,0:T(8,128)(2,1)S(1)} %pad_maximum_fusion.2), channel_id=1, source_target_pairs={{0,6},{2,0},{4,2},{6,4},{1,7},{3,1},{5,3},{7,5},{8,14},{10,8},{12,... | collective-permute-start | bytes 2064392 | tf_op jit(solution)/shard_map/ppermute | solution.py:19
  144.7 22.0 %collective-permute-start.24 = (bf16[192,1792]{1,0:T(8,128)(2,1)S(1)}, bf16[192,1792]{1,0:T(8,128)(2,1)S(1)}, u32[]{:S(2)}, u32[]{:S(2)}) collective-permute-start(bf16[192,1792]{1,0:T(8,128)(2,1)S(1)} %pad_maximum_fusion.1), channel_id=1, source_target_pairs={{0,2},{2,4},{4,6},{6,0},{1,3},{3,5},{5,7},{7,1},{8,10},{10,12},{12... | collective-permute-start | bytes 2064392 | tf_op jit(solution)/shard_map/ppermute | solution.py:19
  146.8 24.3 %collective-permute-start.33 = (bf16[128,1792]{1,0:T(8,128)(2,1)S(1)}, bf16[128,1792]{1,0:T(8,128)(2,1)S(1)}, u32[]{:S(2)}, u32[]{:S(2)}) collective-permute-start(bf16[128,1792]{1,0:T(8,128)(2,1)S(1)} %collective-permute-done.30), channel_id=1, source_target_pairs={{0,2},{2,4},{4,6},{6,0},{1,3},{3,5},{5,7},{7,1},{8,10},{10,12},{12... | collective-permute-start | bytes 1376264 | tf_op jit(solution)/shard_map/ppermute | solution.py:19
  146.8 24.8 %collective-permute-start.31 = (bf16[128,1792]{1,0:T(8,128)(2,1)S(1)}, bf16[128,1792]{1,0:T(8,128)(2,1)S(1)}, u32[]{:S(2)}, u32[]{:S(2)}) collective-permute-start(bf16[128,1792]{1,0:T(8,128)(2,1)S(1)} %collective-permute-done.30), channel_id=1, source_target_pairs={{0,6},{2,0},{4,2},{6,4},{1,7},{3,1},{5,3},{7,5},{8,14},{10,8},{12,... | collective-permute-start | bytes 1376264 | tf_op jit(solution)/shard_map/ppermute | solution.py:19
  153.8 17.8 %collective-permute-start.32 = (bf16[128,1792]{1,0:T(8,128)(2,1)S(1)}, bf16[128,1792]{1,0:T(8,128)(2,1)S(1)}, u32[]{:S(2)}, u32[]{:S(2)}) collective-permute-start(bf16[128,1792]{1,0:T(8,128)(2,1)S(1)} %collective-permute-done.28), channel_id=1, source_target_pairs={{0,1},{1,0},{2,3},{3,2},{4,5},{5,4},{6,7},{7,6},{8,9},{9,8},{10,11... | collective-permute-start | bytes 1376264 | tf_op jit(solution)/shard_map/ppermute | solution.py:23

commit v3 on v2

--- a/solution.py
+++ b/solution.py
@@ -61,8 +61,8 @@
 
 def shards(hidden, grad_out, weight, basis, first_moment, second_moment):
     c, z, xh = (lax.axis_index(n) for n in ("c", "z", "xh"))
-    w_mine = lax.dynamic_slice_in_dim(weight, c * 512, 512, axis=1)
-    w_other = lax.dynamic_slice_in_dim(weight, (1 - c) * 512, 512, axis=1)
+    halves = [lax.dynamic_slice_in_dim(weight, k * 512, 512, axis=1) for k in (c, 1 - c)]
+    turned = jnp.concatenate(halves, axis=1)
 
     t = transpose_blocks(grad_out)
     hx, hbelow, habove = x_far(hidden), z_up(hidden), z_down(hidden)
@@ -76,23 +76,26 @@
     half = ring_tokens(pair)
     mine = jnp.sum(part.astype(F32), axis=0).astype(BF16)
     mine, half, hxbelow, hxabove = lax.optimization_barrier((mine, half, hxbelow, hxabove))
-    hfirst, hsecond = z_up(hbelow[:96]), z_down(habove[96:])
+    hfirst = z_up(jnp.concatenate([hbelow[:96], hxbelow[:96]], axis=0))
+    hsecond = z_down(jnp.concatenate([habove[96:], hxabove[96:]], axis=0))
     other = core(half)
     mine = (mine.astype(F32) + core(mine).astype(F32)).astype(BF16)
     mine = pair_tokens(mine)
 
+    sums = dot(jnp.concatenate([half, other], axis=1), turned, 1, 1).astype(BF16)
+
     def partial(i):
-        return dot(token_block(half, i), w_mine, 1, 1) + dot(token_block(other, i), w_other, 1, 1)
+        return token_block(sums, i)
 
-    xup, xdown = partial(3).astype(BF16), partial(7).astype(BF16)
+    xup, xdown = partial(3), partial(7)
     mine, xup, xdown, hfirst, hsecond = lax.optimization_barrier((mine, xup, xdown, hfirst, hsecond))
     xup, xdown = z_up(xup), z_down(xdown)
-    far = x_far(partial(5).astype(BF16))
-    htwo = jnp.concatenate([hfirst, hsecond], axis=0)
-    hxtwo = x_far(htwo)
+    far = x_far(partial(5))
+    htwo = jnp.concatenate([hfirst[:96], hsecond[:96]], axis=0)
+    hxtwo = jnp.concatenate([hfirst[96:], hsecond[96:]], axis=0)
     low = ring_tokens(mine)
-    low, far, xup, xdown = lax.optimization_barrier((low, far, xup, xdown))
-    two = (partial(4) + far.astype(F32)).astype(BF16)
+    far, xup, xdown = lax.optimization_barrier((far, xup, xdown))
+    two = (partial(4).astype(F32) + far.astype(F32)).astype(BF16)
     first, second = z_up(two[:96]), z_down(two[96:])
 
     projected = jnp.zeros((128, 1792), F32)
@@ -115,12 +118,12 @@
     expanded += dot(jnp.concatenate([dx, dxabove, dxtwo, dxbelow], axis=0), columns(1 - xh), 0, 1)
     update = (galore_scale * expanded).astype(BF16)
 
-    up, down = partial(2), partial(6)
+    up, down = partial(2).astype(F32), partial(6).astype(F32)
     up = jnp.concatenate([up[:96] + first.astype(F32), up[96:]], axis=0).astype(BF16)
     down = jnp.concatenate([down[:96], down[96:] + second.astype(F32)], axis=0).astype(BF16)
     up, down = z_up(up), z_down(down)
-    xsum = x_far((partial(1) + xup.astype(F32) + xdown.astype(F32)).astype(BF16))
-    grad_hidden = (partial(0) + up.astype(F32) + down.astype(F32) + xsum.astype(F32)).astype(BF16)
+    xsum = x_far((partial(1).astype(F32) + xup.astype(F32) + xdown.astype(F32)).astype(BF16))
+    grad_hidden = (partial(0).astype(F32) + up.astype(F32) + down.astype(F32) + xsum.astype(F32)).astype(BF16)
     return (grad_hidden, update, new_first, new_second)
 
 

time: 176 us -> 171 us (0.972)
  waiting for transfers between devices: 66 us -> 41.9 us
  starting transfers between devices: 55.8 us -> 74.6 us
  matrix products: 30 us -> 25.2 us
  other arithmetic: 2.12 us -> 6.63 us
  local copies, waits for them, and re-layouts: 4 us -> 6.86 us
  blocking collectives: 16.2 us -> 14.4 us
    ppermute x10 -> x9, waiting for transfers between devices: 41.3 us -> 9.85 us  [swap(): return lambda a: lax.ppermute(a, axis, [(0, 1), (1, 0)])]
    ppermute x10 -> x9, starting transfers between devices: 15 us -> 27.8 us  [swap(): return lambda a: lax.ppermute(a, axis, [(0, 1), (1, 0)])]
    ppermute x23, waiting for transfers between devices: 24.7 us -> 32.1 us  [ring(): return lambda a: lax.ppermute(a, axis, pairs)]
    ppermute x23, starting transfers between devices: 39.2 us -> 45.2 us  [ring(): return lambda a: lax.ppermute(a, axis, pairs)]
    dot_general x27 -> x12, matrix products: 30 us -> 25.2 us  [dot(): lax.dot_general(a, b, (((ca,), (cb,)), ((), ())), preferred_element_type=...]
    convert_element_type x0 -> x2, other arithmetic: none -> 3.94 us  [the longest x1 2.7 us: shards(): (partial(0).astype(F32) + up.astype(F32) + down.astype(F32) + xsum.astype...]
    dynamic_slice x0 -> x2, local copies, waits for them, and re-layouts: none -> 2.44 us  [the longest x1 2.29 us: shards(): lax.dynamic_slice_in_dim(weight, k * 512, 512, axis=1)]
    all_to_all x1, blocking collectives: 16.2 us -> 14.4 us  [shards(): part = lax.all_to_all(part, ('z', 'xh'), 0, 0, tiled=True)]
  transfers between devices with their start and end apart: 34 -> 33, of which waited for: 16 -> 13; matrix products, arithmetic and copies ran while one was open for 18% -> 18% of each run, Pallas kernels for 0% -> 0%
where the time goes in v3:
time: 171 us
  starting transfers between devices  74.6 us (44%)
  waiting for transfers between devices  41.9 us (25%)
  matrix products  25.2 us (15%)
  blocking collectives  14.4 us (8%)
  local copies, waits for them, and re-layouts  6.86 us (4%)
  other arithmetic  6.63 us (4%)
    ppermute x23, starting transfers between devices, ring(): return lambda a: lax.ppermute(a, axis, pairs)  45.2 us
    ppermute x23, waiting for transfers between devices, ring(): return lambda a: lax.ppermute(a, axis, pairs)  32.1 us
    ppermute x9, starting transfers between devices, swap(): return lambda a: lax.ppermute(a, axis, [(0, 1), (1, 0)])  27.8 us
    dot_general x12, matrix products, dot(): lax.dot_general(a, b, (((ca,), (cb,)), ((), ())), preferred_element_type=...  25.2 us
    all_to_all x1, blocking collectives, shards(): part = lax.all_to_all(part, ('z', 'xh'), 0, 0, tiled=True)  14.4 us
    ppermute x9, waiting for transfers between devices, swap(): return lambda a: lax.ppermute(a, axis, [(0, 1), (1, 0)])  9.85 us
  transfers between devices with their start and end apart: 33, of which 13 were waited for; matrix products, arithmetic and copies ran while one was open for 18% of the time, Pallas kernels for 0%

profile of v3, /device:TPU:0, one launch (start us, length us, event | category | flops | bytes accessed | tf_op | source)
XLA Modules:
  0.0 170.8 jit_solution(1301196961465017311)
XLA Ops:
  0.6 1.6 collective-permute-start
  2.2 4.1 %collective-permute-start.2 = (bf16[192,1792]{1,0:T(8,128)(2,1)}, bf16[192,1792]{1,0:T(8,128)(2,1)}, u32[]{:S(2)}, u32[]{:S(2)}) collective-permute-start(bf16[192,1792]{1,0:T(8,128)(2,1)} %param.6), channel_id=1, source_target_pairs={{0,1},{1,0},{2,3},{3,2},{4,5},{5,4},{6,7},{7,6},{8,9},{9,8},{10,11... | collective-permute-start | bytes 2064392 | tf_op jit(solution)/shard_map/ppermute | solution.py:23
  6.3 2.5 %collective-permute-start.3 = (bf16[192,1792]{1,0:T(8,128)(2,1)}, bf16[192,1792]{1,0:T(8,128)(2,1)S(1)}, u32[]{:S(2)}, u32[]{:S(2)}) collective-permute-start(bf16[192,1792]{1,0:T(8,128)(2,1)} %param.6), channel_id=1, source_target_pairs={{0,2},{2,4},{4,6},{6,0},{1,3},{3,5},{5,7},{7,1},{8,10},{10,12},{12... | collective-permute-start | bytes 2064392 | tf_op jit(solution)/shard_map/ppermute | solution.py:19
  8.7 2.7 %collective-permute-start.4 = (bf16[192,1792]{1,0:T(8,128)(2,1)}, bf16[192,1792]{1,0:T(8,128)(2,1)S(1)}, u32[]{:S(2)}, u32[]{:S(2)}) collective-permute-start(bf16[192,1792]{1,0:T(8,128)(2,1)} %param.6), channel_id=1, source_target_pairs={{0,6},{2,0},{4,2},{6,4},{1,7},{3,1},{5,3},{7,5},{8,14},{10,8},{12,... | collective-permute-start | bytes 2064392 | tf_op jit(solution)/shard_map/ppermute | solution.py:19
  11.4 14.3 %collective-permute-start.1 = (bf16[192,512]{1,0:T(8,128)(2,1)S(1)}, bf16[192,512]{1,0:T(8,128)(2,1)S(1)}, u32[]{:S(2)}, u32[]{:S(2)}) collective-permute-start(bf16[192,512]{1,0:T(8,128)(2,1)S(1)} %collective-permute-done), channel_id=1, source_target_pairs={{0,16},{16,0},{1,17},{17,1},{2,18},{18,2},{3,19},{19,3},{4,20},{20... | collective-permute-start | bytes 589832 | tf_op jit(solution)/shard_map/ppermute | solution.py:23
  25.7 1.6 fusion.36
  27.4 2.3 %collective-permute-done.1 = bf16[192,512]{1,0:T(8,128)(2,1)S(1)} collective-permute-done((bf16[192,512]{1,0:T(8,128)(2,1)S(1)}, bf16[192,512]{1,0:T(8,128)(2,1)S(1)}, u32[]{:S(2)}, u32[]{:S(2)}) %collective-permute-start.1) | collective-permute-done | bytes 196640 | tf_op jit(solution)/shard_map/ppermute | solution.py:23
  29.8 3.8 %collective-permute-start.8 = (bf16[192,1792]{1,0:T(8,128)(2,1)}, bf16[192,1792]{1,0:T(8,128)(2,1)}, u32[]{:S(2)}, u32[]{:S(2)}) collective-permute-start(bf16[192,1792]{1,0:T(8,128)(2,1)} %collective-permute-done.2), channel_id=1, source_target_pairs={{0,2},{2,4},{4,6},{6,0},{1,3},{3,5},{5,7},{7,1},{8,10},{10,12},{12... | collective-permute-start | bytes 2064392 | tf_op jit(solution)/shard_map/ppermute | solution.py:19
  33.6 6.8 %collective-permute-start.9 = (bf16[192,1792]{1,0:T(8,128)(2,1)}, bf16[192,1792]{1,0:T(8,128)(2,1)}, u32[]{:S(2)}, u32[]{:S(2)}) collective-permute-start(bf16[192,1792]{1,0:T(8,128)(2,1)} %collective-permute-done.2), channel_id=1, source_target_pairs={{0,6},{2,0},{4,2},{6,4},{1,7},{3,1},{5,3},{7,5},{8,14},{10,8},{12,... | collective-permute-start | bytes 2064392 | tf_op jit(solution)/shard_map/ppermute | solution.py:19
  40.7 2.3 %collective-permute-start.6 = (bf16[384,512]{1,0:T(8,128)(2,1)S(1)}, bf16[384,512]{1,0:T(8,128)(2,1)S(1)}, u32[]{:S(2)}, u32[]{:S(2)}) collective-permute-start(bf16[384,512]{1,0:T(8,128)(2,1)S(1)} %pad_maximum_fusion.5), channel_id=1, source_target_pairs={{0,64},{32,96},{64,0},{96,32},{1,65},{33,97},{65,1},{97,33},{2,66}... | collective-permute-start | bytes 1179656 | tf_op jit(solution)/shard_map/ppermute | solution.py:19
  43.0 2.6 %collective-permute-start.5 = (bf16[384,512]{1,0:T(8,128)(2,1)S(1)}, bf16[384,512]{1,0:T(8,128)(2,1)}, u32[]{:S(2)}, u32[]{:S(2)}) collective-permute-start(bf16[384,512]{1,0:T(8,128)(2,1)S(1)} %pad_maximum_fusion.5), channel_id=1, source_target_pairs={{0,96},{32,0},{64,32},{96,64},{1,97},{33,1},{65,33},{97,65},{2,98}... | collective-permute-start | bytes 1179656 | tf_op jit(solution)/shard_map/ppermute | solution.py:19
  45.6 14.4 %all_to_all.5 = bf16[8,192,128]{2,1,0:T(8,128)(2,1)S(1)} all-to-all(bf16[8,192,128]{2,1,0:T(8,128)(2,1)S(1)} %bitcast.16), channel_id=1, replica_groups=mesh['y'=4,'xl'=2,'c'=2,'z'=4,'xh'=2] {'z','xh'}, dimensions={0} | all-to-all | bytes 786432 | tf_op jit(solution)/shard_map/all_to_all | solution.py:75
  61.6 1.3 pad_maximum_fusion
  63.2 2.3 %constant_dynamic-slice_fusion.14 = (bf16[1792,512]{1,0:T(8,128)(2,1)S(1)}, bf16[1792,512]{1,0:T(8,128)(2,1)S(1)}) fusion(bf16[1792,1024]{1,0:T(8,128)(2,1)} %param.8, s32[]{:T(128)S(6)} %select_n.154, s32[]{:T(128)S(6)} %select_n.158), kind=kLoop, calls=%fused_computation.125 | loop fusion | bytes 7340040 | tf_op jit(solution)/shard_map/dynamic_slice | solution.py:64
  66.0 1.0 slice.53
  67.5 1.0 slice.55
  68.5 1.0 collective-permute-start.12
  69.6 2.2 %collective-permute-start.14 = (bf16[192,1792]{1,0:T(8,128)(2,1)S(1)}, bf16[192,1792]{1,0:T(8,128)(2,1)S(1)}, u32[]{:S(2)}, u32[]{:S(2)}) collective-permute-start(bf16[192,1792]{1,0:T(8,128)(2,1)S(1)} %pad_maximum_fusion.2), channel_id=1, source_target_pairs={{0,6},{2,0},{4,2},{6,4},{1,7},{3,1},{5,3},{7,5},{8,14},{10,8},{12,... | collective-permute-start | bytes 2064392 | tf_op jit(solution)/shard_map/ppermute | solution.py:19
  71.8 1.0 collective-permute-done.12
  72.8 7.3 %convolution_convert_fusion = bf16[1536,1792]{1,0:T(8,128)(2,1)S(1)} fusion(bf16[1792,512]{1,0:T(8,128)(2,1)S(1)} %get-tuple-element.57, bf16[1792,512]{1,0:T(8,128)(2,1)S(1)} %get-tuple-element.56, bf16[1536,512]{1,0:T(8,128)(2,1)} %collective-permute-done.10, bf16[1536,512]{1,0:T(8,128)(2,1)S(1)} %pad_maximum_fusion), kind=kOutput, calls=%fused_computation | convolution fusion | flops 5653528576 | bytes 12320768 | tf_op jit(solution)/shard_map/dot_general | solution.py:59
  80.2 5.6 %collective-permute-done.13 = bf16[192,1792]{1,0:T(8,128)(2,1)S(1)} collective-permute-done((bf16[192,1792]{1,0:T(8,128)(2,1)S(1)}, bf16[192,1792]{1,0:T(8,128)(2,1)S(1)}, u32[]{:S(2)}, u32[]{:S(2)}) %collective-permute-start.13) | collective-permute-done | bytes 688160 | tf_op jit(solution)/shard_map/ppermute | solution.py:19
  87.2 2.8 %collective-permute-start.16 = (bf16[384,128]{1,0:T(8,128)(2,1)S(1)}, bf16[384,128]{1,0:T(8,128)(2,1)S(1)}, u32[]{:S(2)}, u32[]{:S(2)}) collective-permute-start(bf16[384,128]{1,0:T(8,128)(2,1)S(1)} %pad_maximum_fusion.6), channel_id=1, source_target_pairs={{0,64},{32,96},{64,0},{96,32},{1,65},{33,97},{65,1},{97,33},{2,66}... | collective-permute-start | bytes 294920 | tf_op jit(solution)/shard_map/ppermute | solution.py:19
  90.0 1.8 %collective-permute-start.18 = (bf16[192,1792]{1,0:T(8,128)(2,1)S(1)}, bf16[192,1792]{1,0:T(8,128)(2,1)S(1)}, u32[]{:S(2)}, u32[]{:S(2)}) collective-permute-start(bf16[192,1792]{1,0:T(8,128)(2,1)S(1)} %get-tuple-element.54), channel_id=1, source_target_pairs={{0,1},{1,0},{2,3},{3,2},{4,5},{5,4},{6,7},{7,6},{8,9},{9,8},{10,11... | collective-permute-start | bytes 2064392 | tf_op jit(solution)/shard_map/ppermute | solution.py:23
  92.8 2.8 %collective-permute-start.20 = (bf16[192,1792]{1,0:T(8,128)(2,1)S(1)}, bf16[192,1792]{1,0:T(8,128)(2,1)S(1)}, u32[]{:S(2)}, u32[]{:S(2)}) collective-permute-start(bf16[192,1792]{1,0:T(8,128)(2,1)S(1)} %get-tuple-element.37), channel_id=1, source_target_pairs={{0,6},{2,0},{4,2},{6,4},{1,7},{3,1},{5,3},{7,5},{8,14},{10,8},{12,... | collective-permute-start | bytes 2064392 | tf_op jit(solution)/shard_map/ppermute | solution.py:19
  95.9 1.5 fusion.18
  98.0 1.4 fusion.15
  100.4 6.5 %collective-permute-done.18 = bf16[192,1792]{1,0:T(8,128)(2,1)S(1)} collective-permute-done((bf16[192,1792]{1,0:T(8,128)(2,1)S(1)}, bf16[192,1792]{1,0:T(8,128)(2,1)S(1)}, u32[]{:S(2)}, u32[]{:S(2)}) %collective-permute-start.18) | collective-permute-done | bytes 688160 | tf_op jit(solution)/shard_map/ppermute | solution.py:23
  107.0 1.6 collective-permute-done.19
  108.6 1.2 add_convert_fusion.2
  109.9 1.6 collective-permute-start.21
  111.5 1.9 %collective-permute-start.22 = (bf16[96,1792]{1,0:T(8,128)(2,1)S(1)}, bf16[96,1792]{1,0:T(8,128)(2,1)S(1)}, u32[]{:S(2)}, u32[]{:S(2)}) collective-permute-start(bf16[96,1792]{1,0:T(8,128)(2,1)S(1)} %get-tuple-element.66), channel_id=1, source_target_pairs={{0,6},{2,0},{4,2},{6,4},{1,7},{3,1},{5,3},{7,5},{8,14},{10,8},{12,... | collective-permute-start | bytes 1032200 | tf_op jit(solution)/shard_map/ppermute | solution.py:19
  113.4 3.3 %divide_convert_fusion = (bf16[128,1792]{1,0:T(8,128)(2,1)}, f32[128,1792]{1,0:T(8,128)}, f32[128,1792]{1,0:T(8,128)}) fusion(f32[128,1792]{1,0:T(8,128)S(1)} %copy-done.7, f32[128,1792]{1,0:T(8,128)S(1)} %copy-done.8, f32[128,1792]{1,0:T(8,128)S(1)} %fusion.9, bf16[192,1792]{1,0:T(8,128)(2,1)} %collective-permute-done.8, ...), kind=kOutput, calls=%fused_computation.69 | convolution fusion | flops 91521024 | bytes 5783556 | tf_op jit(solution)/shard_map/dot_general | solution.py:59
  116.7 2.1 %collective-permute-start.25 = (bf16[192,1792]{1,0:T(8,128)(2,1)}, bf16[192,1792]{1,0:T(8,128)(2,1)S(1)}, u32[]{:S(2)}, u32[]{:S(2)}) collective-permute-start(bf16[192,1792]{1,0:T(8,128)(2,1)} %get-tuple-element.52), channel_id=1, source_target_pairs={{0,1},{1,0},{2,3},{3,2},{4,5},{5,4},{6,7},{7,6},{8,9},{9,8},{10,11... | collective-permute-start | bytes 2064392 | tf_op jit(solution)/shard_map/ppermute | solution.py:23
  118.8 1.7 collective-permute-start.28
  120.5 2.8 %collective-permute-start.27 = (bf16[128,1792]{1,0:T(8,128)(2,1)}, bf16[128,1792]{1,0:T(8,128)(2,1)}, u32[]{:S(2)}, u32[]{:S(2)}) collective-permute-start(bf16[128,1792]{1,0:T(8,128)(2,1)} %get-tuple-element.43), channel_id=1, source_target_pairs={{0,4},{2,6},{4,0},{6,2},{1,5},{3,7},{5,1},{7,3},{8,12},{10,14},{12... | collective-permute-start | bytes 1376264 | tf_op jit(solution)/shard_map/ppermute | solution.py:19
  123.3 1.3 collective-permute-start.26
  124.7 2.1 %collective-permute-start.29 = (bf16[128,1792]{1,0:T(8,128)(2,1)}, bf16[128,1792]{1,0:T(8,128)(2,1)}, u32[]{:S(2)}, u32[]{:S(2)}) collective-permute-start(bf16[128,1792]{1,0:T(8,128)(2,1)} %get-tuple-element.43), channel_id=1, source_target_pairs={{0,1},{1,0},{2,3},{3,2},{4,5},{5,4},{6,7},{7,6},{8,9},{9,8},{10,11... | collective-permute-start | bytes 1376264 | tf_op jit(solution)/shard_map/ppermute | solution.py:23
  127.9 5.7 %collective-permute-done.28 = bf16[128,1792]{1,0:T(8,128)(2,1)S(1)} collective-permute-done((bf16[128,1792]{1,0:T(8,128)(2,1)}, bf16[128,1792]{1,0:T(8,128)(2,1)S(1)}, u32[]{:S(2)}, u32[]{:S(2)}) %collective-permute-start.28) | collective-permute-done | bytes 458784 | tf_op jit(solution)/shard_map/ppermute | solution.py:19
  133.5 1.8 %collective-permute-start.24 = (bf16[192,1792]{1,0:T(8,128)(2,1)S(1)}, bf16[192,1792]{1,0:T(8,128)(2,1)}, u32[]{:S(2)}, u32[]{:S(2)}) collective-permute-start(bf16[192,1792]{1,0:T(8,128)(2,1)S(1)} %pad_maximum_fusion.4), channel_id=1, source_target_pairs={{0,6},{2,0},{4,2},{6,4},{1,7},{3,1},{5,3},{7,5},{8,14},{10,8},{12,... | collective-permute-start | bytes 2064392 | tf_op jit(solution)/shard_map/ppermute | solution.py:19
  135.3 8.4 %collective-permute-done.27 = bf16[128,1792]{1,0:T(8,128)(2,1)} collective-permute-done((bf16[128,1792]{1,0:T(8,128)(2,1)}, bf16[128,1792]{1,0:T(8,128)(2,1)}, u32[]{:S(2)}, u32[]{:S(2)}) %collective-permute-start.27) | collective-permute-done | bytes 458784 | tf_op jit(solution)/shard_map/ppermute | solution.py:19
  144.6 1.9 %collective-permute-start.31 = (bf16[128,1792]{1,0:T(8,128)(2,1)}, bf16[128,1792]{1,0:T(8,128)(2,1)S(1)}, u32[]{:S(2)}, u32[]{:S(2)}) collective-permute-start(bf16[128,1792]{1,0:T(8,128)(2,1)} %collective-permute-done.27), channel_id=1, source_target_pairs={{0,1},{1,0},{2,3},{3,2},{4,5},{5,4},{6,7},{7,6},{8,9},{9,8},{10,11... | collective-permute-start | bytes 1376264 | tf_op jit(solution)/shard_map/ppermute | solution.py:23
  146.5 3.4 %fusion.21 = f32[1792,1024]{1,0:T(8,128)S(1)} fusion(bf16[128,1792]{1,0:T(8,128)(2,1)S(1)} %copy-done.10, bf16[128,1792]{1,0:T(8,128)(2,1)} %collective-permute-done.27, bf16[128,1792]{1,0:T(8,128)(2,1)} %collective-permute-done.26, bf16[128,1792]{1,0:T(8,128)(2,1)} %get-tuple-element.43, bf16[1024,128]{1,0:T(8,128)(2,1)S(1)} %get-tuple-element.60, ...), kind=kOutput, calls=%fused_computation.31 | convolution fusion | flops 1890582528 | bytes 10223616 | tf_op jit(solution)/shard_map/dot_general | solution.py:59
  150.0 3.5 %collective-permute-start.30 = (bf16[128,1792]{1,0:T(8,128)(2,1)}, bf16[128,1792]{1,0:T(8,128)(2,1)S(1)}, u32[]{:S(2)}, u32[]{:S(2)}) collective-permute-start(bf16[128,1792]{1,0:T(8,128)(2,1)} %collective-permute-done.29), channel_id=1, source_target_pairs={{0,6},{2,0},{4,2},{6,4},{1,7},{3,1},{5,3},{7,5},{8,14},{10,8},{12,... | collective-permute-start | bytes 1376264 | tf_op jit(solution)/shard_map/ppermute | solution.py:19
  153.4 5.9 %collective-permute-done.24 = bf16[192,1792]{1,0:T(8,128)(2,1)} collective-permute-done((bf16[192,1792]{1,0:T(8,128)(2,1)S(1)}, bf16[192,1792]{1,0:T(8,128)(2,1)}, u32[]{:S(2)}, u32[]{:S(2)}) %collective-permute-start.24) | collective-permute-done | bytes 688160 | tf_op jit(solution)/shard_map/ppermute | solution.py:19
  159.3 1.6 collective-permute-done.23
  160.9 2.7 %add_convert_fusion = bf16[192,1792]{1,0:T(8,128)(2,1)} fusion(bf16[192,1792]{1,0:T(8,128)(2,1)S(1)} %collective-permute-done.25, bf16[192,1792]{1,0:T(8,128)(2,1)} %collective-permute-done.24, bf16[192,1792]{1,0:T(8,128)(2,1)} %collective-permute-done.23, bf16[1536,1792]{1,0:T(8,128)(2,1)} %copy-done, s32[]{:T(128)S(6)} %select_n.160), kind=kLoop, calls=%fused_computation.47 | loop fusion | flops 2752512 | bytes 3440644 | tf_op jit(solution)/shard_map/convert_element_type | solution.py:126
  163.6 2.1 %collective-permute-done.32 = bf16[128,1792]{1,0:T(8,128)(2,1)S(1)} collective-permute-done((bf16[128,1792]{1,0:T(8,128)(2,1)}, bf16[128,1792]{1,0:T(8,128)(2,1)S(1)}, u32[]{:S(2)}, u32[]{:S(2)}) %collective-permute-start.32) | collective-permute-done | bytes 458784 | tf_op jit(solution)/shard_map/ppermute | solution.py:19
  165.7 5.1 %multiply_convert_fusion = bf16[1792,1024]{1,0:T(8,128)(2,1)} fusion(f32[1792,1024]{1,0:T(8,128)S(1)} %fusion.21, bf16[128,1792]{1,0:T(8,128)(2,1)S(1)} %collective-permute-done.32, bf16[128,1792]{1,0:T(8,128)(2,1)S(1)} %collective-permute-done.31, bf16[128,1792]{1,0:T(8,128)(2,1)S(1)} %collective-permute-done.30, ...), kind=kOutput, calls=%fused_computation.1 | convolution fusion | flops 1896087552 | bytes 13893632 | tf_op jit(solution)/shard_map/dot_general | solution.py:59
  (83 shorter events, 9.4 us)
Async XLA Ops:
  0.6 10.8 %collective-permute-start = (bf16[192,512]{1,0:T(8,128)(2,1)}, bf16[192,512]{1,0:T(8,128)(2,1)S(1)}, u32[]{:S(2)}, u32[]{:S(2)}) collective-permute-start(bf16[192,512]{1,0:T(8,128)(2,1)} %param.7), channel_id=1, source_target_pairs={{0,0},{1,16},{2,32},{3,48},{4,64},{5,80},{6,96},{7,112},{16,1},{17... | collective-permute-start | bytes 589832 | tf_op jit(solution)/shard_map/ppermute | solution.py:39
  2.2 27.6 %collective-permute-start.2 = (bf16[192,1792]{1,0:T(8,128)(2,1)}, bf16[192,1792]{1,0:T(8,128)(2,1)}, u32[]{:S(2)}, u32[]{:S(2)}) collective-permute-start(bf16[192,1792]{1,0:T(8,128)(2,1)} %param.6), channel_id=1, source_target_pairs={{0,1},{1,0},{2,3},{3,2},{4,5},{5,4},{6,7},{7,6},{8,9},{9,8},{10,11... | collective-permute-start | bytes 2064392 | tf_op jit(solution)/shard_map/ppermute | solution.py:23
  6.3 23.5 %collective-permute-start.3 = (bf16[192,1792]{1,0:T(8,128)(2,1)}, bf16[192,1792]{1,0:T(8,128)(2,1)S(1)}, u32[]{:S(2)}, u32[]{:S(2)}) collective-permute-start(bf16[192,1792]{1,0:T(8,128)(2,1)} %param.6), channel_id=1, source_target_pairs={{0,2},{2,4},{4,6},{6,0},{1,3},{3,5},{5,7},{7,1},{8,10},{10,12},{12... | collective-permute-start | bytes 2064392 | tf_op jit(solution)/shard_map/ppermute | solution.py:19
  8.7 21.1 %collective-permute-start.4 = (bf16[192,1792]{1,0:T(8,128)(2,1)}, bf16[192,1792]{1,0:T(8,128)(2,1)S(1)}, u32[]{:S(2)}, u32[]{:S(2)}) collective-permute-start(bf16[192,1792]{1,0:T(8,128)(2,1)} %param.6), channel_id=1, source_target_pairs={{0,6},{2,0},{4,2},{6,4},{1,7},{3,1},{5,3},{7,5},{8,14},{10,8},{12,... | collective-permute-start | bytes 2064392 | tf_op jit(solution)/shard_map/ppermute | solution.py:19
  11.4 18.3 %collective-permute-start.1 = (bf16[192,512]{1,0:T(8,128)(2,1)S(1)}, bf16[192,512]{1,0:T(8,128)(2,1)S(1)}, u32[]{:S(2)}, u32[]{:S(2)}) collective-permute-start(bf16[192,512]{1,0:T(8,128)(2,1)S(1)} %collective-permute-done), channel_id=1, source_target_pairs={{0,16},{16,0},{1,17},{17,1},{2,18},{18,2},{3,19},{19,3},{4,20},{20... | collective-permute-start | bytes 589832 | tf_op jit(solution)/shard_map/ppermute | solution.py:23
  29.8 35.7 %copy-start.2 = (bf16[192,1792]{1,0:T(8,128)(2,1)}, bf16[192,1792]{1,0:T(8,128)(2,1)S(1)}, u32[]{:S(2)}) copy-start(bf16[192,1792]{1,0:T(8,128)(2,1)S(1)} %collective-permute-done.4) | copy-start | bytes 2064388
  29.8 33.1 %collective-permute-start.8 = (bf16[192,1792]{1,0:T(8,128)(2,1)}, bf16[192,1792]{1,0:T(8,128)(2,1)}, u32[]{:S(2)}, u32[]{:S(2)}) collective-permute-start(bf16[192,1792]{1,0:T(8,128)(2,1)} %collective-permute-done.2), channel_id=1, source_target_pairs={{0,2},{2,4},{4,6},{6,0},{1,3},{3,5},{5,7},{7,1},{8,10},{10,12},{12... | collective-permute-start | bytes 2064392 | tf_op jit(solution)/shard_map/ppermute | solution.py:19
  33.6 29.3 %collective-permute-start.9 = (bf16[192,1792]{1,0:T(8,128)(2,1)}, bf16[192,1792]{1,0:T(8,128)(2,1)}, u32[]{:S(2)}, u32[]{:S(2)}) collective-permute-start(bf16[192,1792]{1,0:T(8,128)(2,1)} %collective-permute-done.2), channel_id=1, source_target_pairs={{0,6},{2,0},{4,2},{6,4},{1,7},{3,1},{5,3},{7,5},{8,14},{10,8},{12,... | collective-permute-start | bytes 2064392 | tf_op jit(solution)/shard_map/ppermute | solution.py:19
  40.4 19.7 %collective-permute-start.7 = (bf16[384,512]{1,0:T(8,128)(2,1)S(1)}, bf16[384,512]{1,0:T(8,128)(2,1)S(1)}, u32[]{:S(2)}, u32[]{:S(2)}) collective-permute-start(bf16[384,512]{1,0:T(8,128)(2,1)S(1)} %pad_maximum_fusion.5), channel_id=1, source_target_pairs={{0,32},{32,64},{64,96},{96,0},{1,33},{33,65},{65,97},{97,1},{2,34}... | collective-permute-start | bytes 1179656 | tf_op jit(solution)/shard_map/ppermute | solution.py:19
  40.7 19.5 %collective-permute-start.6 = (bf16[384,512]{1,0:T(8,128)(2,1)S(1)}, bf16[384,512]{1,0:T(8,128)(2,1)S(1)}, u32[]{:S(2)}, u32[]{:S(2)}) collective-permute-start(bf16[384,512]{1,0:T(8,128)(2,1)S(1)} %pad_maximum_fusion.5), channel_id=1, source_target_pairs={{0,64},{32,96},{64,0},{96,32},{1,65},{33,97},{65,1},{97,33},{2,66}... | collective-permute-start | bytes 1179656 | tf_op jit(solution)/shard_map/ppermute | solution.py:19
  43.0 18.6 %collective-permute-start.5 = (bf16[384,512]{1,0:T(8,128)(2,1)S(1)}, bf16[384,512]{1,0:T(8,128)(2,1)}, u32[]{:S(2)}, u32[]{:S(2)}) collective-permute-start(bf16[384,512]{1,0:T(8,128)(2,1)S(1)} %pad_maximum_fusion.5), channel_id=1, source_target_pairs={{0,96},{32,0},{64,32},{96,64},{1,97},{33,1},{65,33},{97,65},{2,98}... | collective-permute-start | bytes 1179656 | tf_op jit(solution)/shard_map/ppermute | solution.py:19
  60.1 0.7 copy-start.5
  60.9 0.7 copy-start.6
  63.0 9.8 %collective-permute-start.10 = (bf16[1536,512]{1,0:T(8,128)(2,1)S(1)}, bf16[1536,512]{1,0:T(8,128)(2,1)}, u32[]{:S(2)}, u32[]{:S(2)}) collective-permute-start(bf16[1536,512]{1,0:T(8,128)(2,1)S(1)} %pad_maximum_fusion), channel_id=1, source_target_pairs={{0,8},{8,0},{1,9},{9,1},{2,10},{10,2},{3,11},{11,3},{4,12},{12,4},... | collective-permute-start | bytes 4718600 | tf_op jit(solution)/shard_map/ppermute | solution.py:23
  65.5 4.0 %slice-start = ((bf16[192,1792]{1,0:T(8,128)(2,1)}), bf16[96,1792]{1,0:T(8,128)(2,1)S(1)}, s32[]{:S(2)}) async-start(bf16[192,1792]{1,0:T(8,128)(2,1)} %copy-done.2), calls=%async_computation.1 | async-start | bytes 688128 | tf_op jit(solution)/shard_map/slice | solution.py:80
  65.5 3.0 %collective-permute-start.11 = (bf16[192,128]{1,0:T(8,128)(2,1)S(1)}, bf16[192,128]{1,0:T(8,128)(2,1)S(1)}, u32[]{:S(2)}, u32[]{:S(2)}) collective-permute-start(bf16[192,128]{1,0:T(8,128)(2,1)S(1)} %reduce_sum.12), channel_id=1, source_target_pairs={{0,8},{8,0},{1,9},{9,1},{2,10},{10,2},{3,11},{11,3},{4,12},{12,4},... | collective-permute-start | bytes 147464 | tf_op jit(solution)/shard_map/ppermute | solution.py:23
  67.0 18.8 %collective-permute-start.13 = (bf16[192,1792]{1,0:T(8,128)(2,1)S(1)}, bf16[192,1792]{1,0:T(8,128)(2,1)S(1)}, u32[]{:S(2)}, u32[]{:S(2)}) collective-permute-start(bf16[192,1792]{1,0:T(8,128)(2,1)S(1)} %pad_maximum_fusion.1), channel_id=1, source_target_pairs={{0,2},{2,4},{4,6},{6,0},{1,3},{3,5},{5,7},{7,1},{8,10},{10,12},{12... | collective-permute-start | bytes 2064392 | tf_op jit(solution)/shard_map/ppermute | solution.py:19
  68.5 4.2 %collective-permute-start.12 = (bf16[192,128]{1,0:T(8,128)(2,1)S(1)}, bf16[192,128]{1,0:T(8,128)(2,1)S(1)}, u32[]{:S(2)}, u32[]{:S(2)}) collective-permute-start(bf16[192,128]{1,0:T(8,128)(2,1)S(1)} %add_convert_fusion.5), channel_id=1, source_target_pairs={{0,16},{16,0},{1,17},{17,1},{2,18},{18,2},{3,19},{19,3},{4,20},{20... | collective-permute-start | bytes 147464 | tf_op jit(solution)/shard_map/ppermute | solution.py:23
  69.6 17.0 %collective-permute-start.14 = (bf16[192,1792]{1,0:T(8,128)(2,1)S(1)}, bf16[192,1792]{1,0:T(8,128)(2,1)S(1)}, u32[]{:S(2)}, u32[]{:S(2)}) collective-permute-start(bf16[192,1792]{1,0:T(8,128)(2,1)S(1)} %pad_maximum_fusion.2), channel_id=1, source_target_pairs={{0,6},{2,0},{4,2},{6,4},{1,7},{3,1},{5,3},{7,5},{8,14},{10,8},{12,... | collective-permute-start | bytes 2064392 | tf_op jit(solution)/shard_map/ppermute | solution.py:19
  80.0 46.7 %copy-start = (bf16[1536,1792]{1,0:T(8,128)(2,1)}, bf16[1536,1792]{1,0:T(8,128)(2,1)S(1)}, u32[]{:S(2)}) copy-start(bf16[1536,1792]{1,0:T(8,128)(2,1)S(1)} %convolution_convert_fusion) | copy-start | bytes 16515076
  86.6 6.2 %collective-permute-start.15 = (bf16[384,128]{1,0:T(8,128)(2,1)S(1)}, bf16[384,128]{1,0:T(8,128)(2,1)S(1)}, u32[]{:S(2)}, u32[]{:S(2)}) collective-permute-start(bf16[384,128]{1,0:T(8,128)(2,1)S(1)} %pad_maximum_fusion.6), channel_id=1, source_target_pairs={{0,96},{32,0},{64,32},{96,64},{1,97},{33,1},{65,33},{97,65},{2,98}... | collective-permute-start | bytes 294920 | tf_op jit(solution)/shard_map/ppermute | solution.py:19
  87.2 8.4 %collective-permute-start.16 = (bf16[384,128]{1,0:T(8,128)(2,1)S(1)}, bf16[384,128]{1,0:T(8,128)(2,1)S(1)}, u32[]{:S(2)}, u32[]{:S(2)}) collective-permute-start(bf16[384,128]{1,0:T(8,128)(2,1)S(1)} %pad_maximum_fusion.6), channel_id=1, source_target_pairs={{0,64},{32,96},{64,0},{96,32},{1,65},{33,97},{65,1},{97,33},{2,66}... | collective-permute-start | bytes 294920 | tf_op jit(solution)/shard_map/ppermute | solution.py:19
  90.0 5.8 %collective-permute-start.17 = (bf16[384,128]{1,0:T(8,128)(2,1)S(1)}, bf16[384,128]{1,0:T(8,128)(2,1)S(1)}, u32[]{:S(2)}, u32[]{:S(2)}) collective-permute-start(bf16[384,128]{1,0:T(8,128)(2,1)S(1)} %pad_maximum_fusion.6), channel_id=1, source_target_pairs={{0,32},{32,64},{64,96},{96,0},{1,33},{33,65},{65,97},{97,1},{2,34}... | collective-permute-start | bytes 294920 | tf_op jit(solution)/shard_map/ppermute | solution.py:19
  90.0 16.9 %collective-permute-start.18 = (bf16[192,1792]{1,0:T(8,128)(2,1)S(1)}, bf16[192,1792]{1,0:T(8,128)(2,1)S(1)}, u32[]{:S(2)}, u32[]{:S(2)}) collective-permute-start(bf16[192,1792]{1,0:T(8,128)(2,1)S(1)} %get-tuple-element.54), channel_id=1, source_target_pairs={{0,1},{1,0},{2,3},{3,2},{4,5},{5,4},{6,7},{7,6},{8,9},{9,8},{10,11... | collective-permute-start | bytes 2064392 | tf_op jit(solution)/shard_map/ppermute | solution.py:23
  91.8 16.7 %collective-permute-start.19 = (bf16[192,1792]{1,0:T(8,128)(2,1)S(1)}, bf16[192,1792]{1,0:T(8,128)(2,1)S(1)}, u32[]{:S(2)}, u32[]{:S(2)}) collective-permute-start(bf16[192,1792]{1,0:T(8,128)(2,1)S(1)} %get-tuple-element.36), channel_id=1, source_target_pairs={{0,2},{2,4},{4,6},{6,0},{1,3},{3,5},{5,7},{7,1},{8,10},{10,12},{12... | collective-permute-start | bytes 2064392 | tf_op jit(solution)/shard_map/ppermute | solution.py:19
  92.6 4.7 %copy-start.4 = (bf16[192,1792]{1,0:T(8,128)(2,1)S(1)}, bf16[192,1792]{1,0:T(8,128)(2,1)}, u32[]{:S(2)}) copy-start(bf16[192,1792]{1,0:T(8,128)(2,1)} %param.6) | copy-start | bytes 2064388
  92.8 15.8 %collective-permute-start.20 = (bf16[192,1792]{1,0:T(8,128)(2,1)S(1)}, bf16[192,1792]{1,0:T(8,128)(2,1)S(1)}, u32[]{:S(2)}, u32[]{:S(2)}) collective-permute-start(bf16[192,1792]{1,0:T(8,128)(2,1)S(1)} %get-tuple-element.37), channel_id=1, source_target_pairs={{0,6},{2,0},{4,2},{6,4},{1,7},{3,1},{5,3},{7,5},{8,14},{10,8},{12,... | collective-permute-start | bytes 2064392 | tf_op jit(solution)/shard_map/ppermute | solution.py:19
  95.8 1.8 %copy-start.3 = (bf16[192,1792]{1,0:T(8,128)(2,1)S(1)}, bf16[192,1792]{1,0:T(8,128)(2,1)}, u32[]{:S(2)}) copy-start(bf16[192,1792]{1,0:T(8,128)(2,1)} %copy-done.2) | copy-start | bytes 2064388
  100.4 13.0 %copy-start.7 = (f32[128,1792]{1,0:T(8,128)S(1)}, f32[128,1792]{1,0:T(8,128)}, u32[]{:S(2)}) copy-start(f32[128,1792]{1,0:T(8,128)} %param.10) | copy-start | bytes 2752516
  100.4 13.0 %copy-start.8 = (f32[128,1792]{1,0:T(8,128)S(1)}, f32[128,1792]{1,0:T(8,128)}, u32[]{:S(2)}) copy-start(f32[128,1792]{1,0:T(8,128)} %param.11) | copy-start | bytes 2752516
  109.9 8.9 %collective-permute-start.21 = (bf16[96,1792]{1,0:T(8,128)(2,1)S(1)}, bf16[96,1792]{1,0:T(8,128)(2,1)S(1)}, u32[]{:S(2)}, u32[]{:S(2)}) collective-permute-start(bf16[96,1792]{1,0:T(8,128)(2,1)S(1)} %get-tuple-element.67), channel_id=1, source_target_pairs={{0,2},{2,4},{4,6},{6,0},{1,3},{3,5},{5,7},{7,1},{8,10},{10,12},{12... | collective-permute-start | bytes 1032200 | tf_op jit(solution)/shard_map/ppermute | solution.py:19
  111.5 7.3 %collective-permute-start.22 = (bf16[96,1792]{1,0:T(8,128)(2,1)S(1)}, bf16[96,1792]{1,0:T(8,128)(2,1)S(1)}, u32[]{:S(2)}, u32[]{:S(2)}) collective-permute-start(bf16[96,1792]{1,0:T(8,128)(2,1)S(1)} %get-tuple-element.66), channel_id=1, source_target_pairs={{0,6},{2,0},{4,2},{6,4},{1,7},{3,1},{5,3},{7,5},{8,14},{10,8},{12,... | collective-permute-start | bytes 1032200 | tf_op jit(solution)/shard_map/ppermute | solution.py:19
  116.7 33.2 %collective-permute-start.25 = (bf16[192,1792]{1,0:T(8,128)(2,1)}, bf16[192,1792]{1,0:T(8,128)(2,1)S(1)}, u32[]{:S(2)}, u32[]{:S(2)}) collective-permute-start(bf16[192,1792]{1,0:T(8,128)(2,1)} %get-tuple-element.52), channel_id=1, source_target_pairs={{0,1},{1,0},{2,3},{3,2},{4,5},{5,4},{6,7},{7,6},{8,9},{9,8},{10,11... | collective-permute-start | bytes 2064392 | tf_op jit(solution)/shard_map/ppermute | solution.py:23
  118.8 24.9 %copy-start.1 = (bf16[1024,1024]{1,0:T(8,128)(2,1)S(1)}, bf16[1024,1024]{1,0:T(8,128)(2,1)}, u32[]{:S(2)}) copy-start(bf16[1024,1024]{1,0:T(8,128)(2,1)} %param.9) | copy-start | bytes 6291460
  118.8 14.7 %collective-permute-start.28 = (bf16[128,1792]{1,0:T(8,128)(2,1)}, bf16[128,1792]{1,0:T(8,128)(2,1)S(1)}, u32[]{:S(2)}, u32[]{:S(2)}) collective-permute-start(bf16[128,1792]{1,0:T(8,128)(2,1)} %get-tuple-element.43), channel_id=1, source_target_pairs={{0,2},{2,4},{4,6},{6,0},{1,3},{3,5},{5,7},{7,1},{8,10},{10,12},{12... | collective-permute-start | bytes 1376264 | tf_op jit(solution)/shard_map/ppermute | solution.py:19
  120.5 23.2 %collective-permute-start.27 = (bf16[128,1792]{1,0:T(8,128)(2,1)}, bf16[128,1792]{1,0:T(8,128)(2,1)}, u32[]{:S(2)}, u32[]{:S(2)}) collective-permute-start(bf16[128,1792]{1,0:T(8,128)(2,1)} %get-tuple-element.43), channel_id=1, source_target_pairs={{0,4},{2,6},{4,0},{6,2},{1,5},{3,7},{5,1},{7,3},{8,12},{10,14},{12... | collective-permute-start | bytes 1376264 | tf_op jit(solution)/shard_map/ppermute | solution.py:19
  123.3 21.2 %collective-permute-start.26 = (bf16[128,1792]{1,0:T(8,128)(2,1)}, bf16[128,1792]{1,0:T(8,128)(2,1)}, u32[]{:S(2)}, u32[]{:S(2)}) collective-permute-start(bf16[128,1792]{1,0:T(8,128)(2,1)} %get-tuple-element.43), channel_id=1, source_target_pairs={{0,6},{2,0},{4,2},{6,4},{1,7},{3,1},{5,3},{7,5},{8,14},{10,8},{12,... | collective-permute-start | bytes 1376264 | tf_op jit(solution)/shard_map/ppermute | solution.py:19
  124.7 19.6 %collective-permute-start.29 = (bf16[128,1792]{1,0:T(8,128)(2,1)}, bf16[128,1792]{1,0:T(8,128)(2,1)}, u32[]{:S(2)}, u32[]{:S(2)}) collective-permute-start(bf16[128,1792]{1,0:T(8,128)(2,1)} %get-tuple-element.43), channel_id=1, source_target_pairs={{0,1},{1,0},{2,3},{3,2},{4,5},{5,4},{6,7},{7,6},{8,9},{9,8},{10,11... | collective-permute-start | bytes 1376264 | tf_op jit(solution)/shard_map/ppermute | solution.py:23
  133.5 1.8 %copy-start.9 = (bf16[128,1792]{1,0:T(8,128)(2,1)}, bf16[128,1792]{1,0:T(8,128)(2,1)S(1)}, u32[]{:S(2)}) copy-start(bf16[128,1792]{1,0:T(8,128)(2,1)S(1)} %collective-permute-done.28) | copy-start | bytes 1376260
  133.5 25.8 %collective-permute-start.24 = (bf16[192,1792]{1,0:T(8,128)(2,1)S(1)}, bf16[192,1792]{1,0:T(8,128)(2,1)}, u32[]{:S(2)}, u32[]{:S(2)}) collective-permute-start(bf16[192,1792]{1,0:T(8,128)(2,1)S(1)} %pad_maximum_fusion.4), channel_id=1, source_target_pairs={{0,6},{2,0},{4,2},{6,4},{1,7},{3,1},{5,3},{7,5},{8,14},{10,8},{12,... | collective-permute-start | bytes 2064392 | tf_op jit(solution)/shard_map/ppermute | solution.py:19
  143.7 17.2 %collective-permute-start.23 = (bf16[192,1792]{1,0:T(8,128)(2,1)}, bf16[192,1792]{1,0:T(8,128)(2,1)}, u32[]{:S(2)}, u32[]{:S(2)}) collective-permute-start(bf16[192,1792]{1,0:T(8,128)(2,1)} %pad_maximum_fusion.3), channel_id=1, source_target_pairs={{0,2},{2,4},{4,6},{6,0},{1,3},{3,5},{5,7},{7,1},{8,10},{10,12},{12... | collective-permute-start | bytes 2064392 | tf_op jit(solution)/shard_map/ppermute | solution.py:19
  143.8 2.8 %copy-start.10 = (bf16[128,1792]{1,0:T(8,128)(2,1)S(1)}, bf16[128,1792]{1,0:T(8,128)(2,1)}, u32[]{:S(2)}) copy-start(bf16[128,1792]{1,0:T(8,128)(2,1)} %copy-done.9) | copy-start | bytes 1376260
  144.3 21.4 %collective-permute-start.32 = (bf16[128,1792]{1,0:T(8,128)(2,1)}, bf16[128,1792]{1,0:T(8,128)(2,1)S(1)}, u32[]{:S(2)}, u32[]{:S(2)}) collective-permute-start(bf16[128,1792]{1,0:T(8,128)(2,1)} %collective-permute-done.29), channel_id=1, source_target_pairs={{0,2},{2,4},{4,6},{6,0},{1,3},{3,5},{5,7},{7,1},{8,10},{10,12},{12... | collective-permute-start | bytes 1376264 | tf_op jit(solution)/shard_map/ppermute | solution.py:19
  144.6 21.2 %collective-permute-start.31 = (bf16[128,1792]{1,0:T(8,128)(2,1)}, bf16[128,1792]{1,0:T(8,128)(2,1)S(1)}, u32[]{:S(2)}, u32[]{:S(2)}) collective-permute-start(bf16[128,1792]{1,0:T(8,128)(2,1)} %collective-permute-done.27), channel_id=1, source_target_pairs={{0,1},{1,0},{2,3},{3,2},{4,5},{5,4},{6,7},{7,6},{8,9},{9,8},{10,11... | collective-permute-start | bytes 1376264 | tf_op jit(solution)/shard_map/ppermute | solution.py:23
  150.0 15.8 %collective-permute-start.30 = (bf16[128,1792]{1,0:T(8,128)(2,1)}, bf16[128,1792]{1,0:T(8,128)(2,1)S(1)}, u32[]{:S(2)}, u32[]{:S(2)}) collective-permute-start(bf16[128,1792]{1,0:T(8,128)(2,1)} %collective-permute-done.29), channel_id=1, source_target_pairs={{0,6},{2,0},{4,2},{6,4},{1,7},{3,1},{5,3},{7,5},{8,14},{10,8},{12,... | collective-permute-start | bytes 1376264 | tf_op jit(solution)/shard_map/ppermute | solution.py:19

commit v4 on v3

--- a/solution.py
+++ b/solution.py
@@ -88,7 +88,7 @@
         return token_block(sums, i)
 
     xup, xdown = partial(3), partial(7)
-    mine, xup, xdown, hfirst, hsecond = lax.optimization_barrier((mine, xup, xdown, hfirst, hsecond))
+    xup, xdown, hfirst, hsecond = lax.optimization_barrier((xup, xdown, hfirst, hsecond))
     xup, xdown = z_up(xup), z_down(xdown)
     far = x_far(partial(5))
     htwo = jnp.concatenate([hfirst[:96], hsecond[:96]], axis=0)

time: 171 us -> 173 us (1.012)
  waiting for transfers between devices: 41.9 us -> 60.3 us
  blocking collectives: 14.4 us -> 0 us
  matrix products: 25.2 us -> 21.8 us
  local copies, waits for them, and re-layouts: 6.86 us -> 8.77 us
    all_to_all x1 -> x0, blocking collectives: 14.4 us -> none  [shards(): part = lax.all_to_all(part, ('z', 'xh'), 0, 0, tiled=True)]
    all_to_all x0 -> x1, waiting for transfers between devices: none -> 9.49 us  [shards(): part = lax.all_to_all(part, ('z', 'xh'), 0, 0, tiled=True)]
    ppermute x23, waiting for transfers between devices: 32.1 us -> 38.7 us  [ring(): return lambda a: lax.ppermute(a, axis, pairs)]
    ppermute x9, starting transfers between devices: 27.8 us -> 22.6 us  [swap(): return lambda a: lax.ppermute(a, axis, [(0, 1), (1, 0)])]
    all_to_all x0 -> x1, starting transfers between devices: none -> 5.05 us  [shards(): part = lax.all_to_all(part, ('z', 'xh'), 0, 0, tiled=True)]
    dot_general x12, matrix products: 25.2 us -> 21.8 us  [dot(): lax.dot_general(a, b, (((ca,), (cb,)), ((), ())), preferred_element_type=...]
    ppermute x9, waiting for transfers between devices: 9.85 us -> 12.1 us  [swap(): return lambda a: lax.ppermute(a, axis, [(0, 1), (1, 0)])]
    unnamed x25 -> x34, local copies, waits for them, and re-layouts: 1.56 us -> 3.51 us
  transfers between devices with their start and end apart: 33 -> 34, of which waited for: 13 -> 15; matrix products, arithmetic and copies ran while one was open for 18% -> 16% of each run, Pallas kernels for 0% -> 0%
where the time goes in v4:
time: 173 us
  starting transfers between devices  74 us (43%)
  waiting for transfers between devices  60.3 us (35%)
  matrix products  21.8 us (13%)
  local copies, waits for them, and re-layouts  8.77 us (5%)
  other arithmetic  6.67 us (4%)
    ppermute x23, starting transfers between devices, ring(): return lambda a: lax.ppermute(a, axis, pairs)  44.8 us
    ppermute x23, waiting for transfers between devices, ring(): return lambda a: lax.ppermute(a, axis, pairs)  38.7 us
    ppermute x9, starting transfers between devices, swap(): return lambda a: lax.ppermute(a, axis, [(0, 1), (1, 0)])  22.6 us
    dot_general x12, matrix products, dot(): lax.dot_general(a, b, (((ca,), (cb,)), ((), ())), preferred_element_type=...  21.8 us
    ppermute x9, waiting for transfers between devices, swap(): return lambda a: lax.ppermute(a, axis, [(0, 1), (1, 0)])  12.1 us
    all_to_all x1, waiting for transfers between devices, shards(): part = lax.all_to_all(part, ('z', 'xh'), 0, 0, tiled=True)  9.49 us
    all_to_all x1, starting transfers between devices, shards(): part = lax.all_to_all(part, ('z', 'xh'), 0, 0, tiled=True)  5.05 us
    dynamic_slice x1, local copies, waits for them, and re-layouts, shards(): lax.dynamic_slice_in_dim(weight, k * 512, 512, axis=1)  3.52 us
  transfers between devices with their start and end apart: 34, of which 15 were waited for; matrix products, arithmetic and copies ran while one was open for 16% of the time, Pallas kernels for 0%

profile of v4, /device:TPU:0, one launch (start us, length us, event | category | flops | bytes accessed | tf_op | source)
XLA Modules:
  0.0 172.7 jit_solution(8671704528094293318)
XLA Ops:
  0.6 1.6 collective-permute-start
  2.2 4.1 %collective-permute-start.2 = (bf16[192,1792]{1,0:T(8,128)(2,1)}, bf16[192,1792]{1,0:T(8,128)(2,1)}, u32[]{:S(2)}, u32[]{:S(2)}) collective-permute-start(bf16[192,1792]{1,0:T(8,128)(2,1)} %param.6), channel_id=1, source_target_pairs={{0,1},{1,0},{2,3},{3,2},{4,5},{5,4},{6,7},{7,6},{8,9},{9,8},{10,11... | collective-permute-start | bytes 2064392 | tf_op jit(solution)/shard_map/ppermute | solution.py:23
  6.3 2.5 %collective-permute-start.3 = (bf16[192,1792]{1,0:T(8,128)(2,1)}, bf16[192,1792]{1,0:T(8,128)(2,1)S(1)}, u32[]{:S(2)}, u32[]{:S(2)}) collective-permute-start(bf16[192,1792]{1,0:T(8,128)(2,1)} %param.6), channel_id=1, source_target_pairs={{0,2},{2,4},{4,6},{6,0},{1,3},{3,5},{5,7},{7,1},{8,10},{10,12},{12... | collective-permute-start | bytes 2064392 | tf_op jit(solution)/shard_map/ppermute | solution.py:19
  8.7 2.7 %collective-permute-start.4 = (bf16[192,1792]{1,0:T(8,128)(2,1)}, bf16[192,1792]{1,0:T(8,128)(2,1)S(1)}, u32[]{:S(2)}, u32[]{:S(2)}) collective-permute-start(bf16[192,1792]{1,0:T(8,128)(2,1)} %param.6), channel_id=1, source_target_pairs={{0,6},{2,0},{4,2},{6,4},{1,7},{3,1},{5,3},{7,5},{8,14},{10,8},{12,... | collective-permute-start | bytes 2064392 | tf_op jit(solution)/shard_map/ppermute | solution.py:19
  11.4 14.3 %collective-permute-start.1 = (bf16[192,512]{1,0:T(8,128)(2,1)S(1)}, bf16[192,512]{1,0:T(8,128)(2,1)S(1)}, u32[]{:S(2)}, u32[]{:S(2)}) collective-permute-start(bf16[192,512]{1,0:T(8,128)(2,1)S(1)} %collective-permute-done), channel_id=1, source_target_pairs={{0,16},{16,0},{1,17},{17,1},{2,18},{18,2},{3,19},{19,3},{4,20},{20... | collective-permute-start | bytes 589832 | tf_op jit(solution)/shard_map/ppermute | solution.py:23
  25.7 1.6 fusion.36
  28.1 1.6 collective-permute-done.1
  29.8 3.8 %collective-permute-start.8 = (bf16[192,1792]{1,0:T(8,128)(2,1)}, bf16[192,1792]{1,0:T(8,128)(2,1)S(1)}, u32[]{:S(2)}, u32[]{:S(2)}) collective-permute-start(bf16[192,1792]{1,0:T(8,128)(2,1)} %collective-permute-done.2), channel_id=1, source_target_pairs={{0,2},{2,4},{4,6},{6,0},{1,3},{3,5},{5,7},{7,1},{8,10},{10,12},{12... | collective-permute-start | bytes 2064392 | tf_op jit(solution)/shard_map/ppermute | solution.py:19
  33.6 6.8 %collective-permute-start.9 = (bf16[192,1792]{1,0:T(8,128)(2,1)}, bf16[192,1792]{1,0:T(8,128)(2,1)S(1)}, u32[]{:S(2)}, u32[]{:S(2)}) collective-permute-start(bf16[192,1792]{1,0:T(8,128)(2,1)} %collective-permute-done.2), channel_id=1, source_target_pairs={{0,6},{2,0},{4,2},{6,4},{1,7},{3,1},{5,3},{7,5},{8,14},{10,8},{12,... | collective-permute-start | bytes 2064392 | tf_op jit(solution)/shard_map/ppermute | solution.py:19
  40.7 2.3 %collective-permute-start.6 = (bf16[384,512]{1,0:T(8,128)(2,1)S(1)}, bf16[384,512]{1,0:T(8,128)(2,1)}, u32[]{:S(2)}, u32[]{:S(2)}) collective-permute-start(bf16[384,512]{1,0:T(8,128)(2,1)S(1)} %pad_maximum_fusion.5), channel_id=1, source_target_pairs={{0,64},{32,96},{64,0},{96,32},{1,65},{33,97},{65,1},{97,33},{2,66}... | collective-permute-start | bytes 1179656 | tf_op jit(solution)/shard_map/ppermute | solution.py:19
  43.0 2.6 %collective-permute-start.5 = (bf16[384,512]{1,0:T(8,128)(2,1)S(1)}, bf16[384,512]{1,0:T(8,128)(2,1)}, u32[]{:S(2)}, u32[]{:S(2)}) collective-permute-start(bf16[384,512]{1,0:T(8,128)(2,1)S(1)} %pad_maximum_fusion.5), channel_id=1, source_target_pairs={{0,96},{32,0},{64,32},{96,64},{1,97},{33,1},{65,33},{97,65},{2,98}... | collective-permute-start | bytes 1179656 | tf_op jit(solution)/shard_map/ppermute | solution.py:19
  45.6 5.0 %all-to-all-start = ((bf16[8,192,128]{2,1,0:T(8,128)(2,1)}), bf16[8,192,128]{2,1,0:T(8,128)(2,1)S(1)}, u32[]{:S(2)}, u32[]{:S(2)}) async-start(bf16[8,192,128]{2,1,0:T(8,128)(2,1)} %bitcast.15), calls=%async_computation | async-start | bytes 786432 | tf_op jit(solution)/shard_map/all_to_all | solution.py:75
  50.7 9.5 %all-to-all-done = bf16[8,192,128]{2,1,0:T(8,128)(2,1)S(1)} async-done(((bf16[8,192,128]{2,1,0:T(8,128)(2,1)}), bf16[8,192,128]{2,1,0:T(8,128)(2,1)S(1)}, u32[]{:S(2)}, u32[]{:S(2)}) %all-to-all-start) | async-done | bytes 393248 | tf_op jit(solution)/shard_map/all_to_all | solution.py:75
  60.3 1.3 pad_maximum_fusion
  62.5 0.8 copy-done.7
  63.3 3.5 %constant_dynamic-slice_fusion.14 = (bf16[1792,512]{1,0:T(8,128)(2,1)S(1)}, bf16[1792,512]{1,0:T(8,128)(2,1)}) fusion(bf16[1792,1024]{1,0:T(8,128)(2,1)} %param.8, s32[]{:T(128)S(6)} %select_n.154, s32[]{:T(128)S(6)} %select_n.158), kind=kLoop, calls=%fused_computation.126 | loop fusion | bytes 7340040 | tf_op jit(solution)/shard_map/dynamic_slice | solution.py:64
  68.0 0.9 collective-permute-start.16
  68.9 2.8 %collective-permute-done.12 = bf16[192,128]{1,0:T(8,128)(2,1)S(1)} collective-permute-done((bf16[192,128]{1,0:T(8,128)(2,1)S(1)}, bf16[192,128]{1,0:T(8,128)(2,1)S(1)}, u32[]{:S(2)}, u32[]{:S(2)}) %collective-permute-start.12) | collective-permute-done | bytes 49184 | tf_op jit(solution)/shard_map/ppermute | solution.py:23
  71.7 0.9 collective-permute-start.13
  72.6 1.7 %collective-permute-start.17 = (bf16[192,1792]{1,0:T(8,128)(2,1)S(1)}, bf16[192,1792]{1,0:T(8,128)(2,1)S(1)}, u32[]{:S(2)}, u32[]{:S(2)}) collective-permute-start(bf16[192,1792]{1,0:T(8,128)(2,1)S(1)} %pad_maximum_fusion.2), channel_id=1, source_target_pairs={{0,6},{2,0},{4,2},{6,4},{1,7},{3,1},{5,3},{7,5},{8,14},{10,8},{12,... | collective-permute-start | bytes 2064392 | tf_op jit(solution)/shard_map/ppermute | solution.py:19
  74.4 1.4 collective-permute-start.14
  75.8 1.6 collective-permute-done.13
  77.4 3.2 %collective-permute-done.14 = bf16[384,128]{1,0:T(8,128)(2,1)S(1)} collective-permute-done((bf16[384,128]{1,0:T(8,128)(2,1)S(1)}, bf16[384,128]{1,0:T(8,128)(2,1)S(1)}, u32[]{:S(2)}, u32[]{:S(2)}) %collective-permute-start.14) | collective-permute-done | bytes 98336 | tf_op jit(solution)/shard_map/ppermute | solution.py:19
  80.6 2.6 %collective-permute-done.15 = bf16[384,128]{1,0:T(8,128)(2,1)S(1)} collective-permute-done((bf16[384,128]{1,0:T(8,128)(2,1)S(1)}, bf16[384,128]{1,0:T(8,128)(2,1)S(1)}, u32[]{:S(2)}, u32[]{:S(2)}) %collective-permute-start.15) | collective-permute-done | bytes 98336 | tf_op jit(solution)/shard_map/ppermute | solution.py:19
  83.2 1.5 fusion.18
  86.6 6.1 %convolution_convert_fusion = bf16[1536,1792]{1,0:T(8,128)(2,1)S(1)} fusion(bf16[1792,512]{1,0:T(8,128)(2,1)S(1)} %copy-done.2, bf16[1792,512]{1,0:T(8,128)(2,1)S(1)} %get-tuple-element.58, bf16[1536,512]{1,0:T(8,128)(2,1)S(1)} %collective-permute-done.10, bf16[1536,512]{1,0:T(8,128)(2,1)S(1)} %pad_maximum_fusion), kind=kOutput, calls=%fused_computation | convolution fusion | flops 5653528576 | bytes 12320768 | tf_op jit(solution)/shard_map/dot_general | solution.py:59
  92.9 2.3 %collective-permute-start.18 = (bf16[192,1792]{1,0:T(8,128)(2,1)S(1)}, bf16[192,1792]{1,0:T(8,128)(2,1)S(1)}, u32[]{:S(2)}, u32[]{:S(2)}) collective-permute-start(bf16[192,1792]{1,0:T(8,128)(2,1)S(1)} %get-tuple-element.56), channel_id=1, source_target_pairs={{0,1},{1,0},{2,3},{3,2},{4,5},{5,4},{6,7},{7,6},{8,9},{9,8},{10,11... | collective-permute-start | bytes 2064392 | tf_op jit(solution)/shard_map/ppermute | solution.py:23
  95.8 2.5 %collective-permute-start.20 = (bf16[192,1792]{1,0:T(8,128)(2,1)S(1)}, bf16[192,1792]{1,0:T(8,128)(2,1)S(1)}, u32[]{:S(2)}, u32[]{:S(2)}) collective-permute-start(bf16[192,1792]{1,0:T(8,128)(2,1)S(1)} %get-tuple-element.35), channel_id=1, source_target_pairs={{0,6},{2,0},{4,2},{6,4},{1,7},{3,1},{5,3},{7,5},{8,14},{10,8},{12,... | collective-permute-start | bytes 2064392 | tf_op jit(solution)/shard_map/ppermute | solution.py:19
  100.3 7.7 %collective-permute-done.18 = bf16[192,1792]{1,0:T(8,128)(2,1)S(1)} collective-permute-done((bf16[192,1792]{1,0:T(8,128)(2,1)S(1)}, bf16[192,1792]{1,0:T(8,128)(2,1)S(1)}, u32[]{:S(2)}, u32[]{:S(2)}) %collective-permute-start.18) | collective-permute-done | bytes 688160 | tf_op jit(solution)/shard_map/ppermute | solution.py:23
  108.0 2.5 %collective-permute-done.19 = bf16[192,1792]{1,0:T(8,128)(2,1)S(1)} collective-permute-done((bf16[192,1792]{1,0:T(8,128)(2,1)S(1)}, bf16[192,1792]{1,0:T(8,128)(2,1)S(1)}, u32[]{:S(2)}, u32[]{:S(2)}) %collective-permute-start.19) | collective-permute-done | bytes 688160 | tf_op jit(solution)/shard_map/ppermute | solution.py:19
  110.4 1.2 add_convert_fusion.2
  111.7 0.9 collective-permute-start.21
  112.7 2.4 %collective-permute-start.22 = (bf16[96,1792]{1,0:T(8,128)(2,1)S(1)}, bf16[96,1792]{1,0:T(8,128)(2,1)S(1)}, u32[]{:S(2)}, u32[]{:S(2)}) collective-permute-start(bf16[96,1792]{1,0:T(8,128)(2,1)S(1)} %get-tuple-element.68), channel_id=1, source_target_pairs={{0,6},{2,0},{4,2},{6,4},{1,7},{3,1},{5,3},{7,5},{8,14},{10,8},{12,... | collective-permute-start | bytes 1032200 | tf_op jit(solution)/shard_map/ppermute | solution.py:19
  115.0 2.3 %divide_convert_fusion = (bf16[128,1792]{1,0:T(8,128)(2,1)}, f32[128,1792]{1,0:T(8,128)}, f32[128,1792]{1,0:T(8,128)}) fusion(f32[128,1792]{1,0:T(8,128)S(1)} %copy-done.12, f32[128,1792]{1,0:T(8,128)S(1)} %copy-done.13, f32[128,1792]{1,0:T(8,128)S(1)} %fusion.9, bf16[192,1792]{1,0:T(8,128)(2,1)S(1)} %copy-done.10, ...), kind=kOutput, calls=%fused_computation.69 | convolution fusion | flops 91521024 | bytes 5783556 | tf_op jit(solution)/shard_map/dot_general | solution.py:59
  117.9 3.5 %collective-permute-done.21 = bf16[96,1792]{1,0:T(8,128)(2,1)S(1)} collective-permute-done((bf16[96,1792]{1,0:T(8,128)(2,1)S(1)}, bf16[96,1792]{1,0:T(8,128)(2,1)S(1)}, u32[]{:S(2)}, u32[]{:S(2)}) %collective-permute-start.21) | collective-permute-done | bytes 344096 | tf_op jit(solution)/shard_map/ppermute | solution.py:19
  121.4 4.1 %collective-permute-done.22 = bf16[96,1792]{1,0:T(8,128)(2,1)S(1)} collective-permute-done((bf16[96,1792]{1,0:T(8,128)(2,1)S(1)}, bf16[96,1792]{1,0:T(8,128)(2,1)S(1)}, u32[]{:S(2)}, u32[]{:S(2)}) %collective-permute-start.22) | collective-permute-done | bytes 344096 | tf_op jit(solution)/shard_map/ppermute | solution.py:19
  125.5 5.2 %collective-permute-start.27 = (bf16[128,1792]{1,0:T(8,128)(2,1)}, bf16[128,1792]{1,0:T(8,128)(2,1)}, u32[]{:S(2)}, u32[]{:S(2)}) collective-permute-start(bf16[128,1792]{1,0:T(8,128)(2,1)} %get-tuple-element.41), channel_id=1, source_target_pairs={{0,4},{2,6},{4,0},{6,2},{1,5},{3,7},{5,1},{7,3},{8,12},{10,14},{12... | collective-permute-start | bytes 1376264 | tf_op jit(solution)/shard_map/ppermute | solution.py:19
  130.9 0.9 pad_maximum_fusion.3
  131.8 5.1 %collective-permute-done.28 = bf16[128,1792]{1,0:T(8,128)(2,1)S(1)} collective-permute-done((bf16[128,1792]{1,0:T(8,128)(2,1)}, bf16[128,1792]{1,0:T(8,128)(2,1)S(1)}, u32[]{:S(2)}, u32[]{:S(2)}) %collective-permute-start.28) | collective-permute-done | bytes 458784 | tf_op jit(solution)/shard_map/ppermute | solution.py:19
  136.9 4.0 %collective-permute-start.24 = (bf16[192,1792]{1,0:T(8,128)(2,1)S(1)}, bf16[192,1792]{1,0:T(8,128)(2,1)}, u32[]{:S(2)}, u32[]{:S(2)}) collective-permute-start(bf16[192,1792]{1,0:T(8,128)(2,1)S(1)} %pad_maximum_fusion.4), channel_id=1, source_target_pairs={{0,6},{2,0},{4,2},{6,4},{1,7},{3,1},{5,3},{7,5},{8,14},{10,8},{12,... | collective-permute-start | bytes 2064392 | tf_op jit(solution)/shard_map/ppermute | solution.py:19
  140.9 9.4 %collective-permute-done.27 = bf16[128,1792]{1,0:T(8,128)(2,1)} collective-permute-done((bf16[128,1792]{1,0:T(8,128)(2,1)}, bf16[128,1792]{1,0:T(8,128)(2,1)}, u32[]{:S(2)}, u32[]{:S(2)}) %collective-permute-start.27) | collective-permute-done | bytes 458784 | tf_op jit(solution)/shard_map/ppermute | solution.py:19
  151.3 3.4 %fusion.21 = f32[1792,1024]{1,0:T(8,128)S(1)} fusion(bf16[128,1792]{1,0:T(8,128)(2,1)S(1)} %copy-done.15, bf16[128,1792]{1,0:T(8,128)(2,1)} %collective-permute-done.27, bf16[128,1792]{1,0:T(8,128)(2,1)} %collective-permute-done.26, bf16[128,1792]{1,0:T(8,128)(2,1)} %get-tuple-element.41, bf16[1024,128]{1,0:T(8,128)(2,1)S(1)} %get-tuple-element.62, ...), kind=kOutput, calls=%fused_computation.31 | convolution fusion | flops 1890582528 | bytes 10223616 | tf_op jit(solution)/shard_map/dot_general | solution.py:59
  154.8 3.3 %collective-permute-start.30 = (bf16[128,1792]{1,0:T(8,128)(2,1)}, bf16[128,1792]{1,0:T(8,128)(2,1)S(1)}, u32[]{:S(2)}, u32[]{:S(2)}) collective-permute-start(bf16[128,1792]{1,0:T(8,128)(2,1)} %collective-permute-done.29), channel_id=1, source_target_pairs={{0,6},{2,0},{4,2},{6,4},{1,7},{3,1},{5,3},{7,5},{8,14},{10,8},{12,... | collective-permute-start | bytes 1376264 | tf_op jit(solution)/shard_map/ppermute | solution.py:19
  158.1 1.3 collective-permute-done.24
  159.4 3.4 %collective-permute-done.23 = bf16[192,1792]{1,0:T(8,128)(2,1)} collective-permute-done((bf16[192,1792]{1,0:T(8,128)(2,1)}, bf16[192,1792]{1,0:T(8,128)(2,1)}, u32[]{:S(2)}, u32[]{:S(2)}) %collective-permute-start.23) | collective-permute-done | bytes 688160 | tf_op jit(solution)/shard_map/ppermute | solution.py:19
  162.7 2.7 %add_convert_fusion = bf16[192,1792]{1,0:T(8,128)(2,1)} fusion(bf16[192,1792]{1,0:T(8,128)(2,1)S(1)} %collective-permute-done.25, bf16[192,1792]{1,0:T(8,128)(2,1)} %collective-permute-done.24, bf16[192,1792]{1,0:T(8,128)(2,1)} %collective-permute-done.23, bf16[1536,1792]{1,0:T(8,128)(2,1)} %copy-done, s32[]{:T(128)S(6)} %select_n.160), kind=kLoop, calls=%fused_computation.47 | loop fusion | flops 2752512 | bytes 3440644 | tf_op jit(solution)/shard_map/convert_element_type | solution.py:126
  165.4 2.1 %collective-permute-done.32 = bf16[128,1792]{1,0:T(8,128)(2,1)S(1)} collective-permute-done((bf16[128,1792]{1,0:T(8,128)(2,1)}, bf16[128,1792]{1,0:T(8,128)(2,1)S(1)}, u32[]{:S(2)}, u32[]{:S(2)}) %collective-permute-start.32) | collective-permute-done | bytes 458784 | tf_op jit(solution)/shard_map/ppermute | solution.py:19
  167.6 5.1 %multiply_convert_fusion = bf16[1792,1024]{1,0:T(8,128)(2,1)} fusion(f32[1792,1024]{1,0:T(8,128)S(1)} %fusion.21, bf16[128,1792]{1,0:T(8,128)(2,1)S(1)} %collective-permute-done.32, bf16[128,1792]{1,0:T(8,128)(2,1)S(1)} %collective-permute-done.31, bf16[128,1792]{1,0:T(8,128)(2,1)S(1)} %collective-permute-done.30, ...), kind=kOutput, calls=%fused_computation.1 | convolution fusion | flops 1896087552 | bytes 13893632 | tf_op jit(solution)/shard_map/dot_general | solution.py:59
  (97 shorter events, 9.8 us)
Async XLA Ops:
  0.6 10.8 %collective-permute-start = (bf16[192,512]{1,0:T(8,128)(2,1)}, bf16[192,512]{1,0:T(8,128)(2,1)S(1)}, u32[]{:S(2)}, u32[]{:S(2)}) collective-permute-start(bf16[192,512]{1,0:T(8,128)(2,1)} %param.7), channel_id=1, source_target_pairs={{0,0},{1,16},{2,32},{3,48},{4,64},{5,80},{6,96},{7,112},{16,1},{17... | collective-permute-start | bytes 589832 | tf_op jit(solution)/shard_map/ppermute | solution.py:39
  2.2 27.6 %collective-permute-start.2 = (bf16[192,1792]{1,0:T(8,128)(2,1)}, bf16[192,1792]{1,0:T(8,128)(2,1)}, u32[]{:S(2)}, u32[]{:S(2)}) collective-permute-start(bf16[192,1792]{1,0:T(8,128)(2,1)} %param.6), channel_id=1, source_target_pairs={{0,1},{1,0},{2,3},{3,2},{4,5},{5,4},{6,7},{7,6},{8,9},{9,8},{10,11... | collective-permute-start | bytes 2064392 | tf_op jit(solution)/shard_map/ppermute | solution.py:23
  6.3 23.5 %collective-permute-start.3 = (bf16[192,1792]{1,0:T(8,128)(2,1)}, bf16[192,1792]{1,0:T(8,128)(2,1)S(1)}, u32[]{:S(2)}, u32[]{:S(2)}) collective-permute-start(bf16[192,1792]{1,0:T(8,128)(2,1)} %param.6), channel_id=1, source_target_pairs={{0,2},{2,4},{4,6},{6,0},{1,3},{3,5},{5,7},{7,1},{8,10},{10,12},{12... | collective-permute-start | bytes 2064392 | tf_op jit(solution)/shard_map/ppermute | solution.py:19
  8.7 21.1 %collective-permute-start.4 = (bf16[192,1792]{1,0:T(8,128)(2,1)}, bf16[192,1792]{1,0:T(8,128)(2,1)S(1)}, u32[]{:S(2)}, u32[]{:S(2)}) collective-permute-start(bf16[192,1792]{1,0:T(8,128)(2,1)} %param.6), channel_id=1, source_target_pairs={{0,6},{2,0},{4,2},{6,4},{1,7},{3,1},{5,3},{7,5},{8,14},{10,8},{12,... | collective-permute-start | bytes 2064392 | tf_op jit(solution)/shard_map/ppermute | solution.py:19
  11.4 18.3 %collective-permute-start.1 = (bf16[192,512]{1,0:T(8,128)(2,1)S(1)}, bf16[192,512]{1,0:T(8,128)(2,1)S(1)}, u32[]{:S(2)}, u32[]{:S(2)}) collective-permute-start(bf16[192,512]{1,0:T(8,128)(2,1)S(1)} %collective-permute-done), channel_id=1, source_target_pairs={{0,16},{16,0},{1,17},{17,1},{2,18},{18,2},{3,19},{19,3},{4,20},{20... | collective-permute-start | bytes 589832 | tf_op jit(solution)/shard_map/ppermute | solution.py:23
  29.8 15.8 %copy-start.3 = (bf16[192,1792]{1,0:T(8,128)(2,1)}, bf16[192,1792]{1,0:T(8,128)(2,1)S(1)}, u32[]{:S(2)}) copy-start(bf16[192,1792]{1,0:T(8,128)(2,1)S(1)} %collective-permute-done.3) | copy-start | bytes 2064388
  29.8 30.4 %copy-start.5 = (bf16[192,1792]{1,0:T(8,128)(2,1)}, bf16[192,1792]{1,0:T(8,128)(2,1)S(1)}, u32[]{:S(2)}) copy-start(bf16[192,1792]{1,0:T(8,128)(2,1)S(1)} %collective-permute-done.4) | copy-start | bytes 2064388
  29.8 31.8 %collective-permute-start.8 = (bf16[192,1792]{1,0:T(8,128)(2,1)}, bf16[192,1792]{1,0:T(8,128)(2,1)S(1)}, u32[]{:S(2)}, u32[]{:S(2)}) collective-permute-start(bf16[192,1792]{1,0:T(8,128)(2,1)} %collective-permute-done.2), channel_id=1, source_target_pairs={{0,2},{2,4},{4,6},{6,0},{1,3},{3,5},{5,7},{7,1},{8,10},{10,12},{12... | collective-permute-start | bytes 2064392 | tf_op jit(solution)/shard_map/ppermute | solution.py:19
  33.6 28.0 %collective-permute-start.9 = (bf16[192,1792]{1,0:T(8,128)(2,1)}, bf16[192,1792]{1,0:T(8,128)(2,1)S(1)}, u32[]{:S(2)}, u32[]{:S(2)}) collective-permute-start(bf16[192,1792]{1,0:T(8,128)(2,1)} %collective-permute-done.2), channel_id=1, source_target_pairs={{0,6},{2,0},{4,2},{6,4},{1,7},{3,1},{5,3},{7,5},{8,14},{10,8},{12,... | collective-permute-start | bytes 2064392 | tf_op jit(solution)/shard_map/ppermute | solution.py:19
  40.4 19.8 %collective-permute-start.7 = (bf16[384,512]{1,0:T(8,128)(2,1)S(1)}, bf16[384,512]{1,0:T(8,128)(2,1)}, u32[]{:S(2)}, u32[]{:S(2)}) collective-permute-start(bf16[384,512]{1,0:T(8,128)(2,1)S(1)} %pad_maximum_fusion.5), channel_id=1, source_target_pairs={{0,32},{32,64},{64,96},{96,0},{1,33},{33,65},{65,97},{97,1},{2,34}... | collective-permute-start | bytes 1179656 | tf_op jit(solution)/shard_map/ppermute | solution.py:19
  40.7 19.6 %collective-permute-start.6 = (bf16[384,512]{1,0:T(8,128)(2,1)S(1)}, bf16[384,512]{1,0:T(8,128)(2,1)}, u32[]{:S(2)}, u32[]{:S(2)}) collective-permute-start(bf16[384,512]{1,0:T(8,128)(2,1)S(1)} %pad_maximum_fusion.5), channel_id=1, source_target_pairs={{0,64},{32,96},{64,0},{96,32},{1,65},{33,97},{65,1},{97,33},{2,66}... | collective-permute-start | bytes 1179656 | tf_op jit(solution)/shard_map/ppermute | solution.py:19
  43.0 17.3 %collective-permute-start.5 = (bf16[384,512]{1,0:T(8,128)(2,1)S(1)}, bf16[384,512]{1,0:T(8,128)(2,1)}, u32[]{:S(2)}, u32[]{:S(2)}) collective-permute-start(bf16[384,512]{1,0:T(8,128)(2,1)S(1)} %pad_maximum_fusion.5), channel_id=1, source_target_pairs={{0,96},{32,0},{64,32},{96,64},{1,97},{33,1},{65,33},{97,65},{2,98}... | collective-permute-start | bytes 1179656 | tf_op jit(solution)/shard_map/ppermute | solution.py:19
  45.6 14.5 %all-to-all-start = ((bf16[8,192,128]{2,1,0:T(8,128)(2,1)}), bf16[8,192,128]{2,1,0:T(8,128)(2,1)S(1)}, u32[]{:S(2)}, u32[]{:S(2)}) async-start(bf16[8,192,128]{2,1,0:T(8,128)(2,1)} %bitcast.15), calls=%async_computation | async-start | bytes 786432 | tf_op jit(solution)/shard_map/all_to_all | solution.py:75
  63.3 4.1 %collective-permute-start.11 = (bf16[192,128]{1,0:T(8,128)(2,1)S(1)}, bf16[192,128]{1,0:T(8,128)(2,1)S(1)}, u32[]{:S(2)}, u32[]{:S(2)}) collective-permute-start(bf16[192,128]{1,0:T(8,128)(2,1)S(1)} %reduce_sum.12), channel_id=1, source_target_pairs={{0,8},{8,0},{1,9},{9,1},{2,10},{10,2},{3,11},{11,3},{4,12},{12,4},... | collective-permute-start | bytes 147464 | tf_op jit(solution)/shard_map/ppermute | solution.py:23
  66.8 1.1 slice-start.3
  66.8 5.8 %slice-start.1 = ((bf16[192,1792]{1,0:T(8,128)(2,1)}), bf16[96,1792]{1,0:T(8,128)(2,1)S(1)}, s32[]{:S(2)}) async-start(bf16[192,1792]{1,0:T(8,128)(2,1)} %copy-done.5), calls=%async_computation.2 | async-start | bytes 688128 | tf_op jit(solution)/shard_map/slice | solution.py:80
  66.8 5.8 %slice-start.2 = ((bf16[192,1792]{1,0:T(8,128)(2,1)}), bf16[96,1792]{1,0:T(8,128)(2,1)S(1)}, s32[]{:S(2)}) async-start(bf16[192,1792]{1,0:T(8,128)(2,1)} %copy-done.7), calls=%async_computation.3 | async-start | bytes 688128 | tf_op jit(solution)/shard_map/slice | solution.py:80
  66.8 19.3 %collective-permute-start.10 = (bf16[1536,512]{1,0:T(8,128)(2,1)S(1)}, bf16[1536,512]{1,0:T(8,128)(2,1)S(1)}, u32[]{:S(2)}, u32[]{:S(2)}) collective-permute-start(bf16[1536,512]{1,0:T(8,128)(2,1)S(1)} %pad_maximum_fusion), channel_id=1, source_target_pairs={{0,8},{8,0},{1,9},{9,1},{2,10},{10,2},{3,11},{11,3},{4,12},{12,4},... | collective-permute-start | bytes 4718600 | tf_op jit(solution)/shard_map/ppermute | solution.py:23
  67.4 4.2 %collective-permute-start.12 = (bf16[192,128]{1,0:T(8,128)(2,1)S(1)}, bf16[192,128]{1,0:T(8,128)(2,1)S(1)}, u32[]{:S(2)}, u32[]{:S(2)}) collective-permute-start(bf16[192,128]{1,0:T(8,128)(2,1)S(1)} %add_convert_fusion.5), channel_id=1, source_target_pairs={{0,16},{16,0},{1,17},{17,1},{2,18},{18,2},{3,19},{19,3},{4,20},{20... | collective-permute-start | bytes 147464 | tf_op jit(solution)/shard_map/ppermute | solution.py:23
  68.0 27.2 %collective-permute-start.16 = (bf16[192,1792]{1,0:T(8,128)(2,1)S(1)}, bf16[192,1792]{1,0:T(8,128)(2,1)S(1)}, u32[]{:S(2)}, u32[]{:S(2)}) collective-permute-start(bf16[192,1792]{1,0:T(8,128)(2,1)S(1)} %pad_maximum_fusion.1), channel_id=1, source_target_pairs={{0,2},{2,4},{4,6},{6,0},{1,3},{3,5},{5,7},{7,1},{8,10},{10,12},{12... | collective-permute-start | bytes 2064392 | tf_op jit(solution)/shard_map/ppermute | solution.py:19
  68.9 15.8 %copy-start.11 = (bf16[192,1792]{1,0:T(8,128)(2,1)S(1)}, bf16[192,1792]{1,0:T(8,128)(2,1)}, u32[]{:S(2)}) copy-start(bf16[192,1792]{1,0:T(8,128)(2,1)} %param.6) | copy-start | bytes 2064388
  71.7 5.7 %collective-permute-start.13 = (bf16[384,128]{1,0:T(8,128)(2,1)S(1)}, bf16[384,128]{1,0:T(8,128)(2,1)S(1)}, u32[]{:S(2)}, u32[]{:S(2)}) collective-permute-start(bf16[384,128]{1,0:T(8,128)(2,1)S(1)} %pad_maximum_fusion.6), channel_id=1, source_target_pairs={{0,96},{32,0},{64,32},{96,64},{1,97},{33,1},{65,33},{97,65},{2,98}... | collective-permute-start | bytes 294920 | tf_op jit(solution)/shard_map/ppermute | solution.py:19
  72.6 22.5 %collective-permute-start.17 = (bf16[192,1792]{1,0:T(8,128)(2,1)S(1)}, bf16[192,1792]{1,0:T(8,128)(2,1)S(1)}, u32[]{:S(2)}, u32[]{:S(2)}) collective-permute-start(bf16[192,1792]{1,0:T(8,128)(2,1)S(1)} %pad_maximum_fusion.2), channel_id=1, source_target_pairs={{0,6},{2,0},{4,2},{6,4},{1,7},{3,1},{5,3},{7,5},{8,14},{10,8},{12,... | collective-permute-start | bytes 2064392 | tf_op jit(solution)/shard_map/ppermute | solution.py:19
  74.4 6.2 %collective-permute-start.14 = (bf16[384,128]{1,0:T(8,128)(2,1)S(1)}, bf16[384,128]{1,0:T(8,128)(2,1)S(1)}, u32[]{:S(2)}, u32[]{:S(2)}) collective-permute-start(bf16[384,128]{1,0:T(8,128)(2,1)S(1)} %pad_maximum_fusion.6), channel_id=1, source_target_pairs={{0,64},{32,96},{64,0},{96,32},{1,65},{33,97},{65,1},{97,33},{2,66}... | collective-permute-start | bytes 294920 | tf_op jit(solution)/shard_map/ppermute | solution.py:19
  77.4 5.8 %collective-permute-start.15 = (bf16[384,128]{1,0:T(8,128)(2,1)S(1)}, bf16[384,128]{1,0:T(8,128)(2,1)S(1)}, u32[]{:S(2)}, u32[]{:S(2)}) collective-permute-start(bf16[384,128]{1,0:T(8,128)(2,1)S(1)} %pad_maximum_fusion.6), channel_id=1, source_target_pairs={{0,32},{32,64},{64,96},{96,0},{1,33},{33,65},{65,97},{97,1},{2,34}... | collective-permute-start | bytes 294920 | tf_op jit(solution)/shard_map/ppermute | solution.py:19
  83.2 1.8 %copy-start.6 = (bf16[192,1792]{1,0:T(8,128)(2,1)S(1)}, bf16[192,1792]{1,0:T(8,128)(2,1)}, u32[]{:S(2)}) copy-start(bf16[192,1792]{1,0:T(8,128)(2,1)} %copy-done.5) | copy-start | bytes 2064388
  85.0 1.6 copy-start.2
  92.7 38.0 %copy-start = (bf16[1536,1792]{1,0:T(8,128)(2,1)}, bf16[1536,1792]{1,0:T(8,128)(2,1)S(1)}, u32[]{:S(2)}) copy-start(bf16[1536,1792]{1,0:T(8,128)(2,1)S(1)} %convolution_convert_fusion) | copy-start | bytes 16515076
  92.9 15.1 %collective-permute-start.18 = (bf16[192,1792]{1,0:T(8,128)(2,1)S(1)}, bf16[192,1792]{1,0:T(8,128)(2,1)S(1)}, u32[]{:S(2)}, u32[]{:S(2)}) collective-permute-start(bf16[192,1792]{1,0:T(8,128)(2,1)S(1)} %get-tuple-element.56), channel_id=1, source_target_pairs={{0,1},{1,0},{2,3},{3,2},{4,5},{5,4},{6,7},{7,6},{8,9},{9,8},{10,11... | collective-permute-start | bytes 2064392 | tf_op jit(solution)/shard_map/ppermute | solution.py:23
  95.2 15.3 %collective-permute-start.19 = (bf16[192,1792]{1,0:T(8,128)(2,1)S(1)}, bf16[192,1792]{1,0:T(8,128)(2,1)S(1)}, u32[]{:S(2)}, u32[]{:S(2)}) collective-permute-start(bf16[192,1792]{1,0:T(8,128)(2,1)S(1)} %get-tuple-element.34), channel_id=1, source_target_pairs={{0,2},{2,4},{4,6},{6,0},{1,3},{3,5},{5,7},{7,1},{8,10},{10,12},{12... | collective-permute-start | bytes 2064392 | tf_op jit(solution)/shard_map/ppermute | solution.py:19
  95.8 14.6 %collective-permute-start.20 = (bf16[192,1792]{1,0:T(8,128)(2,1)S(1)}, bf16[192,1792]{1,0:T(8,128)(2,1)S(1)}, u32[]{:S(2)}, u32[]{:S(2)}) collective-permute-start(bf16[192,1792]{1,0:T(8,128)(2,1)S(1)} %get-tuple-element.35), channel_id=1, source_target_pairs={{0,6},{2,0},{4,2},{6,4},{1,7},{3,1},{5,3},{7,5},{8,14},{10,8},{12,... | collective-permute-start | bytes 2064392 | tf_op jit(solution)/shard_map/ppermute | solution.py:19
  100.2 14.8 %copy-start.10 = (bf16[192,1792]{1,0:T(8,128)(2,1)S(1)}, bf16[192,1792]{1,0:T(8,128)(2,1)}, u32[]{:S(2)}) copy-start(bf16[192,1792]{1,0:T(8,128)(2,1)} %copy-done.9) | copy-start | bytes 2064388
  100.2 14.8 %copy-start.12 = (f32[128,1792]{1,0:T(8,128)S(1)}, f32[128,1792]{1,0:T(8,128)}, u32[]{:S(2)}) copy-start(f32[128,1792]{1,0:T(8,128)} %param.10) | copy-start | bytes 2752516
  100.2 14.8 %copy-start.13 = (f32[128,1792]{1,0:T(8,128)S(1)}, f32[128,1792]{1,0:T(8,128)}, u32[]{:S(2)}) copy-start(f32[128,1792]{1,0:T(8,128)} %param.11) | copy-start | bytes 2752516
  111.7 9.6 %collective-permute-start.21 = (bf16[96,1792]{1,0:T(8,128)(2,1)S(1)}, bf16[96,1792]{1,0:T(8,128)(2,1)S(1)}, u32[]{:S(2)}, u32[]{:S(2)}) collective-permute-start(bf16[96,1792]{1,0:T(8,128)(2,1)S(1)} %get-tuple-element.69), channel_id=1, source_target_pairs={{0,2},{2,4},{4,6},{6,0},{1,3},{3,5},{5,7},{7,1},{8,10},{10,12},{12... | collective-permute-start | bytes 1032200 | tf_op jit(solution)/shard_map/ppermute | solution.py:19
  112.7 12.8 %collective-permute-start.22 = (bf16[96,1792]{1,0:T(8,128)(2,1)S(1)}, bf16[96,1792]{1,0:T(8,128)(2,1)S(1)}, u32[]{:S(2)}, u32[]{:S(2)}) collective-permute-start(bf16[96,1792]{1,0:T(8,128)(2,1)S(1)} %get-tuple-element.68), channel_id=1, source_target_pairs={{0,6},{2,0},{4,2},{6,4},{1,7},{3,1},{5,3},{7,5},{8,14},{10,8},{12,... | collective-permute-start | bytes 1032200 | tf_op jit(solution)/shard_map/ppermute | solution.py:19
  117.3 37.4 %collective-permute-start.25 = (bf16[192,1792]{1,0:T(8,128)(2,1)}, bf16[192,1792]{1,0:T(8,128)(2,1)S(1)}, u32[]{:S(2)}, u32[]{:S(2)}) collective-permute-start(bf16[192,1792]{1,0:T(8,128)(2,1)} %get-tuple-element.54), channel_id=1, source_target_pairs={{0,1},{1,0},{2,3},{3,2},{4,5},{5,4},{6,7},{7,6},{8,9},{9,8},{10,11... | collective-permute-start | bytes 2064392 | tf_op jit(solution)/shard_map/ppermute | solution.py:23
  125.5 24.8 %copy-start.1 = (bf16[1024,1024]{1,0:T(8,128)(2,1)S(1)}, bf16[1024,1024]{1,0:T(8,128)(2,1)}, u32[]{:S(2)}) copy-start(bf16[1024,1024]{1,0:T(8,128)(2,1)} %param.9) | copy-start | bytes 6291460
  125.5 11.4 %collective-permute-start.28 = (bf16[128,1792]{1,0:T(8,128)(2,1)}, bf16[128,1792]{1,0:T(8,128)(2,1)S(1)}, u32[]{:S(2)}, u32[]{:S(2)}) collective-permute-start(bf16[128,1792]{1,0:T(8,128)(2,1)} %get-tuple-element.41), channel_id=1, source_target_pairs={{0,2},{2,4},{4,6},{6,0},{1,3},{3,5},{5,7},{7,1},{8,10},{10,12},{12... | collective-permute-start | bytes 1376264 | tf_op jit(solution)/shard_map/ppermute | solution.py:19
  125.5 24.8 %collective-permute-start.27 = (bf16[128,1792]{1,0:T(8,128)(2,1)}, bf16[128,1792]{1,0:T(8,128)(2,1)}, u32[]{:S(2)}, u32[]{:S(2)}) collective-permute-start(bf16[128,1792]{1,0:T(8,128)(2,1)} %get-tuple-element.41), channel_id=1, source_target_pairs={{0,4},{2,6},{4,0},{6,2},{1,5},{3,7},{5,1},{7,3},{8,12},{10,14},{12... | collective-permute-start | bytes 1376264 | tf_op jit(solution)/shard_map/ppermute | solution.py:19
  130.6 20.3 %collective-permute-start.26 = (bf16[128,1792]{1,0:T(8,128)(2,1)}, bf16[128,1792]{1,0:T(8,128)(2,1)}, u32[]{:S(2)}, u32[]{:S(2)}) collective-permute-start(bf16[128,1792]{1,0:T(8,128)(2,1)} %get-tuple-element.41), channel_id=1, source_target_pairs={{0,6},{2,0},{4,2},{6,4},{1,7},{3,1},{5,3},{7,5},{8,14},{10,8},{12,... | collective-permute-start | bytes 1376264 | tf_op jit(solution)/shard_map/ppermute | solution.py:19
  130.6 20.2 %collective-permute-start.29 = (bf16[128,1792]{1,0:T(8,128)(2,1)}, bf16[128,1792]{1,0:T(8,128)(2,1)}, u32[]{:S(2)}, u32[]{:S(2)}) collective-permute-start(bf16[128,1792]{1,0:T(8,128)(2,1)} %get-tuple-element.41), channel_id=1, source_target_pairs={{0,1},{1,0},{2,3},{3,2},{4,5},{5,4},{6,7},{7,6},{8,9},{9,8},{10,11... | collective-permute-start | bytes 1376264 | tf_op jit(solution)/shard_map/ppermute | solution.py:23
  136.9 4.0 %copy-start.14 = (bf16[128,1792]{1,0:T(8,128)(2,1)}, bf16[128,1792]{1,0:T(8,128)(2,1)S(1)}, u32[]{:S(2)}) copy-start(bf16[128,1792]{1,0:T(8,128)(2,1)S(1)} %collective-permute-done.28) | copy-start | bytes 1376260
  136.9 22.5 %collective-permute-start.24 = (bf16[192,1792]{1,0:T(8,128)(2,1)S(1)}, bf16[192,1792]{1,0:T(8,128)(2,1)}, u32[]{:S(2)}, u32[]{:S(2)}) collective-permute-start(bf16[192,1792]{1,0:T(8,128)(2,1)S(1)} %pad_maximum_fusion.4), channel_id=1, source_target_pairs={{0,6},{2,0},{4,2},{6,4},{1,7},{3,1},{5,3},{7,5},{8,14},{10,8},{12,... | collective-permute-start | bytes 2064392 | tf_op jit(solution)/shard_map/ppermute | solution.py:19
  150.3 12.5 %collective-permute-start.23 = (bf16[192,1792]{1,0:T(8,128)(2,1)}, bf16[192,1792]{1,0:T(8,128)(2,1)}, u32[]{:S(2)}, u32[]{:S(2)}) collective-permute-start(bf16[192,1792]{1,0:T(8,128)(2,1)} %pad_maximum_fusion.3), channel_id=1, source_target_pairs={{0,2},{2,4},{4,6},{6,0},{1,3},{3,5},{5,7},{7,1},{8,10},{10,12},{12... | collective-permute-start | bytes 2064392 | tf_op jit(solution)/shard_map/ppermute | solution.py:19
  150.9 16.7 %collective-permute-start.32 = (bf16[128,1792]{1,0:T(8,128)(2,1)}, bf16[128,1792]{1,0:T(8,128)(2,1)S(1)}, u32[]{:S(2)}, u32[]{:S(2)}) collective-permute-start(bf16[128,1792]{1,0:T(8,128)(2,1)} %collective-permute-done.29), channel_id=1, source_target_pairs={{0,2},{2,4},{4,6},{6,0},{1,3},{3,5},{5,7},{7,1},{8,10},{10,12},{12... | collective-permute-start | bytes 1376264 | tf_op jit(solution)/shard_map/ppermute | solution.py:19
  151.0 16.6 %collective-permute-start.31 = (bf16[128,1792]{1,0:T(8,128)(2,1)}, bf16[128,1792]{1,0:T(8,128)(2,1)S(1)}, u32[]{:S(2)}, u32[]{:S(2)}) collective-permute-start(bf16[128,1792]{1,0:T(8,128)(2,1)} %collective-permute-done.27), channel_id=1, source_target_pairs={{0,1},{1,0},{2,3},{3,2},{4,5},{5,4},{6,7},{7,6},{8,9},{9,8},{10,11... | collective-permute-start | bytes 1376264 | tf_op jit(solution)/shard_map/ppermute | solution.py:23
  154.8 12.8 %collective-permute-start.30 = (bf16[128,1792]{1,0:T(8,128)(2,1)}, bf16[128,1792]{1,0:T(8,128)(2,1)S(1)}, u32[]{:S(2)}, u32[]{:S(2)}) collective-permute-start(bf16[128,1792]{1,0:T(8,128)(2,1)} %collective-permute-done.29), channel_id=1, source_target_pairs={{0,6},{2,0},{4,2},{6,4},{1,7},{3,1},{5,3},{7,5},{8,14},{10,8},{12,... | collective-permute-start | bytes 1376264 | tf_op jit(solution)/shard_map/ppermute | solution.py:19
  (6 other events, 6.0 us)
